TPU v7x, 32 devices: a whole 2x2x4 slice. The times are simulated.
32 devices in a mesh: zg: 4 (over y, core), gx: 8 (over z, x).
Axes of the slice: x: 2, y: 2, z: 4, core: 2. Of those that a mesh axis runs over, the one named last changes fastest.
Arguments:
- observed: float32 [128, 512, 256], P('zg', 'gx'), may hold values from 0.25 to 4
- kernel_x: float32 [33], replicated, may hold values from 0.2 to 1
- kernel_y: float32 [33], replicated, may hold values from 0.2 to 1
- kernel_z: float32 [65], replicated, may hold values from 0.2 to 1
Outputs:
- estimate: float32 [128, 512, 256], P('zg', 'gx')
All inputs are finite; a program needn't handle non-finite values.
Results may differ from a plain program's by a relative error of at most 0.0001.
Values sent between devices are 32-bit elements; how exact they have to be, the bound alone decides.
No kernel may reach another device: no remote copies, remote signals or barrier semaphores. Data moves between devices by JAX's collectives and lax.ppermute only.
A program may use at most 64 MiB of HBM per device.

v0:
```python
import jax
import jax.numpy as jnp
from jax import lax
from jax.sharding import PartitionSpec as P

ITERS = 2


def with_halo(x, sides, width):
    for axis, dim in sides:
        peers, length = (lax.axis_size(axis), x.shape[dim])
        up = [(i, (i + 1) % peers) for i in range(peers - 1)]
        down = [(j, i) for i, j in up]
        last = lax.slice_in_dim(x, length - width, length, axis=dim)
        leading = lax.slice_in_dim(x, 0, width, axis=dim)
        before = lax.ppermute(last, axis, up)
        after = lax.ppermute(leading, axis, down)
        x = jnp.concatenate([before, x, after], axis=dim)
    return x


def band(prof, n_out, n_in, offset):
    diff = (
        jnp.arange(n_in, dtype=jnp.int32)[None, :]
        - jnp.arange(n_out, dtype=jnp.int32)[:, None]
        + offset
    )

    def add_tap(tap, acc):
        return acc + jnp.where(diff == tap, prof[tap], 0.0)

    return lax.fori_loop(0, prof.shape[0], add_tap, jnp.zeros((n_out, n_in), jnp.float32))


def lateral(volume, mat_x, mat_y, half_x):
    hp = lax.Precision.HIGHEST
    padded = with_halo(volume, (("gx", 1),), half_x)
    out = jnp.einsum("ij,zjy->ziy", mat_x, padded, precision=hp)
    return jnp.einsum("zxj,ij->zxi", out, mat_y, precision=hp)


def axial(mat_z, volume):
    return jnp.einsum("ij,jxy->ixy", mat_z, volume, precision=lax.Precision.HIGHEST)


def shards(observed, kernel_x, kernel_y, kernel_z):
    prof_x = kernel_x / jnp.sum(kernel_x)
    prof_y = kernel_y / jnp.sum(kernel_y)
    prof_z = kernel_z / jnp.sum(kernel_z)
    slab_z, cols_x, size_y = observed.shape
    half_x = (prof_x.shape[0] - 1) // 2
    half_y = (prof_y.shape[0] - 1) // 2
    half_z = (prof_z.shape[0] - 1) // 2
    fwd_x = band(prof_x, cols_x, cols_x + 2 * half_x, 0)
    adj_x = band(prof_x[::-1], cols_x, cols_x + 2 * half_x, 0)
    fwd_y = band(prof_y, size_y, size_y, half_y)
    adj_y = band(prof_y[::-1], size_y, size_y, half_y)
    observed_col = lax.all_to_all(observed, "zg", split_axis=1, concat_axis=0, tiled=True)
    whole_z = observed_col.shape[0]
    fwd_z = band(prof_z, whole_z, whole_z, half_z)
    adj_z = band(prof_z[::-1], whole_z, whole_z, half_z)
    estimate = observed
    for step in range(ITERS):
        smeared = lateral(estimate, fwd_x, fwd_y, half_x)
        columns = lax.all_to_all(smeared, "zg", split_axis=1, concat_axis=0, tiled=True)
        blurred = axial(fwd_z, columns)
        ratio = observed_col / blurred
        back_col = axial(adj_z, ratio)
        back = lax.all_to_all(back_col, "zg", split_axis=0, concat_axis=1, tiled=True)
        correction = lateral(back, adj_x, adj_y, half_x)
        estimate = estimate * correction
    return estimate


def solution(mesh):
    return jax.shard_map(
        shards,
        mesh=mesh,
        in_specs=(P("zg", "gx", None), P(), P(), P()),
        out_specs=P("zg", "gx", None),
        check_vma=False,
    )
```

profile of v0, /device:TPU:25, one launch (start us, length us, event | category | flops | bytes accessed | tf_op | source)
XLA Modules:
  0.0 540.4 jit_solution(5957516649010245110)
XLA Ops:
  2.4 3.1 collective-permute-start
  5.5 3.1 collective-permute-start.1
  11.2 5.8 %all-to-all-start = ((f32[32,64,256]{2,0,1:T(8,128)}), f32[32,64,256]{2,0,1:T(8,128)}, u32[]{:S(2)}, u32[]{:S(2)}) async-start(f32[32,64,256]{2,0,1:T(8,128)} %copy.19), calls=%async_computation | async-start | bytes 4194304 | tf_op jit(solution)/shard_map/all_to_all | solution.py:58
  19.7 84.2 %while.85 = (s32[]{:T(128)}, f32[128,128]{1,0:T(8,128)S(1)}, f32[65]{0:T(128)S(1)}, s32[]{:T(128)}, s32[]{:T(128)}) while((s32[]{:T(128)}, f32[128,128]{1,0:T(8,128)S(1)}, f32[65]{0:T(128)S(1)}, s32[]{:T(128)}, s32[]{:T(128)}) %tuple.180), condition=%wide.region_4.5_spmd.clone, body=%wide.region_3.4_spmd.clone.sunk | while | flops 98307 | bytes 131171 | solution.py:32
  104.5 45.6 %while.87 = (s32[]{:T(128)}, f32[256,256]{1,0:T(8,128)S(1)}, f32[33]{0:T(128)S(1)}, s32[]{:T(128)}, s32[]{:T(128)}) while((s32[]{:T(128)}, f32[256,256]{1,0:T(8,128)S(1)}, f32[33]{0:T(128)S(1)}, s32[]{:T(128)}, s32[]{:T(128)}) %tuple.177), condition=%wide.region_10.11_spmd.clone, body=%wide.region_9.10_spmd.clone.sunk | while | flops 393219 | bytes 524387 | solution.py:32
  150.7 37.5 %while.86 = (s32[]{:T(128)}, f32[64,96]{1,0:T(8,128)S(1)}, f32[33]{0:T(128)S(1)}, s32[]{:T(128)}, s32[]{:T(128)}) while((s32[]{:T(128)}, f32[64,96]{1,0:T(8,128)S(1)}, f32[33]{0:T(128)S(1)}, s32[]{:T(128)}, s32[]{:T(128)}) %tuple.174), condition=%wide.region_7.8_spmd.clone, body=%wide.region_6.7_spmd.clone.sunk | while | flops 30723 | bytes 49251 | solution.py:32
  188.3 3.3 fusion.51
  191.6 4.2 fusion.42
  195.8 4.6 all-to-all-start.1
  200.5 83.1 %while.84 = (s32[]{:T(128)}, f32[128,128]{1,0:T(8,128)S(1)}, f32[65]{0:T(128)S(1)}, s32[]{:T(128)}, s32[]{:T(128)}) while((s32[]{:T(128)}, f32[128,128]{1,0:T(8,128)S(1)}, f32[65]{0:T(128)S(1)}, s32[]{:T(128)}, s32[]{:T(128)}) %tuple.183), condition=%wide.region_2.0_spmd.clone, body=%wide.region_1.0_spmd.clone.sunk | while | flops 98307 | bytes 131171 | solution.py:32
  283.6 3.2 copy.20
  286.8 3.0 copy.23
  289.8 3.2 bitcast_divide_fusion.1
  297.4 4.4 all-to-all-start.2
  301.9 47.6 %while.89 = (s32[]{:T(128)}, f32[256,256]{1,0:T(8,128)S(1)}, f32[33]{0:T(128)S(1)}, s32[]{:T(128)}, s32[]{:T(128)}) while((s32[]{:T(128)}, f32[256,256]{1,0:T(8,128)S(1)}, f32[33]{0:T(128)S(1)}, s32[]{:T(128)}, s32[]{:T(128)}) %tuple.189), condition=%wide.region_14.15_spmd.clone, body=%wide.region_13.14_spmd.clone.sunk | while | flops 393219 | bytes 524387 | solution.py:32
  349.5 3.2 copy.26
  355.0 3.0 collective-permute-start.2
  358.0 3.2 collective-permute-start.3
  361.1 42.2 %while.88 = (s32[]{:T(128)}, f32[64,96]{1,0:T(8,128)S(1)}, f32[33]{0:T(128)S(1)}, s32[]{:T(128)}, s32[]{:T(128)}) while((s32[]{:T(128)}, f32[64,96]{1,0:T(8,128)S(1)}, f32[33]{0:T(128)S(1)}, s32[]{:T(128)}, s32[]{:T(128)}) %tuple.186), condition=%wide.region_12.13_spmd.clone, body=%wide.region_11.12_spmd.clone.sunk | while | flops 30723 | bytes 49251 | solution.py:32
  403.4 3.8 fusion.18
  409.2 2.9 collective-permute-start.4
  412.1 3.5 collective-permute-start.5
  415.7 9.3 %collective-permute-done.4 = f32[32,16,256]{2,1,0:T(8,128)S(1)} collective-permute-done((f32[32,16,256]{2,1,0:T(8,128)S(1)}, f32[32,16,256]{2,1,0:T(8,128)S(1)}, u32[]{:S(2)}, u32[]{:S(2)}) %collective-permute-start.4) | collective-permute-done | bytes 524320 | tf_op jit(solution)/shard_map/ppermute | solution.py:16
  424.9 12.2 %collective-permute-done.5 = f32[32,16,256]{2,1,0:T(8,128)S(1)} collective-permute-done((f32[32,16,256]{2,1,0:T(8,128)S(1)}, f32[32,16,256]{2,1,0:T(8,128)S(1)}, u32[]{:S(2)}, u32[]{:S(2)}) %collective-permute-start.5) | collective-permute-done | bytes 524320 | tf_op jit(solution)/shard_map/ppermute | solution.py:17
  439.4 3.0 fusion.40
  442.4 27.9 %all_to_all.90 = f32[32,64,256]{2,0,1:T(8,128)S(1)} all-to-all(f32[32,64,256]{2,0,1:T(8,128)S(1)} %fusion.40), channel_id=1, replica_groups=mesh['zg'=4,'gx'=8] {'zg'}, dimensions={1} | all-to-all | bytes 4194304 | tf_op jit(solution)/shard_map/all_to_all | solution.py:65
  471.8 3.1 bitcast_divide_fusion
  478.1 28.2 %all_to_all.91 = f32[128,16,256]{2,1,0:T(8,128)S(1)} all-to-all(f32[128,16,256]{2,1,0:T(8,128)S(1)} %copy.31), channel_id=1, replica_groups=mesh['zg'=4,'gx'=8] {'zg'}, dimensions={0} | all-to-all | bytes 4194304 | tf_op jit(solution)/shard_map/all_to_all | solution.py:69
  508.5 4.5 collective-permute-start.7
  513.0 8.8 %collective-permute-done.6 = f32[32,16,256]{2,1,0:T(8,128)S(1)} collective-permute-done((f32[32,16,256]{2,1,0:T(8,128)S(1)}, f32[32,16,256]{2,1,0:T(8,128)S(1)}, u32[]{:S(2)}, u32[]{:S(2)}) %collective-permute-start.6) | collective-permute-done | bytes 524320 | tf_op jit(solution)/shard_map/ppermute | solution.py:16
  521.8 12.7 %collective-permute-done.7 = f32[32,16,256]{2,1,0:T(8,128)S(1)} collective-permute-done((f32[32,16,256]{2,1,0:T(8,128)S(1)}, f32[32,16,256]{2,1,0:T(8,128)S(1)}, u32[]{:S(2)}, u32[]{:S(2)}) %collective-permute-start.7) | collective-permute-done | bytes 524320 | tf_op jit(solution)/shard_map/ppermute | solution.py:17
  536.7 3.2 fusion.57
  (573 shorter events, 363.2 us)
Async XLA Ops:
  0.0 8.6 %copy-start = (f32[32,64,256]{2,1,0:T(8,128)S(1)}, f32[32,64,256]{2,1,0:T(8,128)}, u32[]{:S(2)}) copy-start(f32[32,64,256]{2,1,0:T(8,128)} %param.16) | copy-start | bytes 6291460
  2.4 185.8 %collective-permute-start = (f32[32,16,256]{2,1,0:T(8,128)}, f32[32,16,256]{2,1,0:T(8,128)S(1)}, u32[]{:S(2)}, u32[]{:S(2)}) collective-permute-start(f32[32,16,256]{2,1,0:T(8,128)} %get-tuple-element.611), channel_id=1, source_target_pairs={{0,1},{1,2},{2,3},{3,4},{4,5},{5,6},{6,7},{8,9},{9,10},{10,11},{11... | collective-permute-start | bytes 1572872 | tf_op jit(solution)/shard_map/ppermute | solution.py:16
  5.5 182.7 %collective-permute-start.1 = (f32[32,16,256]{2,1,0:T(8,128)}, f32[32,16,256]{2,1,0:T(8,128)}, u32[]{:S(2)}, u32[]{:S(2)}) collective-permute-start(f32[32,16,256]{2,1,0:T(8,128)} %get-tuple-element.612), channel_id=1, source_target_pairs={{1,0},{2,1},{3,2},{4,3},{5,4},{6,5},{7,6},{9,8},{10,9},{11,10},{12... | collective-permute-start | bytes 1572872 | tf_op jit(solution)/shard_map/ppermute | solution.py:17
  11.2 5.8 %copy-start.5 = (f32[33]{0:T(128)S(1)}, f32[33]{0:T(128)}, u32[]{:S(2)}) copy-start(f32[33]{0:T(128)} %param.17) | copy-start | bytes 400
  11.2 6.5 %copy-start.4 = (f32[33]{0:T(128)S(1)}, f32[33]{0:T(128)}, u32[]{:S(2)}) copy-start(f32[33]{0:T(128)} %param.18) | copy-start | bytes 400
  11.2 7.2 %copy-start.3 = (f32[65]{0:T(128)S(1)}, f32[65]{0:T(128)}, u32[]{:S(2)}) copy-start(f32[65]{0:T(128)} %param.19) | copy-start | bytes 784
  11.2 184.7 %all-to-all-start = ((f32[32,64,256]{2,0,1:T(8,128)}), f32[32,64,256]{2,0,1:T(8,128)}, u32[]{:S(2)}, u32[]{:S(2)}) async-start(f32[32,64,256]{2,0,1:T(8,128)} %copy.19), calls=%async_computation | async-start | bytes 4194304 | tf_op jit(solution)/shard_map/all_to_all | solution.py:58
  195.8 91.0 %all-to-all-start.1 = ((f32[32,64,256]{2,0,1:T(8,128)}), f32[32,64,256]{2,0,1:T(8,128)}, u32[]{:S(2)}, u32[]{:S(2)}) async-start(f32[32,64,256]{2,0,1:T(8,128)} %fusion.42), calls=%async_computation.1 | async-start | bytes 4194304 | tf_op jit(solution)/shard_map/all_to_all | solution.py:65
  286.8 3.0 copy-start.1
  297.4 52.1 %all-to-all-start.2 = ((f32[128,16,256]{2,1,0:T(8,128)}), f32[128,16,256]{2,1,0:T(8,128)}, u32[]{:S(2)}, u32[]{:S(2)}) async-start(f32[128,16,256]{2,1,0:T(8,128)} %copy.25), calls=%async_computation.2 | async-start | bytes 4194304 | tf_op jit(solution)/shard_map/all_to_all | solution.py:69
  355.0 48.4 %collective-permute-start.2 = (f32[32,16,256]{2,1,0:T(8,128)}, f32[32,16,256]{2,1,0:T(8,128)S(1)}, u32[]{:S(2)}, u32[]{:S(2)}) collective-permute-start(f32[32,16,256]{2,1,0:T(8,128)} %get-tuple-element.609), channel_id=1, source_target_pairs={{0,1},{1,2},{2,3},{3,4},{4,5},{5,6},{6,7},{8,9},{9,10},{10,11},{11... | collective-permute-start | bytes 1572872 | tf_op jit(solution)/shard_map/ppermute | solution.py:16
  358.0 45.4 %collective-permute-start.3 = (f32[32,16,256]{2,1,0:T(8,128)}, f32[32,16,256]{2,1,0:T(8,128)}, u32[]{:S(2)}, u32[]{:S(2)}) collective-permute-start(f32[32,16,256]{2,1,0:T(8,128)} %get-tuple-element.610), channel_id=1, source_target_pairs={{1,0},{2,1},{3,2},{4,3},{5,4},{6,5},{7,6},{9,8},{10,9},{11,10},{12... | collective-permute-start | bytes 1572872 | tf_op jit(solution)/shard_map/ppermute | solution.py:17
  409.2 15.7 %collective-permute-start.4 = (f32[32,16,256]{2,1,0:T(8,128)S(1)}, f32[32,16,256]{2,1,0:T(8,128)S(1)}, u32[]{:S(2)}, u32[]{:S(2)}) collective-permute-start(f32[32,16,256]{2,1,0:T(8,128)S(1)} %get-tuple-element.607), channel_id=1, source_target_pairs={{0,1},{1,2},{2,3},{3,4},{4,5},{5,6},{6,7},{8,9},{9,10},{10,11},{11... | collective-permute-start | bytes 1572872 | tf_op jit(solution)/shard_map/ppermute | solution.py:16
  412.1 25.0 %collective-permute-start.5 = (f32[32,16,256]{2,1,0:T(8,128)S(1)}, f32[32,16,256]{2,1,0:T(8,128)S(1)}, u32[]{:S(2)}, u32[]{:S(2)}) collective-permute-start(f32[32,16,256]{2,1,0:T(8,128)S(1)} %get-tuple-element.608), channel_id=1, source_target_pairs={{1,0},{2,1},{3,2},{4,3},{5,4},{6,5},{7,6},{9,8},{10,9},{11,10},{12... | collective-permute-start | bytes 1572872 | tf_op jit(solution)/shard_map/ppermute | solution.py:17
  470.2 1.6 copy-start.2
  506.6 15.2 %collective-permute-start.6 = (f32[32,16,256]{2,1,0:T(8,128)S(1)}, f32[32,16,256]{2,1,0:T(8,128)S(1)}, u32[]{:S(2)}, u32[]{:S(2)}) collective-permute-start(f32[32,16,256]{2,1,0:T(8,128)S(1)} %get-tuple-element.605), channel_id=1, source_target_pairs={{0,1},{1,2},{2,3},{3,4},{4,5},{5,6},{6,7},{8,9},{9,10},{10,11},{11... | collective-permute-start | bytes 1572872 | tf_op jit(solution)/shard_map/ppermute | solution.py:16
  508.5 25.9 %collective-permute-start.7 = (f32[32,16,256]{2,1,0:T(8,128)S(1)}, f32[32,16,256]{2,1,0:T(8,128)S(1)}, u32[]{:S(2)}, u32[]{:S(2)}) collective-permute-start(f32[32,16,256]{2,1,0:T(8,128)S(1)} %get-tuple-element.606), channel_id=1, source_target_pairs={{1,0},{2,1},{3,2},{4,3},{5,4},{6,5},{7,6},{9,8},{10,9},{11,10},{12... | collective-permute-start | bytes 1572872 | tf_op jit(solution)/shard_map/ppermute | solution.py:17
where the time goes:
time: 549 us; the launch traced here: 540 us
  local copies, waits for them, and re-layouts  182 us (33%)
  other arithmetic  179 us (33%)
  blocking collectives  56 us (10%)
  waiting for transfers between devices  42.9 us (8%)
  starting transfers between devices  40 us (7%)
  matrix products  34.1 us (6%)
  loops' own time  6.23 us (1%)
    add x262, other arithmetic, add_tap(): return acc + jnp.where(diff == tap, prof[tap], 0.0)  175 us
    dynamic_slice x262, local copies, waits for them, and re-layouts, add_tap(): return acc + jnp.where(diff == tap, prof[tap], 0.0)  159 us
    all_to_all x1, blocking collectives, shards(): lax.all_to_all(back_col, 'zg', split_axis=0, concat_axis=1, tiled=True)  28.2 us
    all_to_all x1, blocking collectives, shards(): lax.all_to_all(smeared, 'zg', split_axis=1, concat_axis=0, tiled=True)  27.9 us
    ppermute x4, waiting for transfers between devices, with_halo(): after = lax.ppermute(leading, axis, down)  24.8 us
    ppermute x4, waiting for transfers between devices, with_halo(): before = lax.ppermute(last, axis, up)  18.1 us
    ppermute x4, starting transfers between devices, with_halo(): after = lax.ppermute(leading, axis, down)  14.3 us
    dot_general x4, matrix products, lateral(): return jnp.einsum('zxj,ij->zxi', out, mat_y, precision=hp)  12.3 us
  transfers between devices with their start and end apart: 11, of which 4 were waited for; matrix products, arithmetic and copies ran while one was open for 65% of the time, Pallas kernels for 0%

commit v1 on v0

v1 whole, which is shorter than its diff:
```python
import functools

import jax
import jax.numpy as jnp
from jax import lax
from jax.experimental import pallas as pl
from jax.experimental.pallas import tpu as pltpu
from jax.sharding import PartitionSpec as P

ITERS = 2
LANES = 128
AXES = ("zg", "gx")
F32 = jnp.float32
BF16 = jnp.bfloat16
VMEM_LIMIT = 40 * 1024 * 1024


def params(n=1):
    return pltpu.CompilerParams(dimension_semantics=("arbitrary",) * n, vmem_limit_bytes=VMEM_LIMIT)


def cost(flops, data):
    return pl.CostEstimate(flops=flops, bytes_accessed=data, transcendentals=0)


def swaps(pairs):
    return [q for a, b in pairs for q in ((a, b), (b, a))]


class Links:
    def __init__(self, n_zg, n_gx):
        chips = n_zg // 2
        dev = lambda z, x: z * n_gx + x
        every = range(n_gx)
        self.inner = swaps((dev(2 * k, x), dev(2 * k + 1, x)) for k in range(chips) for x in every)
        self.x = swaps((dev(2 * k + 1, x), dev(2 * k, x + 1)) for k in range(chips) for x in range(n_gx - 1))
        z_pairs = lambda first: swaps(
            (dev(2 * k + c, x), dev(2 * k + 2 + c, x)) for k in range(first, chips - 1, 2) for c in (0, 1) for x in every
        )
        self.z_even = z_pairs(0)
        self.z_odd = z_pairs(1)


def send(v, pairs):
    return lax.ppermute(v, AXES, pairs)


def split(v):
    hi = v.astype(BF16)
    return hi, (v - hi.astype(F32)).astype(BF16)


def dot(a, b):
    return jnp.dot(a, b, preferred_element_type=F32)


def matrices(ids, kernel_x, kernel_y, kernel_z, slab, group, size_y, n_pieces):
    taps_x, taps_y, taps_z = (k.shape[0] for k in (kernel_x, kernel_y, kernel_z))
    half_x, half_y, half_z = ((n - 1) // 2 for n in (taps_x, taps_y, taps_z))
    m_x, k_x = 2 * group, 4 * group
    m_z, k_z = 2 * slab, n_pieces * slab

    def body(ids_ref, x_ref, y_ref, z_ref, fx_ref, ax_ref, fyh_ref, fyl_ref, ayh_ref, ayl_ref, fz_ref, az_ref):
        core, par = ids_ref[0], ids_ref[1]

        def band(ref, n_taps, diff):
            def step(t, carry):
                fwd, adj, total = carry
                tap = ref[t]
                fwd = jnp.where(diff == t, tap, fwd)
                adj = jnp.where(diff == n_taps - 1 - t, tap, adj)
                return fwd, adj, total + tap

            zero = jnp.zeros(diff.shape, F32)
            fwd, adj, total = lax.fori_loop(0, n_taps, step, (zero, zero, jnp.float32(0.0)))
            return fwd / total, adj / total

        def places(shape, dim, size, bases):
            at = lax.broadcasted_iota(jnp.int32, shape, dim)
            place = at
            for n, base in enumerate(bases):
                place = jnp.where(at // size == n, at - n * size + base, place)
            return place

        e, i = group * core, group * (1 - core)
        outer, inner = -group + 3 * group * core, 2 * group - 3 * group * core
        rows = places((m_x, k_x), 0, group, (e, i))
        cols = places((m_x, k_x), 1, group, (outer, e, i, inner))
        for ref, mat in zip((fx_ref, ax_ref), band(x_ref, taps_x, cols - rows + half_x)):
            hi, lo = split(mat)
            ref[...] = jnp.concatenate([hi, lo, hi], axis=1)

        a, b = slab * (1 - par), slab * par
        even, odd = 2 * slab - 3 * slab * par, -slab + 3 * slab * par
        rows = places((m_z, k_z), 0, slab, (a, b))
        cols = places((m_z, k_z), 1, slab, (a, b, even, odd)[:n_pieces])
        for ref, mat in zip((fz_ref, az_ref), band(z_ref, taps_z, cols - rows + half_z)):
            hi, lo = split(mat)
            ref[...] = jnp.concatenate([hi, lo], axis=0)

        rows_per = 64
        for r in range(0, size_y, rows_per):
            shape = (rows_per, size_y)
            diff = r + lax.broadcasted_iota(jnp.int32, shape, 0) - lax.broadcasted_iota(jnp.int32, shape, 1) + half_y
            mats = band(y_ref, taps_y, diff)
            for hi_ref, lo_ref, mat in zip((fyh_ref, ayh_ref), (fyl_ref, ayl_ref), mats):
                hi_ref[r : r + rows_per, :], lo_ref[r : r + rows_per, :] = split(mat)

    smem = pl.BlockSpec(memory_space=pltpu.SMEM)
    sds = jax.ShapeDtypeStruct
    out = pl.pallas_call(
        body,
        in_specs=[smem] * 4,
        out_shape=[sds((m_x, 3 * k_x), BF16)] * 2 + [sds((size_y, size_y), BF16)] * 4 + [sds((2 * m_z, k_z), BF16)] * 2,
        compiler_params=pltpu.CompilerParams(vmem_limit_bytes=VMEM_LIMIT),
        name="band_matrices",
    )(ids, kernel_x, kernel_y, kernel_z)
    fx, ax, fyh, fyl, ayh, ayl, fz, az = out
    return (fx, (fyh, fyl), fz), (ax, (ayh, ayl), az)


def conv_x(mat, pieces, s, over=None, lane=0, block=8):
    planes, group, lanes = pieces[0].shape
    slab = planes // 2
    steps = slab // block

    def body(m_ref, *refs):
        out_ref = refs[-1]
        m = m_ref[...]
        for z in range(0, block, 2):
            cols = [jnp.concatenate([r[z + n] for r in refs[:4]], axis=0) for n in (0, 1)]
            hi, lo = split(jnp.concatenate(cols, axis=1))
            res = dot(m, jnp.concatenate([hi, hi, lo], axis=0))
            for n in (0, 1):
                v = res[:, n * lanes : (n + 1) * lanes]
                if over is not None:
                    v = refs[4][0, z + n] / v
                out_ref[z + n] = v

    piece = pl.BlockSpec((block, group, lanes), lambda k: (s * steps + k, 0, 0))
    in_specs = [pl.BlockSpec(mat.shape, lambda k: (0, 0))] + [piece] * 4
    args = [mat, *pieces]
    if over is not None:
        in_specs.append(pl.BlockSpec((1, block, 2 * group, lanes), lambda k: (s, k, 0, lane)))
        args.append(over)
    return pl.pallas_call(
        body,
        grid=(steps,),
        in_specs=in_specs,
        out_specs=pl.BlockSpec((block, 2 * group, lanes), lambda k: (k, 0, 0)),
        out_shape=jax.ShapeDtypeStruct((slab, 2 * group, lanes), F32),
        cost_estimate=cost(2 * slab * lanes * mat.size, 4 * 6 * slab * group * lanes),
        compiler_params=params(),
        name="conv_x",
    )(*args)


def conv_z(mat, pieces, g, over=None, lane=0, block=8):
    slab, width, lanes = pieces[0].shape
    group = width // 2
    steps = group // block
    n = len(pieces)
    m_z = 2 * slab

    def body(m_ref, *refs):
        out = refs[-1].reshape(m_z * block, lanes)
        m = m_ref[...]
        flat = [r.reshape(slab * block, lanes) for r in refs[:n]]
        for x in range(0, block, 2):
            cols = [
                jnp.concatenate([r[pl.ds(x + j, slab, stride=block), :] for r in flat], axis=0) for j in (0, 1)
            ]
            hi, lo = split(jnp.concatenate(cols, axis=1))
            both = dot(m, hi)
            res = both[:m_z] + (both[m_z:] + dot(m[:m_z], lo))
            for j in (0, 1):
                v = res[:, j * lanes : (j + 1) * lanes]
                if over is not None:
                    v = refs[n].reshape(m_z * block, lanes)[pl.ds(x + j, m_z, stride=block), :] / v
                out[pl.ds(x + j, m_z, stride=block), :] = v

    piece = pl.BlockSpec((slab, block, lanes), lambda k: (0, g * steps + k, 0))
    in_specs = [pl.BlockSpec(mat.shape, lambda k: (0, 0))] + [piece] * n
    args = [mat, *pieces]
    if over is not None:
        in_specs.append(pl.BlockSpec((2, slab, block, lanes), lambda k: (0, 0, g * steps + k, lane)))
        args.append(over)
    return pl.pallas_call(
        body,
        grid=(steps,),
        in_specs=in_specs,
        out_specs=pl.BlockSpec((m_z, block, lanes), lambda k: (0, k, 0)),
        out_shape=jax.ShapeDtypeStruct((m_z, group, lanes), F32),
        cost_estimate=cost(3 * group * lanes * mat.size, 4 * (n + 3) * slab * group * lanes),
        compiler_params=params(),
        name="conv_z",
    )(*args)


def mul_y(v, hi_ref, lo_ref):
    hi, lo = split(v)
    return dot(hi, hi_ref[...]) + (dot(hi, lo_ref[...]) + dot(lo, hi_ref[...]))


class Blocks:
    def __init__(self, slab, group, size_y):
        self.slab, self.group, self.size_y = slab, group, size_y
        half = size_y // 2
        self.full = pl.BlockSpec((1, slab, group, size_y), lambda s, g: (s, 0, g, 0))
        self.by_group = pl.BlockSpec((slab, group, half), lambda s, g: (s, 0, 0))
        self.a = pl.BlockSpec((slab, group, half), lambda s, g: (0, jnp.where(s == 0, g, 1), 0))
        self.b = pl.BlockSpec((slab, group, half), lambda s, g: (0, jnp.where(s == 0, 0, g), 0))
        self.pieces = [self.by_group, self.by_group, self.a, self.b]
        sds = jax.ShapeDtypeStruct
        self.full_shape = sds((2, slab, 2 * group, size_y), F32)
        self.shapes = [sds((2 * slab, group, half), F32)] * 2 + [sds((slab, 2 * group, half), F32)] * 2
        self.mat = pl.BlockSpec((size_y, size_y), lambda s, g: (0, 0))

    def rows(self, v):
        return v.reshape(self.slab * self.group, v.shape[-1])

    def get(self, e, i, a, b):
        s, g = pl.program_id(0), pl.program_id(1)
        left = jnp.where(g == 0, e[...], i[...])
        right = jnp.where(s == 0, a[...], b[...])
        return jnp.concatenate([self.rows(left), self.rows(right)], axis=1)

    def put(self, v, e, i, a, b):
        s, g = pl.program_id(0), pl.program_id(1)
        half = self.size_y // 2
        left = v[:, :half].reshape(self.slab, self.group, half)
        right = v[:, half:].reshape(self.slab, self.group, half)
        for ref, when, val in ((e, g == 0, left), (i, g == 1, left), (a, s == 0, right), (b, s == 1, right)):

            @pl.when(when)
            def _(ref=ref, val=val):
                ref[...] = val


def first_y(ids, own, received, mat, bl):
    def body(ids_ref, own_ref, got_ref, h_ref, l_ref, obs_ref, *pieces):
        mine = (ids_ref[0] != ids_ref[1]) == (pl.program_id(0) == 0)
        v = jnp.where(mine, own_ref[...], got_ref[...])
        obs_ref[0] = v
        bl.put(mul_y(bl.rows(v), h_ref, l_ref), *pieces)

    src = pl.BlockSpec((bl.slab, bl.group, bl.size_y), lambda s, g: (0, g, 0))
    return pl.pallas_call(
        body,
        grid=(2, 2),
        in_specs=[pl.BlockSpec(memory_space=pltpu.SMEM), src, src, bl.mat, bl.mat],
        out_specs=[bl.full, *bl.pieces],
        out_shape=[bl.full_shape, *bl.shapes],
        compiler_params=params(2),
        name="first_y",
    )(ids, own, received, *mat)


def update_y(estimate, pieces, adj, fwd, bl):
    def body(est_ref, e, i, a, b, ah_ref, al_ref, fh_ref, fl_ref, new_ref, *outs):
        corr = mul_y(bl.get(e, i, a, b), ah_ref, al_ref)
        new = bl.rows(est_ref[0]) * corr
        new_ref[0] = new.reshape(bl.slab, bl.group, bl.size_y)
        bl.put(mul_y(new, fh_ref, fl_ref), *outs)

    return pl.pallas_call(
        body,
        grid=(2, 2),
        in_specs=[bl.full, *bl.pieces] + [bl.mat] * 4,
        out_specs=[bl.full, *bl.pieces],
        out_shape=[bl.full_shape, *bl.shapes],
        compiler_params=params(2),
        name="update_y",
    )(estimate, *pieces, *adj, *fwd)


def last_y(ids, estimate, pieces, adj, bl):
    def body(ids_ref, est_ref, e, i, a, b, ah_ref, al_ref, keep_ref, give_ref):
        corr = mul_y(bl.get(e, i, a, b), ah_ref, al_ref)
        new = (bl.rows(est_ref[0]) * corr).reshape(bl.slab, bl.group, bl.size_y)
        mine = (ids_ref[0] != ids_ref[1]) == (pl.program_id(0) == 0)
        group = pl.ds(pl.multiple_of(pl.program_id(1) * bl.group, bl.group), bl.group)

        @pl.when(mine)
        def _():
            keep_ref[:, group, :] = new

        @pl.when(jnp.logical_not(mine))
        def _():
            give_ref[:, group, :] = new

    whole = pl.BlockSpec((bl.slab, 2 * bl.group, bl.size_y), lambda s, g: (0, 0, 0))
    return pl.pallas_call(
        body,
        grid=(2, 2),
        in_specs=[pl.BlockSpec(memory_space=pltpu.SMEM), bl.full, *bl.pieces] + [bl.mat] * 2,
        out_specs=[whole, whole],
        out_shape=[jax.ShapeDtypeStruct((bl.slab, 2 * bl.group, bl.size_y), F32)] * 2,
        compiler_params=params(2),
        name="last_y",
    )(ids, estimate, *pieces, *adj)


def halves(ids, volume, group):
    slab, _, size_y = volume.shape

    def body(ids_ref, a_ref, b_ref, keep_ref, give_ref):
        keep_ref[...] = a_ref[...]
        give_ref[...] = b_ref[...]

    block = (slab, group, size_y)
    near = pl.BlockSpec(block, lambda g, ids: (0, jnp.where(ids[0] == 0, g, 3 - g), 0))
    far = pl.BlockSpec(block, lambda g, ids: (0, jnp.where(ids[0] == 0, 3 - g, g), 0))
    out = pl.BlockSpec(block, lambda g, ids: (0, g, 0))
    return pl.pallas_call(
        body,
        grid_spec=pltpu.PrefetchScalarGridSpec(num_scalar_prefetch=1, grid=(2,), in_specs=[near, far], out_specs=[out, out]),
        out_shape=[jax.ShapeDtypeStruct((slab, 2 * group, size_y), F32)] * 2,
        compiler_params=params(),
        name="halves",
    )(ids, volume, volume)


def whole_block(ids, own, received, group):
    slab, _, size_y = own.shape

    def body(ids_ref, own_ref, got_ref, out_ref):
        mine = (pl.program_id(0) // 2) == ids_ref[0]
        out_ref[...] = jnp.where(mine, own_ref[...], got_ref[...])

    block = (slab, group, size_y)
    src = pl.BlockSpec(block, lambda g: (0, jnp.minimum(g, 3 - g), 0))
    return pl.pallas_call(
        body,
        grid=(4,),
        in_specs=[pl.BlockSpec(memory_space=pltpu.SMEM), src, src],
        out_specs=pl.BlockSpec(block, lambda g: (0, g, 0)),
        out_shape=jax.ShapeDtypeStruct((slab, 4 * group, size_y), F32),
        compiler_params=params(),
        name="whole_block",
    )(ids, own, received)


def shards(observed, kernel_x, kernel_y, kernel_z):
    n_zg, n_gx = lax.axis_size("zg"), lax.axis_size("gx")
    links = Links(n_zg, n_gx)
    slab, cols, size_y = observed.shape
    group = cols // 4
    assert (kernel_x.shape[0] - 1) // 2 <= group
    assert (kernel_z.shape[0] - 1) // 2 <= slab
    n_pieces = 4 if links.z_odd else 3
    zg = lax.axis_index("zg")
    ids = jnp.stack([zg % 2, (zg // 2) % 2]).astype(jnp.int32)
    bl = Blocks(slab, group, size_y)

    own, give = halves(ids, observed, group)
    received = send(give, links.inner)
    fwd, adj = matrices(ids, kernel_x, kernel_y, kernel_z, slab, group, size_y, n_pieces)

    def x_pass(mat, e, i, over=None, lane=0):
        outer, inner = send(e, links.x), send(i, links.inner)
        return [conv_x(mat, (outer, e, i, inner), s, over, lane) for s in (0, 1)]

    def z_pass(mat, a, b, over=None, lane=0):
        pieces = [a, b, send(a, links.z_even)]
        if links.z_odd:
            pieces.append(send(b, links.z_odd))
        return [conv_z(mat, pieces, g, over, lane) for g in (0, 1)]

    obs, e, i, a, b = first_y(ids, own, received, fwd[1], bl)
    estimate = obs
    for step in range(ITERS):
        left = x_pass(fwd[0], e, i)
        right = z_pass(fwd[2], a, b)
        left = z_pass(fwd[2], *left, over=obs, lane=0)
        right = x_pass(fwd[0], *right, over=obs, lane=1)
        left = x_pass(adj[0], *left)
        right = z_pass(adj[2], *right)
        left = z_pass(adj[2], *left)
        right = x_pass(adj[0], *right)
        if step < ITERS - 1:
            estimate, e, i, a, b = update_y(estimate, (*left, *right), adj[1], fwd[1], bl)
    own, give = last_y(ids, estimate, (*left, *right), adj[1], bl)
    return whole_block(ids, own, send(give, links.inner), group)


def solution(mesh):
    return jax.shard_map(
        shards,
        mesh=mesh,
        in_specs=(P("zg", "gx", None), P(), P(), P()),
        out_specs=P("zg", "gx", None),
        check_vma=False,
    )
```

time: 549 us -> 159 us (0.29); the launches traced: 540 us -> 157 us
  local copies, waits for them, and re-layouts: 182 us -> 1.6 us
  other arithmetic: 179 us -> 0.07 us
  blocking collectives: 56 us -> 0 us
  Pallas kernels: 0 us -> 42.9 us
  matrix products: 34.1 us -> 0 us
  waiting for transfers between devices: 42.9 us -> 76.8 us
  loops' own time: 6.23 us -> 0 us
    add x262 -> x0, other arithmetic: 175 us -> none  [add_tap(): return acc + jnp.where(diff == tap, prof[tap], 0.0)]
    dynamic_slice x262 -> x0, local copies, waits for them, and re-layouts: 159 us -> none  [add_tap(): return acc + jnp.where(diff == tap, prof[tap], 0.0)]
    all_to_all x2 -> x0, blocking collectives: 56 us -> none  [the longest x1 28.2 us: shards(): lax.all_to_all(back_col, 'zg', split_axis=0, concat_axis=1, tiled=True)]
    pallas_call x0 -> x38, Pallas kernels: none -> 42.9 us  [the longest x16 12.4 us: conv_x(): pl.pallas_call(body, grid=(steps,), in_specs=in_specs, out_specs=pl.Block...]
    dot_general x12 -> x0, matrix products: 34.1 us -> none  [the longest x4 12.3 us: lateral(): return jnp.einsum('zxj,ij->zxi', out, mat_y, precision=hp)]
    ppermute x8 -> x26, waiting for transfers between devices: 42.9 us -> 76.8 us  [send(): return lax.ppermute(v, AXES, pairs)]
    all_to_all x3 -> x0, starting transfers between devices: 14.9 us -> none  [the longest x1 5.78 us: shards(): lax.all_to_all(observed, 'zg', split_axis=1, concat_axis=0, tiled=True)]
    all_to_all x5 -> x0, local copies, waits for them, and re-layouts: 10.7 us -> none  [the longest x2 4.17 us: shards(): lax.all_to_all(smeared, 'zg', split_axis=1, concat_axis=0, tiled=True)]
  transfers between devices with their start and end apart: 11 -> 26, of which waited for: 4 -> 16; matrix products, arithmetic and copies ran while one was open for 65% -> 0% of each run, Pallas kernels for 0% -> 17%
where the time goes in v1:
time: 159 us; the launch traced here: 157 us
  waiting for transfers between devices  76.8 us (48%)
  Pallas kernels  42.9 us (27%)
  starting transfers between devices  35.4 us (22%)
  local copies, waits for them, and re-layouts  1.6 us (1%)
    ppermute x26, waiting for transfers between devices, send(): return lax.ppermute(v, AXES, pairs)  76.8 us
    ppermute x26, starting transfers between devices, send(): return lax.ppermute(v, AXES, pairs)  35.4 us
    pallas_call x16, Pallas kernels, conv_x(): pl.pallas_call(body, grid=(steps,), in_specs=in_specs, out_specs=pl.Block...  12.4 us
    pallas_call x16, Pallas kernels, conv_z(): pl.pallas_call(body, grid=(steps,), in_specs=in_specs, out_specs=pl.Block...  12.3 us
    pallas_call x1, Pallas kernels, update_y(): pl.pallas_call(body, grid=(2, 2), in_specs=[bl.full, *bl.pieces] + [bl.ma...  4.61 us
    pallas_call x1, Pallas kernels, matrices(): pl.pallas_call(body, in_specs=[smem] * 4, out_shape=[sds((m_x, 3 * k_x),...  4.53 us
  transfers between devices with their start and end apart: 26, of which 16 were waited for; matrix products, arithmetic and copies ran while one was open for 0% of the time, Pallas kernels for 17%

profile of v1, /device:TPU:25, one launch (start us, length us, event | category | flops | bytes accessed | tf_op | source)
XLA Modules:
  0.0 157.2 jit_solution(16699641250769658303)
XLA Ops:
  0.1 1.6 %copy-done = f32[32,64,256]{2,1,0:T(8,128)S(1)} copy-done((f32[32,64,256]{2,1,0:T(8,128)S(1)}, f32[32,64,256]{2,1,0:T(8,128)}, u32[]{:S(2)}) %copy-start) | copy-done | bytes 2097176
  3.5 4.5 %band_matrices.1 = (bf16[32,192]{1,0:T(8,128)(2,1)S(1)}, bf16[32,192]{1,0:T(8,128)(2,1)S(1)}, bf16[256,256]{1,0:T(8,128)(2,1)S(1)}, bf16[256,256]{1,0:T(8,128)(2...) custom-call(s32[2]{0:T(128)S(1)} %pad_add_fusion.ids_ref, ...), custom_call_target="tpu_custom_call" | custom-call | tf_op jit(solution)/shard_map/band_matrices/pallas_call | solution.py:111
  8.0 2.9 %first_y.1 = (f32[2,32,32,256]{3,2,1,0:T(8,128)S(1)}, f32[64,16,128]{2,1,0:T(8,128)S(1)}, f32[64,16,128]{2,1,0:T(8,128)S(1)}, f32[32,32,128]{2,1,0:T(8,128)S(1)}, f32[32,32,128]{2,1,0:T(8,128)S(1)}) custom-call(s32[2]{0:T(128)S(1)} %pad_add_fusion.ids_ref, f32[32,32,256]{2,1,0:T(8,128)S(1)} %get-tuple-element.27.own_ref, ...), custom_call_target="tpu_custom_call" | custom-call | tf_op jit(solution)/shard_map/first_y/pallas_call | solution.py:248
  10.9 3.0 %collective-permute-start.1 = (f32[64,16,128]{2,1,0:T(8,128)S(1)}, f32[64,16,128]{2,1,0:T(8,128)S(1)}, u32[]{:S(2)}, u32[]{:S(2)}) collective-permute-start(f32[64,16,128]{2,1,0:T(8,128)S(1)} %get-tuple-element.36.refs_1_), channel_id=1, source_target_pairs={{8,1},{1,8},{9,2},{2,9},{10,3},{3,10},{11,4},{4,11},{12,5},{5,12},... | collective-permute-start | bytes 1572872 | tf_op jit(solution)/shard_map/ppermute | solution.py:45
  15.7 11.7 %collective-permute-done.1.refs_0_ = f32[64,16,128]{2,1,0:T(8,128)S(1)} collective-permute-done((f32[64,16,128]{2,1,0:T(8,128)S(1)}, f32[64,16,128]{2,1,0:T(8,128)S(1)}, u32[]{:S(2)}, u32[]{:S(2)}) %collective-permute-start.1) | collective-permute-done | bytes 524320 | tf_op jit(solution)/shard_map/ppermute | solution.py:45
  28.1 1.3 collective-permute-start.3
  30.1 2.0 %collective-permute-start.8 = (f32[64,16,128]{2,1,0:T(8,128)S(1)}, f32[64,16,128]{2,1,0:T(8,128)S(1)}, u32[]{:S(2)}, u32[]{:S(2)}) collective-permute-start(f32[64,16,128]{2,1,0:T(8,128)S(1)} %conv_z.20.refs_1_), channel_id=1, source_target_pairs={{8,1},{1,8},{9,2},{2,9},{10,3},{3,10},{11,4},{4,11},{12,5},{5,12},... | collective-permute-start | bytes 1572872 | tf_op jit(solution)/shard_map/ppermute | solution.py:45
  33.7 5.9 %collective-permute-done.3.refs_2_ = f32[32,32,128]{2,1,0:T(8,128)S(1)} collective-permute-done((f32[32,32,128]{2,1,0:T(8,128)S(1)}, f32[32,32,128]{2,1,0:T(8,128)S(1)}, u32[]{:S(2)}, u32[]{:S(2)}) %collective-permute-start.3) | collective-permute-done | bytes 524320 | tf_op jit(solution)/shard_map/ppermute | solution.py:45
  40.4 2.6 %collective-permute-start.4 = (f32[64,16,128]{2,1,0:T(8,128)S(1)}, f32[64,16,128]{2,1,0:T(8,128)S(1)}, u32[]{:S(2)}, u32[]{:S(2)}) collective-permute-start(f32[64,16,128]{2,1,0:T(8,128)S(1)} %conv_z.16.refs_1_), channel_id=1, source_target_pairs={{8,1},{1,8},{9,2},{2,9},{10,3},{3,10},{11,4},{4,11},{12,5},{5,12},... | collective-permute-start | bytes 1572872 | tf_op jit(solution)/shard_map/ppermute | solution.py:45
  44.0 7.8 %collective-permute-done.8.refs_0_ = f32[64,16,128]{2,1,0:T(8,128)S(1)} collective-permute-done((f32[64,16,128]{2,1,0:T(8,128)S(1)}, f32[64,16,128]{2,1,0:T(8,128)S(1)}, u32[]{:S(2)}, u32[]{:S(2)}) %collective-permute-start.8) | collective-permute-done | bytes 524320 | tf_op jit(solution)/shard_map/ppermute | solution.py:45
  54.2 3.1 %collective-permute-done.4.refs_0_ = f32[64,16,128]{2,1,0:T(8,128)S(1)} collective-permute-done((f32[64,16,128]{2,1,0:T(8,128)S(1)}, f32[64,16,128]{2,1,0:T(8,128)S(1)}, u32[]{:S(2)}, u32[]{:S(2)}) %collective-permute-start.4) | collective-permute-done | bytes 524320 | tf_op jit(solution)/shard_map/ppermute | solution.py:45
  58.8 6.6 %collective-permute-done.10.refs_2_ = f32[32,32,128]{2,1,0:T(8,128)S(1)} collective-permute-done((f32[32,32,128]{2,1,0:T(8,128)S(1)}, f32[32,32,128]{2,1,0:T(8,128)S(1)}, u32[]{:S(2)}, u32[]{:S(2)}) %collective-permute-start.10) | collective-permute-done | bytes 524320 | tf_op jit(solution)/shard_map/ppermute | solution.py:45
  66.2 2.4 %collective-permute-start.11 = (f32[64,16,128]{2,1,0:T(8,128)S(1)}, f32[64,16,128]{2,1,0:T(8,128)S(1)}, u32[]{:S(2)}, u32[]{:S(2)}) collective-permute-start(f32[64,16,128]{2,1,0:T(8,128)S(1)} %conv_z.22.refs_1_), channel_id=1, source_target_pairs={{8,1},{1,8},{9,2},{2,9},{10,3},{3,10},{11,4},{4,11},{12,5},{5,12},... | collective-permute-start | bytes 1572872 | tf_op jit(solution)/shard_map/ppermute | solution.py:45
  72.3 4.4 %collective-permute-done.11.refs_0_ = f32[64,16,128]{2,1,0:T(8,128)S(1)} collective-permute-done((f32[64,16,128]{2,1,0:T(8,128)S(1)}, f32[64,16,128]{2,1,0:T(8,128)S(1)}, u32[]{:S(2)}, u32[]{:S(2)}) %collective-permute-start.11) | collective-permute-done | bytes 524320 | tf_op jit(solution)/shard_map/ppermute | solution.py:45
  78.2 4.6 %update_y.1 = (f32[2,32,32,256]{3,2,1,0:T(8,128)S(1)}, f32[64,16,128]{2,1,0:T(8,128)S(1)}, f32[64,16,128]{2,1,0:T(8,128)S(1)}, f32[32,32,128]{2,1,0:T(8,128)S(1)}, f32[32,32,128]{2,1,0:T(8,128)S(1)}) custom-call(f32[2,32,32,256]{3,2,1,0:T(8,128)S(1)} %get-tuple-element.31.refs_3_.refs_4_.est_ref, f32[64,16,128]{2,1,0:T(8,128)S(1)} %conv_z.18.e, ...), custom_call_target="tpu_custom_call" | custom-call | tf_op jit(solution)/shard_map/update_y/pallas_call | solution.py:266
  82.8 2.4 %collective-permute-start.13 = (f32[64,16,128]{2,1,0:T(8,128)S(1)}, f32[64,16,128]{2,1,0:T(8,128)S(1)}, u32[]{:S(2)}, u32[]{:S(2)}) collective-permute-start(f32[64,16,128]{2,1,0:T(8,128)S(1)} %get-tuple-element.43.refs_1_), channel_id=1, source_target_pairs={{8,1},{1,8},{9,2},{2,9},{10,3},{3,10},{11,4},{4,11},{12,5},{5,12},... | collective-permute-start | bytes 1572872 | tf_op jit(solution)/shard_map/ppermute | solution.py:45
  85.3 1.3 collective-permute-start.19
  86.6 8.4 %collective-permute-done.13.refs_0_ = f32[64,16,128]{2,1,0:T(8,128)S(1)} collective-permute-done((f32[64,16,128]{2,1,0:T(8,128)S(1)}, f32[64,16,128]{2,1,0:T(8,128)S(1)}, u32[]{:S(2)}, u32[]{:S(2)}) %collective-permute-start.13) | collective-permute-done | bytes 524320 | tf_op jit(solution)/shard_map/ppermute | solution.py:45
  95.7 1.3 collective-permute-start.15
  97.0 1.4 collective-permute-done.19.refs_2_
  99.1 4.8 %collective-permute-start.20 = (f32[64,16,128]{2,1,0:T(8,128)S(1)}, f32[64,16,128]{2,1,0:T(8,128)S(1)}, u32[]{:S(2)}, u32[]{:S(2)}) collective-permute-start(f32[64,16,128]{2,1,0:T(8,128)S(1)} %conv_z.28.refs_1_), channel_id=1, source_target_pairs={{8,1},{1,8},{9,2},{2,9},{10,3},{3,10},{11,4},{4,11},{12,5},{5,12},... | collective-permute-start | bytes 1572872 | tf_op jit(solution)/shard_map/ppermute | solution.py:45
  105.6 4.2 %collective-permute-done.15.refs_2_ = f32[32,32,128]{2,1,0:T(8,128)S(1)} collective-permute-done((f32[32,32,128]{2,1,0:T(8,128)S(1)}, f32[32,32,128]{2,1,0:T(8,128)S(1)}, u32[]{:S(2)}, u32[]{:S(2)}) %collective-permute-start.15) | collective-permute-done | bytes 524320 | tf_op jit(solution)/shard_map/ppermute | solution.py:45
  110.6 4.2 %collective-permute-start.16 = (f32[64,16,128]{2,1,0:T(8,128)S(1)}, f32[64,16,128]{2,1,0:T(8,128)S(1)}, u32[]{:S(2)}, u32[]{:S(2)}) collective-permute-start(f32[64,16,128]{2,1,0:T(8,128)S(1)} %conv_z.24.refs_1_), channel_id=1, source_target_pairs={{8,1},{1,8},{9,2},{2,9},{10,3},{3,10},{11,4},{4,11},{12,5},{5,12},... | collective-permute-start | bytes 1572872 | tf_op jit(solution)/shard_map/ppermute | solution.py:45
  117.3 1.3 collective-permute-start.22
  119.5 8.5 %collective-permute-done.16.refs_0_ = f32[64,16,128]{2,1,0:T(8,128)S(1)} collective-permute-done((f32[64,16,128]{2,1,0:T(8,128)S(1)}, f32[64,16,128]{2,1,0:T(8,128)S(1)}, u32[]{:S(2)}, u32[]{:S(2)}) %collective-permute-start.16) | collective-permute-done | bytes 524320 | tf_op jit(solution)/shard_map/ppermute | solution.py:45
  128.7 1.3 collective-permute-start.18
  131.8 2.9 %collective-permute-start.23 = (f32[64,16,128]{2,1,0:T(8,128)S(1)}, f32[64,16,128]{2,1,0:T(8,128)S(1)}, u32[]{:S(2)}, u32[]{:S(2)}) collective-permute-start(f32[64,16,128]{2,1,0:T(8,128)S(1)} %conv_z.30.refs_1_), channel_id=1, source_target_pairs={{8,1},{1,8},{9,2},{2,9},{10,3},{3,10},{11,4},{4,11},{12,5},{5,12},... | collective-permute-start | bytes 1572872 | tf_op jit(solution)/shard_map/ppermute | solution.py:45
  136.3 6.3 %collective-permute-done.18.refs_2_ = f32[32,32,128]{2,1,0:T(8,128)S(1)} collective-permute-done((f32[32,32,128]{2,1,0:T(8,128)S(1)}, f32[32,32,128]{2,1,0:T(8,128)S(1)}, u32[]{:S(2)}, u32[]{:S(2)}) %collective-permute-start.18) | collective-permute-done | bytes 524320 | tf_op jit(solution)/shard_map/ppermute | solution.py:45
  144.1 3.8 %collective-permute-done.23.refs_0_ = f32[64,16,128]{2,1,0:T(8,128)S(1)} collective-permute-done((f32[64,16,128]{2,1,0:T(8,128)S(1)}, f32[64,16,128]{2,1,0:T(8,128)S(1)}, u32[]{:S(2)}, u32[]{:S(2)}) %collective-permute-start.23) | collective-permute-done | bytes 524320 | tf_op jit(solution)/shard_map/ppermute | solution.py:45
  149.4 2.6 %last_y.1 = (f32[32,32,256]{2,1,0:T(8,128)S(1)}, f32[32,32,256]{2,1,0:T(8,128)S(1)}) custom-call(s32[2]{0:T(128)S(1)} %pad_add_fusion.ids_ref, f32[2,32,32,256]{3,2,1,0:T(8,128)S(1)} %get-tuple-element.42.est_ref, f32[64,16,128]{2,1,0:T(8,128)S(1)} %conv_z.26.e, f32[64,16,128]{2,1,0:T(8,128)S(1)} %conv_z.27.i, f32[32,32,128]{2,1,0:T(8,128)S(1)} %conv_x.30.a, ...), custom_call_target="tpu_custom_call" | custom-call | tf_op jit(solution)/shard_map/last_y/pallas_call | solution.py:293
  152.0 2.6 %collective-permute-done.25.got_ref = f32[32,32,256]{2,1,0:T(8,128)S(1)} collective-permute-done((f32[32,32,256]{2,1,0:T(8,128)S(1)}, f32[32,32,256]{2,1,0:T(8,128)S(1)}, u32[]{:S(2)}, u32[]{:S(2)}) %collective-permute-start.25) | collective-permute-done | bytes 1048608 | tf_op jit(solution)/shard_map/ppermute | solution.py:45
  154.6 2.6 %whole_block.1 = f32[32,64,256]{2,1,0:T(8,128)} custom-call(s32[2]{0:T(128)S(1)} %pad_add_fusion.ids_ref, f32[32,32,256]{2,1,0:T(8,128)S(1)} %get-tuple-element.47.own_ref, f32[32,32,256]{2,1,0:T(8,128)S(1)} %collective-permute-done.25.got_ref), custom_call_target="tpu_custom_call" | custom-call | tf_op jit(solution)/shard_map/whole_block/pallas_call | solution.py:333
  (67 shorter events, 32.5 us)
Async XLA Ops:
  0.1 1.6 %copy-start = (f32[32,64,256]{2,1,0:T(8,128)S(1)}, f32[32,64,256]{2,1,0:T(8,128)}, u32[]{:S(2)}) copy-start(f32[32,64,256]{2,1,0:T(8,128)} %b_ref.1) | copy-start | bytes 6291460
  1.7 1.8 %copy-start.1 = (f32[33]{0:T(128)S(1)}, f32[33]{0:T(128)}, u32[]{:S(2)}) copy-start(f32[33]{0:T(128)} %x_ref.1) | copy-start | bytes 400
  1.7 1.8 %copy-start.2 = (f32[33]{0:T(128)S(1)}, f32[33]{0:T(128)}, u32[]{:S(2)}) copy-start(f32[33]{0:T(128)} %y_ref.1) | copy-start | bytes 400
  1.7 1.8 %copy-start.3 = (f32[65]{0:T(128)S(1)}, f32[65]{0:T(128)}, u32[]{:S(2)}) copy-start(f32[65]{0:T(128)} %z_ref.1) | copy-start | bytes 784
  2.7 5.3 %collective-permute-start = (f32[32,32,256]{2,1,0:T(8,128)S(1)}, f32[32,32,256]{2,1,0:T(8,128)S(1)}, u32[]{:S(2)}, u32[]{:S(2)}) collective-permute-start(f32[32,32,256]{2,1,0:T(8,128)S(1)} %get-tuple-element.28), channel_id=1, source_target_pairs={{0,8},{8,0},{1,9},{9,1},{2,10},{10,2},{3,11},{11,3},{4,12},{12,4},... | collective-permute-start | bytes 3145736 | tf_op jit(solution)/shard_map/ppermute | solution.py:45
  10.9 16.4 %collective-permute-start.1 = (f32[64,16,128]{2,1,0:T(8,128)S(1)}, f32[64,16,128]{2,1,0:T(8,128)S(1)}, u32[]{:S(2)}, u32[]{:S(2)}) collective-permute-start(f32[64,16,128]{2,1,0:T(8,128)S(1)} %get-tuple-element.36.refs_1_), channel_id=1, source_target_pairs={{8,1},{1,8},{9,2},{2,9},{10,3},{3,10},{11,4},{4,11},{12,5},{5,12},... | collective-permute-start | bytes 1572872 | tf_op jit(solution)/shard_map/ppermute | solution.py:45
  14.0 13.4 %collective-permute-start.2 = (f32[64,16,128]{2,1,0:T(8,128)S(1)}, f32[64,16,128]{2,1,0:T(8,128)S(1)}, u32[]{:S(2)}, u32[]{:S(2)}) collective-permute-start(f32[64,16,128]{2,1,0:T(8,128)S(1)} %get-tuple-element.37.refs_2_), channel_id=1, source_target_pairs={{0,8},{8,0},{1,9},{9,1},{2,10},{10,2},{3,11},{11,3},{4,12},{12,4},... | collective-permute-start | bytes 1572872 | tf_op jit(solution)/shard_map/ppermute | solution.py:45
  14.4 15.0 %collective-permute-start.7 = (f32[32,32,128]{2,1,0:T(8,128)S(1)}, f32[32,32,128]{2,1,0:T(8,128)S(1)}, u32[]{:S(2)}, u32[]{:S(2)}) collective-permute-start(f32[32,32,128]{2,1,0:T(8,128)S(1)} %get-tuple-element.38.refs_0_), channel_id=1, source_target_pairs={{0,16},{16,0},{1,17},{17,1},{2,18},{18,2},{3,19},{19,3},{4,20},{20... | collective-permute-start | bytes 1572872 | tf_op jit(solution)/shard_map/ppermute | solution.py:45
  28.1 11.5 %collective-permute-start.3 = (f32[32,32,128]{2,1,0:T(8,128)S(1)}, f32[32,32,128]{2,1,0:T(8,128)S(1)}, u32[]{:S(2)}, u32[]{:S(2)}) collective-permute-start(f32[32,32,128]{2,1,0:T(8,128)S(1)} %conv_x.16.refs_0_), channel_id=1, source_target_pairs={{0,16},{16,0},{1,17},{17,1},{2,18},{18,2},{3,19},{19,3},{4,20},{20... | collective-permute-start | bytes 1572872 | tf_op jit(solution)/shard_map/ppermute | solution.py:45
  30.1 21.6 %collective-permute-start.8 = (f32[64,16,128]{2,1,0:T(8,128)S(1)}, f32[64,16,128]{2,1,0:T(8,128)S(1)}, u32[]{:S(2)}, u32[]{:S(2)}) collective-permute-start(f32[64,16,128]{2,1,0:T(8,128)S(1)} %conv_z.20.refs_1_), channel_id=1, source_target_pairs={{8,1},{1,8},{9,2},{2,9},{10,3},{3,10},{11,4},{4,11},{12,5},{5,12},... | collective-permute-start | bytes 1572872 | tf_op jit(solution)/shard_map/ppermute | solution.py:45
  32.9 18.8 %collective-permute-start.9 = (f32[64,16,128]{2,1,0:T(8,128)S(1)}, f32[64,16,128]{2,1,0:T(8,128)S(1)}, u32[]{:S(2)}, u32[]{:S(2)}) collective-permute-start(f32[64,16,128]{2,1,0:T(8,128)S(1)} %conv_z.21.refs_2_), channel_id=1, source_target_pairs={{0,8},{8,0},{1,9},{9,1},{2,10},{10,2},{3,11},{11,3},{4,12},{12,4},... | collective-permute-start | bytes 1572872 | tf_op jit(solution)/shard_map/ppermute | solution.py:45
  40.4 16.9 %collective-permute-start.4 = (f32[64,16,128]{2,1,0:T(8,128)S(1)}, f32[64,16,128]{2,1,0:T(8,128)S(1)}, u32[]{:S(2)}, u32[]{:S(2)}) collective-permute-start(f32[64,16,128]{2,1,0:T(8,128)S(1)} %conv_z.16.refs_1_), channel_id=1, source_target_pairs={{8,1},{1,8},{9,2},{2,9},{10,3},{3,10},{11,4},{4,11},{12,5},{5,12},... | collective-permute-start | bytes 1572872 | tf_op jit(solution)/shard_map/ppermute | solution.py:45
  43.9 13.5 %collective-permute-start.5 = (f32[64,16,128]{2,1,0:T(8,128)S(1)}, f32[64,16,128]{2,1,0:T(8,128)S(1)}, u32[]{:S(2)}, u32[]{:S(2)}) collective-permute-start(f32[64,16,128]{2,1,0:T(8,128)S(1)} %conv_z.17.refs_2_), channel_id=1, source_target_pairs={{0,8},{8,0},{1,9},{9,1},{2,10},{10,2},{3,11},{11,3},{4,12},{12,4},... | collective-permute-start | bytes 1572872 | tf_op jit(solution)/shard_map/ppermute | solution.py:45
  52.6 12.8 %collective-permute-start.10 = (f32[32,32,128]{2,1,0:T(8,128)S(1)}, f32[32,32,128]{2,1,0:T(8,128)S(1)}, u32[]{:S(2)}, u32[]{:S(2)}) collective-permute-start(f32[32,32,128]{2,1,0:T(8,128)S(1)} %conv_x.20.refs_0_), channel_id=1, source_target_pairs={{0,16},{16,0},{1,17},{17,1},{2,18},{18,2},{3,19},{19,3},{4,20},{20... | collective-permute-start | bytes 1572872 | tf_op jit(solution)/shard_map/ppermute | solution.py:45
  58.1 12.7 %collective-permute-start.6 = (f32[32,32,128]{2,1,0:T(8,128)S(1)}, f32[32,32,128]{2,1,0:T(8,128)S(1)}, u32[]{:S(2)}, u32[]{:S(2)}) collective-permute-start(f32[32,32,128]{2,1,0:T(8,128)S(1)} %conv_x.18.refs_0_), channel_id=1, source_target_pairs={{0,16},{16,0},{1,17},{17,1},{2,18},{18,2},{3,19},{19,3},{4,20},{20... | collective-permute-start | bytes 1572872 | tf_op jit(solution)/shard_map/ppermute | solution.py:45
  66.2 10.5 %collective-permute-start.11 = (f32[64,16,128]{2,1,0:T(8,128)S(1)}, f32[64,16,128]{2,1,0:T(8,128)S(1)}, u32[]{:S(2)}, u32[]{:S(2)}) collective-permute-start(f32[64,16,128]{2,1,0:T(8,128)S(1)} %conv_z.22.refs_1_), channel_id=1, source_target_pairs={{8,1},{1,8},{9,2},{2,9},{10,3},{3,10},{11,4},{4,11},{12,5},{5,12},... | collective-permute-start | bytes 1572872 | tf_op jit(solution)/shard_map/ppermute | solution.py:45
  69.4 7.3 %collective-permute-start.12 = (f32[64,16,128]{2,1,0:T(8,128)S(1)}, f32[64,16,128]{2,1,0:T(8,128)S(1)}, u32[]{:S(2)}, u32[]{:S(2)}) collective-permute-start(f32[64,16,128]{2,1,0:T(8,128)S(1)} %conv_z.23.refs_2_), channel_id=1, source_target_pairs={{0,8},{8,0},{1,9},{9,1},{2,10},{10,2},{3,11},{11,3},{4,12},{12,4},... | collective-permute-start | bytes 1572872 | tf_op jit(solution)/shard_map/ppermute | solution.py:45
  82.8 12.2 %collective-permute-start.13 = (f32[64,16,128]{2,1,0:T(8,128)S(1)}, f32[64,16,128]{2,1,0:T(8,128)S(1)}, u32[]{:S(2)}, u32[]{:S(2)}) collective-permute-start(f32[64,16,128]{2,1,0:T(8,128)S(1)} %get-tuple-element.43.refs_1_), channel_id=1, source_target_pairs={{8,1},{1,8},{9,2},{2,9},{10,3},{3,10},{11,4},{4,11},{12,5},{5,12},... | collective-permute-start | bytes 1572872 | tf_op jit(solution)/shard_map/ppermute | solution.py:45
  85.2 9.8 %collective-permute-start.14 = (f32[64,16,128]{2,1,0:T(8,128)S(1)}, f32[64,16,128]{2,1,0:T(8,128)S(1)}, u32[]{:S(2)}, u32[]{:S(2)}) collective-permute-start(f32[64,16,128]{2,1,0:T(8,128)S(1)} %get-tuple-element.44.refs_2_), channel_id=1, source_target_pairs={{0,8},{8,0},{1,9},{9,1},{2,10},{10,2},{3,11},{11,3},{4,12},{12,4},... | collective-permute-start | bytes 1572872 | tf_op jit(solution)/shard_map/ppermute | solution.py:45
  85.3 13.1 %collective-permute-start.19 = (f32[32,32,128]{2,1,0:T(8,128)S(1)}, f32[32,32,128]{2,1,0:T(8,128)S(1)}, u32[]{:S(2)}, u32[]{:S(2)}) collective-permute-start(f32[32,32,128]{2,1,0:T(8,128)S(1)} %get-tuple-element.45.refs_0_), channel_id=1, source_target_pairs={{0,16},{16,0},{1,17},{17,1},{2,18},{18,2},{3,19},{19,3},{4,20},{20... | collective-permute-start | bytes 1572872 | tf_op jit(solution)/shard_map/ppermute | solution.py:45
  95.7 14.1 %collective-permute-start.15 = (f32[32,32,128]{2,1,0:T(8,128)S(1)}, f32[32,32,128]{2,1,0:T(8,128)S(1)}, u32[]{:S(2)}, u32[]{:S(2)}) collective-permute-start(f32[32,32,128]{2,1,0:T(8,128)S(1)} %conv_x.24.refs_0_), channel_id=1, source_target_pairs={{0,16},{16,0},{1,17},{17,1},{2,18},{18,2},{3,19},{19,3},{4,20},{20... | collective-permute-start | bytes 1572872 | tf_op jit(solution)/shard_map/ppermute | solution.py:45
  99.1 17.3 %collective-permute-start.20 = (f32[64,16,128]{2,1,0:T(8,128)S(1)}, f32[64,16,128]{2,1,0:T(8,128)S(1)}, u32[]{:S(2)}, u32[]{:S(2)}) collective-permute-start(f32[64,16,128]{2,1,0:T(8,128)S(1)} %conv_z.28.refs_1_), channel_id=1, source_target_pairs={{8,1},{1,8},{9,2},{2,9},{10,3},{3,10},{11,4},{4,11},{12,5},{5,12},... | collective-permute-start | bytes 1572872 | tf_op jit(solution)/shard_map/ppermute | solution.py:45
  104.7 11.7 %collective-permute-start.21 = (f32[64,16,128]{2,1,0:T(8,128)S(1)}, f32[64,16,128]{2,1,0:T(8,128)S(1)}, u32[]{:S(2)}, u32[]{:S(2)}) collective-permute-start(f32[64,16,128]{2,1,0:T(8,128)S(1)} %conv_z.29.refs_2_), channel_id=1, source_target_pairs={{0,8},{8,0},{1,9},{9,1},{2,10},{10,2},{3,11},{11,3},{4,12},{12,4},... | collective-permute-start | bytes 1572872 | tf_op jit(solution)/shard_map/ppermute | solution.py:45
  110.6 17.4 %collective-permute-start.16 = (f32[64,16,128]{2,1,0:T(8,128)S(1)}, f32[64,16,128]{2,1,0:T(8,128)S(1)}, u32[]{:S(2)}, u32[]{:S(2)}) collective-permute-start(f32[64,16,128]{2,1,0:T(8,128)S(1)} %conv_z.24.refs_1_), channel_id=1, source_target_pairs={{8,1},{1,8},{9,2},{2,9},{10,3},{3,10},{11,4},{4,11},{12,5},{5,12},... | collective-permute-start | bytes 1572872 | tf_op jit(solution)/shard_map/ppermute | solution.py:45
  115.7 12.3 %collective-permute-start.17 = (f32[64,16,128]{2,1,0:T(8,128)S(1)}, f32[64,16,128]{2,1,0:T(8,128)S(1)}, u32[]{:S(2)}, u32[]{:S(2)}) collective-permute-start(f32[64,16,128]{2,1,0:T(8,128)S(1)} %conv_z.25.refs_2_), channel_id=1, source_target_pairs={{0,8},{8,0},{1,9},{9,1},{2,10},{10,2},{3,11},{11,3},{4,12},{12,4},... | collective-permute-start | bytes 1572872 | tf_op jit(solution)/shard_map/ppermute | solution.py:45
  117.3 13.7 %collective-permute-start.22 = (f32[32,32,128]{2,1,0:T(8,128)S(1)}, f32[32,32,128]{2,1,0:T(8,128)S(1)}, u32[]{:S(2)}, u32[]{:S(2)}) collective-permute-start(f32[32,32,128]{2,1,0:T(8,128)S(1)} %conv_x.28.refs_0_), channel_id=1, source_target_pairs={{0,16},{16,0},{1,17},{17,1},{2,18},{18,2},{3,19},{19,3},{4,20},{20... | collective-permute-start | bytes 1572872 | tf_op jit(solution)/shard_map/ppermute | solution.py:45
  128.7 13.9 %collective-permute-start.18 = (f32[32,32,128]{2,1,0:T(8,128)S(1)}, f32[32,32,128]{2,1,0:T(8,128)S(1)}, u32[]{:S(2)}, u32[]{:S(2)}) collective-permute-start(f32[32,32,128]{2,1,0:T(8,128)S(1)} %conv_x.26.refs_0_), channel_id=1, source_target_pairs={{0,16},{16,0},{1,17},{17,1},{2,18},{18,2},{3,19},{19,3},{4,20},{20... | collective-permute-start | bytes 1572872 | tf_op jit(solution)/shard_map/ppermute | solution.py:45
  131.8 16.1 %collective-permute-start.23 = (f32[64,16,128]{2,1,0:T(8,128)S(1)}, f32[64,16,128]{2,1,0:T(8,128)S(1)}, u32[]{:S(2)}, u32[]{:S(2)}) collective-permute-start(f32[64,16,128]{2,1,0:T(8,128)S(1)} %conv_z.30.refs_1_), channel_id=1, source_target_pairs={{8,1},{1,8},{9,2},{2,9},{10,3},{3,10},{11,4},{4,11},{12,5},{5,12},... | collective-permute-start | bytes 1572872 | tf_op jit(solution)/shard_map/ppermute | solution.py:45
  135.4 12.5 %collective-permute-start.24 = (f32[64,16,128]{2,1,0:T(8,128)S(1)}, f32[64,16,128]{2,1,0:T(8,128)S(1)}, u32[]{:S(2)}, u32[]{:S(2)}) collective-permute-start(f32[64,16,128]{2,1,0:T(8,128)S(1)} %conv_z.31.refs_2_), channel_id=1, source_target_pairs={{0,8},{8,0},{1,9},{9,1},{2,10},{10,2},{3,11},{11,3},{4,12},{12,4},... | collective-permute-start | bytes 1572872 | tf_op jit(solution)/shard_map/ppermute | solution.py:45
  151.9 2.7 %collective-permute-start.25 = (f32[32,32,256]{2,1,0:T(8,128)S(1)}, f32[32,32,256]{2,1,0:T(8,128)S(1)}, u32[]{:S(2)}, u32[]{:S(2)}) collective-permute-start(f32[32,32,256]{2,1,0:T(8,128)S(1)} %get-tuple-element.48), channel_id=1, source_target_pairs={{0,8},{8,0},{1,9},{9,1},{2,10},{10,2},{3,11},{11,3},{4,12},{12,4},... | collective-permute-start | bytes 3145736 | tf_op jit(solution)/shard_map/ppermute | solution.py:45

commit v2 on v1

--- a/solution.py
+++ b/solution.py
@@ -33,7 +33,7 @@
         dev = lambda z, x: z * n_gx + x
         every = range(n_gx)
         self.inner = swaps((dev(2 * k, x), dev(2 * k + 1, x)) for k in range(chips) for x in every)
-        self.x = swaps((dev(2 * k + 1, x), dev(2 * k, x + 1)) for k in range(chips) for x in range(n_gx - 1))
+        self.x = swaps((dev(2 * k + 1, x), dev(2 * k, (x + 1) % n_gx)) for k in range(chips) for x in every)
         z_pairs = lambda first: swaps(
             (dev(2 * k + c, x), dev(2 * k + 2 + c, x)) for k in range(first, chips - 1, 2) for c in (0, 1) for x in every
         )
@@ -83,7 +83,7 @@
             return place
 
         e, i = group * core, group * (1 - core)
-        outer, inner = -group + 3 * group * core, 2 * group - 3 * group * core
+        outer, inner = -group + 3 * group * core + ids_ref[2], 2 * group - 3 * group * core
         rows = places((m_x, k_x), 0, group, (e, i))
         cols = places((m_x, k_x), 1, group, (outer, e, i, inner))
         for ref, mat in zip((fx_ref, ax_ref), band(x_ref, taps_x, cols - rows + half_x)):
@@ -350,7 +350,10 @@
     assert (kernel_z.shape[0] - 1) // 2 <= slab
     n_pieces = 4 if links.z_odd else 3
     zg = lax.axis_index("zg")
-    ids = jnp.stack([zg % 2, (zg // 2) % 2]).astype(jnp.int32)
+    gx = lax.axis_index("gx")
+    core = zg % 2
+    beyond = jnp.where(gx == core * (n_gx - 1), 8 * cols, 0)
+    ids = jnp.stack([core, (zg // 2) % 2, beyond]).astype(jnp.int32)
     bl = Blocks(slab, group, size_y)
 
     own, give = halves(ids, observed, group)

time: 159 us -> 150 us (0.943)
  starting transfers between devices: 35.4 us -> 25.1 us
    ppermute x26, starting transfers between devices: 35.4 us -> 25.1 us  [send(): return lax.ppermute(v, AXES, pairs)]
  transfers between devices with their start and end apart: 26 -> 26, of which waited for: 16 -> 16; matrix products, arithmetic and copies ran while one was open for 0% -> 0% of each run, Pallas kernels for 17% -> 18%
where the time goes in v2:
time: 150 us; the launch traced here: 148 us
  waiting for transfers between devices  78 us (52%)
  Pallas kernels  42.8 us (29%)
  starting transfers between devices  25.1 us (17%)
  local copies, waits for them, and re-layouts  1.6 us (1%)
    ppermute x26, waiting for transfers between devices, send(): return lax.ppermute(v, AXES, pairs)  78 us
    ppermute x26, starting transfers between devices, send(): return lax.ppermute(v, AXES, pairs)  25.1 us
    pallas_call x16, Pallas kernels, conv_x(): pl.pallas_call(body, grid=(steps,), in_specs=in_specs, out_specs=pl.Block...  12.4 us
    pallas_call x16, Pallas kernels, conv_z(): pl.pallas_call(body, grid=(steps,), in_specs=in_specs, out_specs=pl.Block...  12.2 us
    pallas_call x1, Pallas kernels, update_y(): pl.pallas_call(body, grid=(2, 2), in_specs=[bl.full, *bl.pieces] + [bl.ma...  4.61 us
    pallas_call x1, Pallas kernels, matrices(): pl.pallas_call(body, in_specs=[smem] * 4, out_shape=[sds((m_x, 3 * k_x),...  4.53 us
  transfers between devices with their start and end apart: 26, of which 16 were waited for; matrix products, arithmetic and copies ran while one was open for 0% of the time, Pallas kernels for 18%

profile of v2, /device:TPU:25, one launch (start us, length us, event | category | flops | bytes accessed | tf_op | source)
XLA Modules:
  0.0 147.8 jit_solution(8015157016367807219)
XLA Ops:
  0.1 1.6 %copy-done = f32[32,64,256]{2,1,0:T(8,128)S(1)} copy-done((f32[32,64,256]{2,1,0:T(8,128)S(1)}, f32[32,64,256]{2,1,0:T(8,128)}, u32[]{:S(2)}) %copy-start) | copy-done | bytes 2097176
  3.5 4.5 %band_matrices.1 = (bf16[32,192]{1,0:T(8,128)(2,1)S(1)}, bf16[32,192]{1,0:T(8,128)(2,1)S(1)}, bf16[256,256]{1,0:T(8,128)(2,1)S(1)}, bf16[256,256]{1,0:T(8,128)(2...) custom-call(s32[3]{0:T(128)S(1)} %pad_add_fusion.ids_ref, ...), custom_call_target="tpu_custom_call" | custom-call | tf_op jit(solution)/shard_map/band_matrices/pallas_call | solution.py:111
  8.0 2.9 %first_y.1 = (f32[2,32,32,256]{3,2,1,0:T(8,128)S(1)}, f32[64,16,128]{2,1,0:T(8,128)S(1)}, f32[64,16,128]{2,1,0:T(8,128)S(1)}, f32[32,32,128]{2,1,0:T(8,128)S(1)}, f32[32,32,128]{2,1,0:T(8,128)S(1)}) custom-call(s32[3]{0:T(128)S(1)} %pad_add_fusion.ids_ref, f32[32,32,256]{2,1,0:T(8,128)S(1)} %get-tuple-element.27.own_ref, ...), custom_call_target="tpu_custom_call" | custom-call | tf_op jit(solution)/shard_map/first_y/pallas_call | solution.py:248
  10.9 1.2 collective-permute-start.1
  12.5 1.2 collective-permute-start.7
  13.7 11.8 %collective-permute-done.1.refs_0_ = f32[64,16,128]{2,1,0:T(8,128)S(1)} collective-permute-done((f32[64,16,128]{2,1,0:T(8,128)S(1)}, f32[64,16,128]{2,1,0:T(8,128)S(1)}, u32[]{:S(2)}, u32[]{:S(2)}) %collective-permute-start.1) | collective-permute-done | bytes 524320 | tf_op jit(solution)/shard_map/ppermute | solution.py:45
  26.3 1.3 collective-permute-start.3
  31.1 6.3 %collective-permute-done.3.refs_2_ = f32[32,32,128]{2,1,0:T(8,128)S(1)} collective-permute-done((f32[32,32,128]{2,1,0:T(8,128)S(1)}, f32[32,32,128]{2,1,0:T(8,128)S(1)}, u32[]{:S(2)}, u32[]{:S(2)}) %collective-permute-start.3) | collective-permute-done | bytes 524320 | tf_op jit(solution)/shard_map/ppermute | solution.py:45
  38.2 1.3 collective-permute-start.4
  40.5 7.5 %collective-permute-done.8.refs_0_ = f32[64,16,128]{2,1,0:T(8,128)S(1)} collective-permute-done((f32[64,16,128]{2,1,0:T(8,128)S(1)}, f32[64,16,128]{2,1,0:T(8,128)S(1)}, u32[]{:S(2)}, u32[]{:S(2)}) %collective-permute-start.8) | collective-permute-done | bytes 524320 | tf_op jit(solution)/shard_map/ppermute | solution.py:45
  50.6 3.0 %collective-permute-done.4.refs_0_ = f32[64,16,128]{2,1,0:T(8,128)S(1)} collective-permute-done((f32[64,16,128]{2,1,0:T(8,128)S(1)}, f32[64,16,128]{2,1,0:T(8,128)S(1)}, u32[]{:S(2)}, u32[]{:S(2)}) %collective-permute-start.4) | collective-permute-done | bytes 524320 | tf_op jit(solution)/shard_map/ppermute | solution.py:45
  55.2 6.5 %collective-permute-done.10.refs_2_ = f32[32,32,128]{2,1,0:T(8,128)S(1)} collective-permute-done((f32[32,32,128]{2,1,0:T(8,128)S(1)}, f32[32,32,128]{2,1,0:T(8,128)S(1)}, u32[]{:S(2)}, u32[]{:S(2)}) %collective-permute-start.10) | collective-permute-done | bytes 524320 | tf_op jit(solution)/shard_map/ppermute | solution.py:45
  62.4 1.8 %collective-permute-start.11 = (f32[64,16,128]{2,1,0:T(8,128)S(1)}, f32[64,16,128]{2,1,0:T(8,128)S(1)}, u32[]{:S(2)}, u32[]{:S(2)}) collective-permute-start(f32[64,16,128]{2,1,0:T(8,128)S(1)} %conv_z.22.refs_1_), channel_id=1, source_target_pairs={{8,1},{1,8},{9,2},{2,9},{10,3},{3,10},{11,4},{4,11},{12,5},{5,12},... | collective-permute-start | bytes 1572872 | tf_op jit(solution)/shard_map/ppermute | solution.py:45
  65.7 1.5 %collective-permute-done.6.refs_2_ = f32[32,32,128]{2,1,0:T(8,128)S(1)} collective-permute-done((f32[32,32,128]{2,1,0:T(8,128)S(1)}, f32[32,32,128]{2,1,0:T(8,128)S(1)}, u32[]{:S(2)}, u32[]{:S(2)}) %collective-permute-start.6) | collective-permute-done | bytes 524320 | tf_op jit(solution)/shard_map/ppermute | solution.py:45
  68.8 2.3 %collective-permute-done.11.refs_0_ = f32[64,16,128]{2,1,0:T(8,128)S(1)} collective-permute-done((f32[64,16,128]{2,1,0:T(8,128)S(1)}, f32[64,16,128]{2,1,0:T(8,128)S(1)}, u32[]{:S(2)}, u32[]{:S(2)}) %collective-permute-start.11) | collective-permute-done | bytes 524320 | tf_op jit(solution)/shard_map/ppermute | solution.py:45
  72.6 4.6 %update_y.1 = (f32[2,32,32,256]{3,2,1,0:T(8,128)S(1)}, f32[64,16,128]{2,1,0:T(8,128)S(1)}, f32[64,16,128]{2,1,0:T(8,128)S(1)}, f32[32,32,128]{2,1,0:T(8,128)S(1)}, f32[32,32,128]{2,1,0:T(8,128)S(1)}) custom-call(f32[2,32,32,256]{3,2,1,0:T(8,128)S(1)} %get-tuple-element.31.refs_3_.refs_4_.est_ref, f32[64,16,128]{2,1,0:T(8,128)S(1)} %conv_z.18.e, ...), custom_call_target="tpu_custom_call" | custom-call | tf_op jit(solution)/shard_map/update_y/pallas_call | solution.py:266
  77.2 2.2 %collective-permute-start.13 = (f32[64,16,128]{2,1,0:T(8,128)S(1)}, f32[64,16,128]{2,1,0:T(8,128)S(1)}, u32[]{:S(2)}, u32[]{:S(2)}) collective-permute-start(f32[64,16,128]{2,1,0:T(8,128)S(1)} %get-tuple-element.43.refs_1_), channel_id=1, source_target_pairs={{8,1},{1,8},{9,2},{2,9},{10,3},{3,10},{11,4},{4,11},{12,5},{5,12},... | collective-permute-start | bytes 1572872 | tf_op jit(solution)/shard_map/ppermute | solution.py:45
  79.4 1.7 %collective-permute-start.19 = (f32[32,32,128]{2,1,0:T(8,128)S(1)}, f32[32,32,128]{2,1,0:T(8,128)S(1)}, u32[]{:S(2)}, u32[]{:S(2)}) collective-permute-start(f32[32,32,128]{2,1,0:T(8,128)S(1)} %get-tuple-element.45.refs_0_), channel_id=1, source_target_pairs={{0,16},{16,0},{1,17},{17,1},{2,18},{18,2},{3,19},{19,3},{4,20},{20... | collective-permute-start | bytes 1572872 | tf_op jit(solution)/shard_map/ppermute | solution.py:45
  81.1 7.7 %collective-permute-done.13.refs_0_ = f32[64,16,128]{2,1,0:T(8,128)S(1)} collective-permute-done((f32[64,16,128]{2,1,0:T(8,128)S(1)}, f32[64,16,128]{2,1,0:T(8,128)S(1)}, u32[]{:S(2)}, u32[]{:S(2)}) %collective-permute-start.13) | collective-permute-done | bytes 524320 | tf_op jit(solution)/shard_map/ppermute | solution.py:45
  89.6 1.8 %collective-permute-start.15 = (f32[32,32,128]{2,1,0:T(8,128)S(1)}, f32[32,32,128]{2,1,0:T(8,128)S(1)}, u32[]{:S(2)}, u32[]{:S(2)}) collective-permute-start(f32[32,32,128]{2,1,0:T(8,128)S(1)} %conv_x.24.refs_0_), channel_id=1, source_target_pairs={{0,16},{16,0},{1,17},{17,1},{2,18},{18,2},{3,19},{19,3},{4,20},{20... | collective-permute-start | bytes 1572872 | tf_op jit(solution)/shard_map/ppermute | solution.py:45
  91.4 1.6 %collective-permute-done.19.refs_2_ = f32[32,32,128]{2,1,0:T(8,128)S(1)} collective-permute-done((f32[32,32,128]{2,1,0:T(8,128)S(1)}, f32[32,32,128]{2,1,0:T(8,128)S(1)}, u32[]{:S(2)}, u32[]{:S(2)}) %collective-permute-start.19) | collective-permute-done | bytes 524320 | tf_op jit(solution)/shard_map/ppermute | solution.py:45
  93.7 1.4 collective-permute-start.20
  97.0 7.2 %collective-permute-done.15.refs_2_ = f32[32,32,128]{2,1,0:T(8,128)S(1)} collective-permute-done((f32[32,32,128]{2,1,0:T(8,128)S(1)}, f32[32,32,128]{2,1,0:T(8,128)S(1)}, u32[]{:S(2)}, u32[]{:S(2)}) %collective-permute-start.15) | collective-permute-done | bytes 524320 | tf_op jit(solution)/shard_map/ppermute | solution.py:45
  108.9 1.4 collective-permute-start.22
  111.1 8.5 %collective-permute-done.16.refs_0_ = f32[64,16,128]{2,1,0:T(8,128)S(1)} collective-permute-done((f32[64,16,128]{2,1,0:T(8,128)S(1)}, f32[64,16,128]{2,1,0:T(8,128)S(1)}, u32[]{:S(2)}, u32[]{:S(2)}) %collective-permute-start.16) | collective-permute-done | bytes 524320 | tf_op jit(solution)/shard_map/ppermute | solution.py:45
  120.3 1.3 collective-permute-start.18
  123.5 2.5 %collective-permute-start.23 = (f32[64,16,128]{2,1,0:T(8,128)S(1)}, f32[64,16,128]{2,1,0:T(8,128)S(1)}, u32[]{:S(2)}, u32[]{:S(2)}) collective-permute-start(f32[64,16,128]{2,1,0:T(8,128)S(1)} %conv_z.30.refs_1_), channel_id=1, source_target_pairs={{8,1},{1,8},{9,2},{2,9},{10,3},{3,10},{11,4},{4,11},{12,5},{5,12},... | collective-permute-start | bytes 1572872 | tf_op jit(solution)/shard_map/ppermute | solution.py:45
  127.6 6.3 %collective-permute-done.18.refs_2_ = f32[32,32,128]{2,1,0:T(8,128)S(1)} collective-permute-done((f32[32,32,128]{2,1,0:T(8,128)S(1)}, f32[32,32,128]{2,1,0:T(8,128)S(1)}, u32[]{:S(2)}, u32[]{:S(2)}) %collective-permute-start.18) | collective-permute-done | bytes 524320 | tf_op jit(solution)/shard_map/ppermute | solution.py:45
  135.3 3.1 %collective-permute-done.23.refs_0_ = f32[64,16,128]{2,1,0:T(8,128)S(1)} collective-permute-done((f32[64,16,128]{2,1,0:T(8,128)S(1)}, f32[64,16,128]{2,1,0:T(8,128)S(1)}, u32[]{:S(2)}, u32[]{:S(2)}) %collective-permute-start.23) | collective-permute-done | bytes 524320 | tf_op jit(solution)/shard_map/ppermute | solution.py:45
  139.9 2.6 %last_y.1 = (f32[32,32,256]{2,1,0:T(8,128)S(1)}, f32[32,32,256]{2,1,0:T(8,128)S(1)}) custom-call(s32[3]{0:T(128)S(1)} %pad_add_fusion.ids_ref, f32[2,32,32,256]{3,2,1,0:T(8,128)S(1)} %get-tuple-element.42.est_ref, f32[64,16,128]{2,1,0:T(8,128)S(1)} %conv_z.26.e, f32[64,16,128]{2,1,0:T(8,128)S(1)} %conv_z.27.i, f32[32,32,128]{2,1,0:T(8,128)S(1)} %conv_x.30.a, ...), custom_call_target="tpu_custom_call" | custom-call | tf_op jit(solution)/shard_map/last_y/pallas_call | solution.py:293
  142.6 2.6 %collective-permute-done.25.got_ref = f32[32,32,256]{2,1,0:T(8,128)S(1)} collective-permute-done((f32[32,32,256]{2,1,0:T(8,128)S(1)}, f32[32,32,256]{2,1,0:T(8,128)S(1)}, u32[]{:S(2)}, u32[]{:S(2)}) %collective-permute-start.25) | collective-permute-done | bytes 1048608 | tf_op jit(solution)/shard_map/ppermute | solution.py:45
  145.2 2.6 %whole_block.1 = f32[32,64,256]{2,1,0:T(8,128)} custom-call(s32[3]{0:T(128)S(1)} %pad_add_fusion.ids_ref, f32[32,32,256]{2,1,0:T(8,128)S(1)} %get-tuple-element.47.own_ref, f32[32,32,256]{2,1,0:T(8,128)S(1)} %collective-permute-done.25.got_ref), custom_call_target="tpu_custom_call" | custom-call | tf_op jit(solution)/shard_map/whole_block/pallas_call | solution.py:333
  (67 shorter events, 33.6 us)
Async XLA Ops:
  0.1 1.6 %copy-start = (f32[32,64,256]{2,1,0:T(8,128)S(1)}, f32[32,64,256]{2,1,0:T(8,128)}, u32[]{:S(2)}) copy-start(f32[32,64,256]{2,1,0:T(8,128)} %b_ref.1) | copy-start | bytes 6291460
  1.7 1.8 %copy-start.1 = (f32[33]{0:T(128)S(1)}, f32[33]{0:T(128)}, u32[]{:S(2)}) copy-start(f32[33]{0:T(128)} %x_ref.1) | copy-start | bytes 400
  1.7 1.8 %copy-start.2 = (f32[33]{0:T(128)S(1)}, f32[33]{0:T(128)}, u32[]{:S(2)}) copy-start(f32[33]{0:T(128)} %y_ref.1) | copy-start | bytes 400
  1.7 1.8 %copy-start.3 = (f32[65]{0:T(128)S(1)}, f32[65]{0:T(128)}, u32[]{:S(2)}) copy-start(f32[65]{0:T(128)} %z_ref.1) | copy-start | bytes 784
  2.7 5.3 %collective-permute-start = (f32[32,32,256]{2,1,0:T(8,128)S(1)}, f32[32,32,256]{2,1,0:T(8,128)S(1)}, u32[]{:S(2)}, u32[]{:S(2)}) collective-permute-start(f32[32,32,256]{2,1,0:T(8,128)S(1)} %get-tuple-element.28), channel_id=1, source_target_pairs={{0,8},{8,0},{1,9},{9,1},{2,10},{10,2},{3,11},{11,3},{4,12},{12,4},... | collective-permute-start | bytes 3145736 | tf_op jit(solution)/shard_map/ppermute | solution.py:45
  10.9 14.6 %collective-permute-start.1 = (f32[64,16,128]{2,1,0:T(8,128)S(1)}, f32[64,16,128]{2,1,0:T(8,128)S(1)}, u32[]{:S(2)}, u32[]{:S(2)}) collective-permute-start(f32[64,16,128]{2,1,0:T(8,128)S(1)} %get-tuple-element.36.refs_1_), channel_id=1, source_target_pairs={{8,1},{1,8},{9,2},{2,9},{10,3},{3,10},{11,4},{4,11},{12,5},{5,12},... | collective-permute-start | bytes 1572872 | tf_op jit(solution)/shard_map/ppermute | solution.py:45
  12.1 13.4 %collective-permute-start.2 = (f32[64,16,128]{2,1,0:T(8,128)S(1)}, f32[64,16,128]{2,1,0:T(8,128)S(1)}, u32[]{:S(2)}, u32[]{:S(2)}) collective-permute-start(f32[64,16,128]{2,1,0:T(8,128)S(1)} %get-tuple-element.37.refs_2_), channel_id=1, source_target_pairs={{0,8},{8,0},{1,9},{9,1},{2,10},{10,2},{3,11},{11,3},{4,12},{12,4},... | collective-permute-start | bytes 1572872 | tf_op jit(solution)/shard_map/ppermute | solution.py:45
  12.5 15.1 %collective-permute-start.7 = (f32[32,32,128]{2,1,0:T(8,128)S(1)}, f32[32,32,128]{2,1,0:T(8,128)S(1)}, u32[]{:S(2)}, u32[]{:S(2)}) collective-permute-start(f32[32,32,128]{2,1,0:T(8,128)S(1)} %get-tuple-element.38.refs_0_), channel_id=1, source_target_pairs={{0,16},{16,0},{1,17},{17,1},{2,18},{18,2},{3,19},{19,3},{4,20},{20... | collective-permute-start | bytes 1572872 | tf_op jit(solution)/shard_map/ppermute | solution.py:45
  26.3 11.1 %collective-permute-start.3 = (f32[32,32,128]{2,1,0:T(8,128)S(1)}, f32[32,32,128]{2,1,0:T(8,128)S(1)}, u32[]{:S(2)}, u32[]{:S(2)}) collective-permute-start(f32[32,32,128]{2,1,0:T(8,128)S(1)} %conv_x.16.refs_0_), channel_id=1, source_target_pairs={{0,16},{16,0},{1,17},{17,1},{2,18},{18,2},{3,19},{19,3},{4,20},{20... | collective-permute-start | bytes 1572872 | tf_op jit(solution)/shard_map/ppermute | solution.py:45
  28.3 19.7 %collective-permute-start.8 = (f32[64,16,128]{2,1,0:T(8,128)S(1)}, f32[64,16,128]{2,1,0:T(8,128)S(1)}, u32[]{:S(2)}, u32[]{:S(2)}) collective-permute-start(f32[64,16,128]{2,1,0:T(8,128)S(1)} %conv_z.20.refs_1_), channel_id=1, source_target_pairs={{8,1},{1,8},{9,2},{2,9},{10,3},{3,10},{11,4},{4,11},{12,5},{5,12},... | collective-permute-start | bytes 1572872 | tf_op jit(solution)/shard_map/ppermute | solution.py:45
  30.2 17.8 %collective-permute-start.9 = (f32[64,16,128]{2,1,0:T(8,128)S(1)}, f32[64,16,128]{2,1,0:T(8,128)S(1)}, u32[]{:S(2)}, u32[]{:S(2)}) collective-permute-start(f32[64,16,128]{2,1,0:T(8,128)S(1)} %conv_z.21.refs_2_), channel_id=1, source_target_pairs={{0,8},{8,0},{1,9},{9,1},{2,10},{10,2},{3,11},{11,3},{4,12},{12,4},... | collective-permute-start | bytes 1572872 | tf_op jit(solution)/shard_map/ppermute | solution.py:45
  38.2 15.4 %collective-permute-start.4 = (f32[64,16,128]{2,1,0:T(8,128)S(1)}, f32[64,16,128]{2,1,0:T(8,128)S(1)}, u32[]{:S(2)}, u32[]{:S(2)}) collective-permute-start(f32[64,16,128]{2,1,0:T(8,128)S(1)} %conv_z.16.refs_1_), channel_id=1, source_target_pairs={{8,1},{1,8},{9,2},{2,9},{10,3},{3,10},{11,4},{4,11},{12,5},{5,12},... | collective-permute-start | bytes 1572872 | tf_op jit(solution)/shard_map/ppermute | solution.py:45
  40.4 13.2 %collective-permute-start.5 = (f32[64,16,128]{2,1,0:T(8,128)S(1)}, f32[64,16,128]{2,1,0:T(8,128)S(1)}, u32[]{:S(2)}, u32[]{:S(2)}) collective-permute-start(f32[64,16,128]{2,1,0:T(8,128)S(1)} %conv_z.17.refs_2_), channel_id=1, source_target_pairs={{0,8},{8,0},{1,9},{9,1},{2,10},{10,2},{3,11},{11,3},{4,12},{12,4},... | collective-permute-start | bytes 1572872 | tf_op jit(solution)/shard_map/ppermute | solution.py:45
  48.9 12.8 %collective-permute-start.10 = (f32[32,32,128]{2,1,0:T(8,128)S(1)}, f32[32,32,128]{2,1,0:T(8,128)S(1)}, u32[]{:S(2)}, u32[]{:S(2)}) collective-permute-start(f32[32,32,128]{2,1,0:T(8,128)S(1)} %conv_x.20.refs_0_), channel_id=1, source_target_pairs={{0,16},{16,0},{1,17},{17,1},{2,18},{18,2},{3,19},{19,3},{4,20},{20... | collective-permute-start | bytes 1572872 | tf_op jit(solution)/shard_map/ppermute | solution.py:45
  54.3 12.9 %collective-permute-start.6 = (f32[32,32,128]{2,1,0:T(8,128)S(1)}, f32[32,32,128]{2,1,0:T(8,128)S(1)}, u32[]{:S(2)}, u32[]{:S(2)}) collective-permute-start(f32[32,32,128]{2,1,0:T(8,128)S(1)} %conv_x.18.refs_0_), channel_id=1, source_target_pairs={{0,16},{16,0},{1,17},{17,1},{2,18},{18,2},{3,19},{19,3},{4,20},{20... | collective-permute-start | bytes 1572872 | tf_op jit(solution)/shard_map/ppermute | solution.py:45
  62.4 8.7 %collective-permute-start.11 = (f32[64,16,128]{2,1,0:T(8,128)S(1)}, f32[64,16,128]{2,1,0:T(8,128)S(1)}, u32[]{:S(2)}, u32[]{:S(2)}) collective-permute-start(f32[64,16,128]{2,1,0:T(8,128)S(1)} %conv_z.22.refs_1_), channel_id=1, source_target_pairs={{8,1},{1,8},{9,2},{2,9},{10,3},{3,10},{11,4},{4,11},{12,5},{5,12},... | collective-permute-start | bytes 1572872 | tf_op jit(solution)/shard_map/ppermute | solution.py:45
  64.9 6.2 %collective-permute-start.12 = (f32[64,16,128]{2,1,0:T(8,128)S(1)}, f32[64,16,128]{2,1,0:T(8,128)S(1)}, u32[]{:S(2)}, u32[]{:S(2)}) collective-permute-start(f32[64,16,128]{2,1,0:T(8,128)S(1)} %conv_z.23.refs_2_), channel_id=1, source_target_pairs={{0,8},{8,0},{1,9},{9,1},{2,10},{10,2},{3,11},{11,3},{4,12},{12,4},... | collective-permute-start | bytes 1572872 | tf_op jit(solution)/shard_map/ppermute | solution.py:45
  77.2 11.7 %collective-permute-start.13 = (f32[64,16,128]{2,1,0:T(8,128)S(1)}, f32[64,16,128]{2,1,0:T(8,128)S(1)}, u32[]{:S(2)}, u32[]{:S(2)}) collective-permute-start(f32[64,16,128]{2,1,0:T(8,128)S(1)} %get-tuple-element.43.refs_1_), channel_id=1, source_target_pairs={{8,1},{1,8},{9,2},{2,9},{10,3},{3,10},{11,4},{4,11},{12,5},{5,12},... | collective-permute-start | bytes 1572872 | tf_op jit(solution)/shard_map/ppermute | solution.py:45
  79.4 9.5 %collective-permute-start.14 = (f32[64,16,128]{2,1,0:T(8,128)S(1)}, f32[64,16,128]{2,1,0:T(8,128)S(1)}, u32[]{:S(2)}, u32[]{:S(2)}) collective-permute-start(f32[64,16,128]{2,1,0:T(8,128)S(1)} %get-tuple-element.44.refs_2_), channel_id=1, source_target_pairs={{0,8},{8,0},{1,9},{9,1},{2,10},{10,2},{3,11},{11,3},{4,12},{12,4},... | collective-permute-start | bytes 1572872 | tf_op jit(solution)/shard_map/ppermute | solution.py:45
  79.4 13.6 %collective-permute-start.19 = (f32[32,32,128]{2,1,0:T(8,128)S(1)}, f32[32,32,128]{2,1,0:T(8,128)S(1)}, u32[]{:S(2)}, u32[]{:S(2)}) collective-permute-start(f32[32,32,128]{2,1,0:T(8,128)S(1)} %get-tuple-element.45.refs_0_), channel_id=1, source_target_pairs={{0,16},{16,0},{1,17},{17,1},{2,18},{18,2},{3,19},{19,3},{4,20},{20... | collective-permute-start | bytes 1572872 | tf_op jit(solution)/shard_map/ppermute | solution.py:45
  89.6 14.6 %collective-permute-start.15 = (f32[32,32,128]{2,1,0:T(8,128)S(1)}, f32[32,32,128]{2,1,0:T(8,128)S(1)}, u32[]{:S(2)}, u32[]{:S(2)}) collective-permute-start(f32[32,32,128]{2,1,0:T(8,128)S(1)} %conv_x.24.refs_0_), channel_id=1, source_target_pairs={{0,16},{16,0},{1,17},{17,1},{2,18},{18,2},{3,19},{19,3},{4,20},{20... | collective-permute-start | bytes 1572872 | tf_op jit(solution)/shard_map/ppermute | solution.py:45
  93.7 14.3 %collective-permute-start.20 = (f32[64,16,128]{2,1,0:T(8,128)S(1)}, f32[64,16,128]{2,1,0:T(8,128)S(1)}, u32[]{:S(2)}, u32[]{:S(2)}) collective-permute-start(f32[64,16,128]{2,1,0:T(8,128)S(1)} %conv_z.28.refs_1_), channel_id=1, source_target_pairs={{8,1},{1,8},{9,2},{2,9},{10,3},{3,10},{11,4},{4,11},{12,5},{5,12},... | collective-permute-start | bytes 1572872 | tf_op jit(solution)/shard_map/ppermute | solution.py:45
  95.9 12.1 %collective-permute-start.21 = (f32[64,16,128]{2,1,0:T(8,128)S(1)}, f32[64,16,128]{2,1,0:T(8,128)S(1)}, u32[]{:S(2)}, u32[]{:S(2)}) collective-permute-start(f32[64,16,128]{2,1,0:T(8,128)S(1)} %conv_z.29.refs_2_), channel_id=1, source_target_pairs={{0,8},{8,0},{1,9},{9,1},{2,10},{10,2},{3,11},{11,3},{4,12},{12,4},... | collective-permute-start | bytes 1572872 | tf_op jit(solution)/shard_map/ppermute | solution.py:45
  105.0 14.6 %collective-permute-start.16 = (f32[64,16,128]{2,1,0:T(8,128)S(1)}, f32[64,16,128]{2,1,0:T(8,128)S(1)}, u32[]{:S(2)}, u32[]{:S(2)}) collective-permute-start(f32[64,16,128]{2,1,0:T(8,128)S(1)} %conv_z.24.refs_1_), channel_id=1, source_target_pairs={{8,1},{1,8},{9,2},{2,9},{10,3},{3,10},{11,4},{4,11},{12,5},{5,12},... | collective-permute-start | bytes 1572872 | tf_op jit(solution)/shard_map/ppermute | solution.py:45
  107.1 12.6 %collective-permute-start.17 = (f32[64,16,128]{2,1,0:T(8,128)S(1)}, f32[64,16,128]{2,1,0:T(8,128)S(1)}, u32[]{:S(2)}, u32[]{:S(2)}) collective-permute-start(f32[64,16,128]{2,1,0:T(8,128)S(1)} %conv_z.25.refs_2_), channel_id=1, source_target_pairs={{0,8},{8,0},{1,9},{9,1},{2,10},{10,2},{3,11},{11,3},{4,12},{12,4},... | collective-permute-start | bytes 1572872 | tf_op jit(solution)/shard_map/ppermute | solution.py:45
  108.9 13.9 %collective-permute-start.22 = (f32[32,32,128]{2,1,0:T(8,128)S(1)}, f32[32,32,128]{2,1,0:T(8,128)S(1)}, u32[]{:S(2)}, u32[]{:S(2)}) collective-permute-start(f32[32,32,128]{2,1,0:T(8,128)S(1)} %conv_x.28.refs_0_), channel_id=1, source_target_pairs={{0,16},{16,0},{1,17},{17,1},{2,18},{18,2},{3,19},{19,3},{4,20},{20... | collective-permute-start | bytes 1572872 | tf_op jit(solution)/shard_map/ppermute | solution.py:45
  120.3 13.5 %collective-permute-start.18 = (f32[32,32,128]{2,1,0:T(8,128)S(1)}, f32[32,32,128]{2,1,0:T(8,128)S(1)}, u32[]{:S(2)}, u32[]{:S(2)}) collective-permute-start(f32[32,32,128]{2,1,0:T(8,128)S(1)} %conv_x.26.refs_0_), channel_id=1, source_target_pairs={{0,16},{16,0},{1,17},{17,1},{2,18},{18,2},{3,19},{19,3},{4,20},{20... | collective-permute-start | bytes 1572872 | tf_op jit(solution)/shard_map/ppermute | solution.py:45
  123.5 15.0 %collective-permute-start.23 = (f32[64,16,128]{2,1,0:T(8,128)S(1)}, f32[64,16,128]{2,1,0:T(8,128)S(1)}, u32[]{:S(2)}, u32[]{:S(2)}) collective-permute-start(f32[64,16,128]{2,1,0:T(8,128)S(1)} %conv_z.30.refs_1_), channel_id=1, source_target_pairs={{8,1},{1,8},{9,2},{2,9},{10,3},{3,10},{11,4},{4,11},{12,5},{5,12},... | collective-permute-start | bytes 1572872 | tf_op jit(solution)/shard_map/ppermute | solution.py:45
  126.7 11.7 %collective-permute-start.24 = (f32[64,16,128]{2,1,0:T(8,128)S(1)}, f32[64,16,128]{2,1,0:T(8,128)S(1)}, u32[]{:S(2)}, u32[]{:S(2)}) collective-permute-start(f32[64,16,128]{2,1,0:T(8,128)S(1)} %conv_z.31.refs_2_), channel_id=1, source_target_pairs={{0,8},{8,0},{1,9},{9,1},{2,10},{10,2},{3,11},{11,3},{4,12},{12,4},... | collective-permute-start | bytes 1572872 | tf_op jit(solution)/shard_map/ppermute | solution.py:45
  142.5 2.7 %collective-permute-start.25 = (f32[32,32,256]{2,1,0:T(8,128)S(1)}, f32[32,32,256]{2,1,0:T(8,128)S(1)}, u32[]{:S(2)}, u32[]{:S(2)}) collective-permute-start(f32[32,32,256]{2,1,0:T(8,128)S(1)} %get-tuple-element.48), channel_id=1, source_target_pairs={{0,8},{8,0},{1,9},{9,1},{2,10},{10,2},{3,11},{11,3},{4,12},{12,4},... | collective-permute-start | bytes 3145736 | tf_op jit(solution)/shard_map/ppermute | solution.py:45

commit v3 on v0

v3 whole, which is shorter than its diff:
```python
import jax
import jax.numpy as jnp
from jax import lax
from jax.experimental import pallas as pl
from jax.experimental.pallas import tpu as pltpu
from jax.sharding import PartitionSpec as P

ITERS = 2
COST = 30
AXES = ("zg", "gx")
F32 = jnp.float32
BF16 = jnp.bfloat16
VMEM_LIMIT = 24 * 1024 * 1024


def params():
    return pltpu.CompilerParams(vmem_limit_bytes=VMEM_LIMIT)


def cost(flops, data):
    return pl.CostEstimate(flops=int(COST * flops), bytes_accessed=int(COST * data), transcendentals=0)


def shape(*dims, dtype=F32):
    return jax.ShapeDtypeStruct(dims, dtype)


VMEM = pl.BlockSpec(memory_space=pltpu.VMEM)
SMEM = pl.BlockSpec(memory_space=pltpu.SMEM)
HBM = pl.BlockSpec(memory_space=pltpu.HBM)


def swaps(pairs):
    return [q for a, b in pairs for q in ((a, b), (b, a))]


class Links:
    def __init__(self, n_zg, n_gx):
        chips = n_zg // 2
        dev = lambda z, x: z * n_gx + x
        every = range(n_gx)
        self.inner = swaps((dev(2 * k, x), dev(2 * k + 1, x)) for k in range(chips) for x in every)
        self.x = swaps((dev(2 * k + 1, x), dev(2 * k, (x + 1) % n_gx)) for k in range(chips) for x in every)
        z_pairs = lambda first: swaps(
            (dev(2 * k + c, x), dev(2 * k + 2 + c, x)) for k in range(first, chips - 1, 2) for c in (0, 1) for x in every
        )
        self.z_even = z_pairs(0)
        self.z_odd = z_pairs(1)


def send(v, pairs):
    return lax.ppermute(v, AXES, pairs)


def split(v):
    hi = v.astype(BF16)
    return hi, (v - hi.astype(F32)).astype(BF16)


def dot(a, b):
    return jnp.dot(a, b, preferred_element_type=F32)


def band(ref, n_taps, diff):
    def step(t, carry):
        fwd, adj, total = carry
        tap = ref[t]
        return jnp.where(diff == t, tap, fwd), jnp.where(diff == n_taps - 1 - t, tap, adj), total + tap

    zero = jnp.zeros(diff.shape, F32)
    fwd, adj, total = lax.fori_loop(0, n_taps, step, (zero, zero, jnp.float32(0.0)), unroll=True)
    return fwd / total, adj / total


def places(dims, dim, size, bases):
    at = lax.broadcasted_iota(jnp.int32, dims, dim)
    place = at
    for n, base in enumerate(bases):
        place = jnp.where(at // size == n, at - n * size + base, place)
    return place


def matrices_y(kernel_y, size_y, rows_per=64):
    taps = kernel_y.shape[0]

    def body(ref, fh_ref, fl_ref, ah_ref, al_ref):
        dims = (rows_per, size_y)

        @pl.loop(0, size_y // rows_per)
        def _(k):
            at = pl.multiple_of(k * rows_per, rows_per)
            rows = pl.ds(at, rows_per)
            diff = at + lax.broadcasted_iota(jnp.int32, dims, 0) - lax.broadcasted_iota(jnp.int32, dims, 1) + (taps - 1) // 2
            fwd, adj = band(ref, taps, diff)
            fh_ref[rows, :], fl_ref[rows, :] = split(fwd)
            ah_ref[rows, :], al_ref[rows, :] = split(adj)

    out = pl.pallas_call(
        body,
        in_specs=[SMEM],
        out_specs=[VMEM] * 4,
        out_shape=[shape(size_y, size_y, dtype=BF16)] * 4,
        compiler_params=params(),
        name="matrices_y",
    )(kernel_y)
    return out[:2], out[2:]


def matrices_xz(ids, kernel_x, kernel_z, slab, group, n_pieces):
    taps_x, taps_z = kernel_x.shape[0], kernel_z.shape[0]
    m_x, k_x = 2 * group, 4 * group
    m_z, k_z = 2 * slab, n_pieces * slab

    def body(ids_ref, x_ref, z_ref, fx_ref, ax_ref, fz_ref, az_ref):
        core, par = ids_ref[0], ids_ref[1]

        e, i = group * core, group * (1 - core)
        outer, inner = -group + 3 * group * core + ids_ref[2], 2 * group - 3 * group * core
        rows = places((m_x, k_x), 0, group, (e, i))
        cols = places((m_x, k_x), 1, group, (outer, e, i, inner))
        for ref, mat in zip((fx_ref, ax_ref), band(x_ref, taps_x, cols - rows + (taps_x - 1) // 2)):
            hi, lo = split(mat)
            ref[...] = jnp.concatenate([hi, lo, hi], axis=1)

        a, b = slab * (1 - par), slab * par
        even, odd = 2 * slab - 3 * slab * par, -slab + 3 * slab * par
        rows = places((m_z, k_z), 0, slab, (a, b))
        cols = places((m_z, k_z), 1, slab, (a, b, even, odd)[:n_pieces])
        for ref, mat in zip((fz_ref, az_ref), band(z_ref, taps_z, cols - rows + (taps_z - 1) // 2)):
            hi, lo = split(mat)
            ref[...] = jnp.concatenate([hi, lo], axis=0)

    fx, ax, fz, az = pl.pallas_call(
        body,
        in_specs=[SMEM] * 3,
        out_specs=[VMEM] * 4,
        out_shape=[shape(m_x, 3 * k_x, dtype=BF16)] * 2 + [shape(2 * m_z, k_z, dtype=BF16)] * 2,
        compiler_params=params(),
        name="matrices_xz",
    )(ids, kernel_x, kernel_z)
    return (fx, fz), (ax, az)


def conv_x(mat, s, outer, e, i, inner, over):
    slab, group, lanes = e.shape

    def body(m_ref, outer_ref, e_ref, i_ref, inner_ref, *rest):
        out_ref = rest[-1]
        m = m_ref[...]
        at = s * slab
        for z in range(0, slab, 2):
            cols = [
                jnp.concatenate([outer_ref[k], e_ref[k], i_ref[at + k], inner_ref[at + k]], axis=0) for k in (z, z + 1)
            ]
            hi, lo = split(jnp.concatenate(cols, axis=1))
            res = dot(m, jnp.concatenate([hi, hi, lo], axis=0))
            for n in (0, 1):
                v = res[:, n * lanes : (n + 1) * lanes]
                if over is not None:
                    v = rest[0][s, z + n] / v
                out_ref[z + n] = v

    args = [mat, outer, e, i, inner] + ([] if over is None else [over])
    return pl.pallas_call(
        body,
        in_specs=[VMEM] * len(args),
        out_specs=VMEM,
        out_shape=shape(slab, 2 * group, lanes),
        cost_estimate=cost(2 * slab * lanes * mat.size, 4 * 6 * slab * group * lanes),
        compiler_params=params(),
        name="conv_x",
    )(*args)


def conv_z(mat, g, pieces, over):
    slab, width, lanes = pieces[0].shape
    group = width // 2
    n = len(pieces)
    m_z = 2 * slab
    outs = [shape(slab, group, lanes)] * 2 if g == 0 else [shape(m_z, group, lanes)]

    def body(m_ref, *refs):
        m = m_ref[...]
        flat = [r.reshape(slab * width, lanes) for r in refs[:n]]
        out = [r.reshape(r.shape[0] * group, lanes) for r in refs[-len(outs) :]]
        for x in range(0, group, 2):
            cols = [
                jnp.concatenate([r[pl.ds(g * group + x + j, slab, stride=width), :] for r in flat], axis=0) for j in (0, 1)
            ]
            hi, lo = split(jnp.concatenate(cols, axis=1))
            both = dot(m, hi)
            res = both[:m_z] + (both[m_z:] + dot(m[:m_z], lo))
            for j in (0, 1):
                v = res[:, j * lanes : (j + 1) * lanes]
                if over is not None:
                    v = refs[n].reshape(m_z * width, lanes)[pl.ds(g * group + x + j, m_z, stride=width), :] / v
                for r, part in zip(out, jnp.split(v, len(out), axis=0)):
                    r[pl.ds(x + j, part.shape[0], stride=group), :] = part

    args = [mat, *pieces] + ([] if over is None else [over])
    return pl.pallas_call(
        body,
        in_specs=[VMEM] * len(args),
        out_specs=[VMEM] * len(outs),
        out_shape=outs,
        cost_estimate=cost(3 * group * lanes * mat.size, 4 * (n + 3) * slab * group * lanes),
        compiler_params=params(),
        name="conv_z",
    )(*args)


def mul_y(v, hi_ref, lo_ref):
    hi, lo = split(v.reshape(-1, v.shape[-1]))
    res = dot(hi, hi_ref[...]) + (dot(hi, lo_ref[...]) + dot(lo, hi_ref[...]))
    return res.reshape(v.shape)


def take(refs, s, z, block):
    slab = refs[0].shape[0]
    left = jnp.concatenate([refs[s][z : z + block], refs[2][s * slab + z : s * slab + z + block]], axis=1)
    return jnp.concatenate([left, refs[3 + s][z : z + block]], axis=2)


def put(refs, s, z, v):
    slab, group, lanes = refs[0].shape
    block = v.shape[0]
    refs[s][z : z + block] = v[:, :group, :lanes]
    refs[2][s * slab + z : s * slab + z + block] = v[:, group:, :lanes]
    refs[3 + s][z : z + block] = v[:, :, lanes:]


def rows(pair, s, z, block):
    return jnp.concatenate([r[s, z : z + block] for r in pair], axis=2)


def put_rows(pair, s, z, v):
    for r, part in zip(pair, jnp.split(v, 2, axis=2)):
        r[s, z : z + v.shape[0]] = part


def piece_shapes(slab, group, size_y):
    half = size_y // 2
    return [shape(slab, group, half)] * 2 + [shape(2 * slab, group, half)] + [shape(slab, 2 * group, half)] * 2


def own_is_a(ids_ref):
    return ids_ref[0] != ids_ref[1]


def first_y(ids, own, received, mat, block=16):
    slab, width, size_y = own.shape

    def body(ids_ref, own_ref, got_ref, h_ref, l_ref, *refs):
        obs, outs = refs[:2], refs[2:]
        for s in (0, 1):
            mine = own_is_a(ids_ref) == (s == 0)
            for z in range(0, slab, block):
                v = jnp.where(mine, own_ref[z : z + block], got_ref[z : z + block])
                put_rows(obs, s, z, v)
                put(outs, s, z, mul_y(v, h_ref, l_ref))

    out = pl.pallas_call(
        body,
        in_specs=[SMEM] + [VMEM] * 4,
        out_specs=[VMEM] * 7,
        out_shape=[shape(2, slab, width, size_y // 2)] * 2 + piece_shapes(slab, width // 2, size_y),
        compiler_params=params(),
        name="first_y",
    )(ids, own, received, *mat)
    return out[:2], out[2:]


def update_y(estimate, parts, adj, fwd, block=16):
    _, slab, width, half = estimate[0].shape

    def body(*refs):
        est, ins, (ah_ref, al_ref, fh_ref, fl_ref), new_est, outs = refs[:2], refs[2:7], refs[7:11], refs[11:13], refs[13:]
        for s in (0, 1):
            for z in range(0, slab, block):
                new = rows(est, s, z, block) * mul_y(take(ins, s, z, block), ah_ref, al_ref)
                put_rows(new_est, s, z, new)
                put(outs, s, z, mul_y(new, fh_ref, fl_ref))

    out = pl.pallas_call(
        body,
        in_specs=[VMEM] * 11,
        out_specs=[VMEM] * 7,
        out_shape=[shape(2, slab, width, half)] * 2 + piece_shapes(slab, width // 2, 2 * half),
        compiler_params=params(),
        name="update_y",
    )(*estimate, *parts, *adj, *fwd)
    return out[:2], out[2:]


def last_slab(ids, estimate, parts, adj, mine, block=16):
    _, slab, width, half = estimate[0].shape

    def body(ids_ref, *refs):
        est, ins, (ah_ref, al_ref, out_ref) = refs[:2], refs[2:7], refs[7:]
        for s in (0, 1):

            @pl.when(own_is_a(ids_ref) == ((s == 0) == mine))
            def _(s=s):
                for z in range(0, slab, block):
                    out_ref[z : z + block] = rows(est, s, z, block) * mul_y(take(ins, s, z, block), ah_ref, al_ref)

    return pl.pallas_call(
        body,
        in_specs=[SMEM] + [VMEM] * 9,
        out_specs=VMEM,
        out_shape=shape(slab, width, 2 * half),
        compiler_params=params(),
        name="last_slab",
    )(ids, *estimate, *parts, *adj)


def outward(core, g, group):
    at = jnp.where(core == 0, g, 3 - g) * group
    return pl.ds(pl.multiple_of(at, group), group)


def half_of(ids, volume, mine):
    slab, cols, size_y = volume.shape
    group = cols // 4

    def body(ids_ref, src_ref, out_ref, sems):
        core = ids_ref[0] if mine else 1 - ids_ref[0]
        copies = [
            pltpu.make_async_copy(
                src_ref.at[:, outward(core, g, group), :], out_ref.at[:, g * group : (g + 1) * group, :], sems.at[g]
            )
            for g in (0, 1)
        ]
        for c in copies:
            c.start()
        for c in copies:
            c.wait()

    return pl.pallas_call(
        body,
        in_specs=[SMEM, HBM],
        out_specs=VMEM,
        out_shape=shape(slab, 2 * group, size_y),
        scratch_shapes=[pltpu.SemaphoreType.DMA((2,))],
        compiler_params=params(),
        name="half_of",
    )(ids, volume)


def put_half(ids, half, mine, whole=None):
    slab, width, size_y = half.shape
    group = width // 2

    def body(ids_ref, src_ref, *refs):
        out_ref, sems = refs[-2:]
        core = ids_ref[0] if mine else 1 - ids_ref[0]
        copies = [
            pltpu.make_async_copy(
                src_ref.at[:, g * group : (g + 1) * group, :], out_ref.at[:, outward(core, g, group), :], sems.at[g]
            )
            for g in (0, 1)
        ]
        for c in copies:
            c.start()
        for c in copies:
            c.wait()

    args = [ids, half] + ([] if whole is None else [whole])
    return pl.pallas_call(
        body,
        in_specs=[SMEM, VMEM] + ([] if whole is None else [HBM]),
        out_specs=HBM,
        out_shape=shape(slab, 2 * width, size_y),
        scratch_shapes=[pltpu.SemaphoreType.DMA((2,))],
        input_output_aliases={} if whole is None else {2: 0},
        compiler_params=params(),
        name="put_half",
    )(*args)


def shards(observed, kernel_x, kernel_y, kernel_z):
    n_zg, n_gx = lax.axis_size("zg"), lax.axis_size("gx")
    links = Links(n_zg, n_gx)
    slab, cols, size_y = observed.shape
    group = cols // 4
    assert (kernel_x.shape[0] - 1) // 2 <= group
    assert (kernel_z.shape[0] - 1) // 2 <= slab
    n_pieces = 4 if links.z_odd else 3
    zg, gx = lax.axis_index("zg"), lax.axis_index("gx")
    core = zg % 2
    beyond = jnp.where(gx == core * (n_gx - 1), 8 * cols, 0)
    ids = jnp.stack([core, (zg // 2) % 2, beyond]).astype(jnp.int32)

    received = send(half_of(ids, observed, False), links.inner)
    own = half_of(ids, observed, True)
    fwd_y, adj_y = matrices_y(kernel_y, size_y)
    fwd, adj = matrices_xz(ids, kernel_x, kernel_z, slab, group, n_pieces)

    def x_pass(mats, parts, over=None):
        e, i = parts[:2], parts[2]
        outer, inner = [send(v, links.x) for v in e], send(i, links.inner)
        return [conv_x(mats[0], s, outer[s], e[s], i, inner, over) for s in (0, 1)]

    def z_pass(mats, parts, over=None):
        halos = [send(v, pairs) for v, pairs in zip(parts, (links.z_even, links.z_odd)) if pairs]
        return [v for g in (0, 1) for v in conv_z(mats[1], g, [*parts, *halos], over)]

    obs, parts = first_y(ids, own, received, fwd_y)
    estimate = obs
    for step in range(ITERS):
        left, right = parts[:3], parts[3:]
        left, right = x_pass(fwd, left), z_pass(fwd, right)
        left, right = z_pass(fwd, left, obs[0]), x_pass(fwd, right, obs[1])
        left, right = x_pass(adj, left), z_pass(adj, right)
        left, right = z_pass(adj, left), x_pass(adj, right)
        parts = [*left, *right]
        if step < ITERS - 1:
            estimate, parts = update_y(estimate, parts, adj_y, fwd_y)
    received = send(last_slab(ids, estimate, parts, adj_y, False), links.inner)
    whole = put_half(ids, last_slab(ids, estimate, parts, adj_y, True), True)
    return put_half(ids, received, False, whole)


def solution(mesh):
    return jax.shard_map(
        shards,
        mesh=mesh,
        in_specs=(P("zg", "gx", None), P(), P(), P()),
        out_specs=P("zg", "gx", None),
        check_vma=False,
    )
```

time: 549 us -> 138 us (0.25)
  local copies, waits for them, and re-layouts: 182 us -> 1.61 us
  other arithmetic: 179 us -> 0.08 us
  blocking collectives: 56 us -> 0 us
  matrix products: 34.1 us -> 0 us
  waiting for transfers between devices: 42.9 us -> 76.6 us
  Pallas kernels: 0 us -> 32.4 us
  starting transfers between devices: 40 us -> 23.7 us
  loops' own time: 6.23 us -> 0 us
    add x262 -> x0, other arithmetic: 175 us -> none  [add_tap(): return acc + jnp.where(diff == tap, prof[tap], 0.0)]
    dynamic_slice x262 -> x0, local copies, waits for them, and re-layouts: 159 us -> none  [add_tap(): return acc + jnp.where(diff == tap, prof[tap], 0.0)]
    all_to_all x2 -> x0, blocking collectives: 56 us -> none  [the longest x1 28.2 us: shards(): lax.all_to_all(back_col, 'zg', split_axis=0, concat_axis=1, tiled=True)]
    dot_general x12 -> x0, matrix products: 34.1 us -> none  [the longest x4 12.3 us: lateral(): return jnp.einsum('zxj,ij->zxi', out, mat_y, precision=hp)]
    ppermute x8 -> x34, waiting for transfers between devices: 42.9 us -> 76.6 us  [send(): return lax.ppermute(v, AXES, pairs)]
    pallas_call x0 -> x42, Pallas kernels: none -> 32.4 us  [the longest x16 12.2 us: conv_z(): pl.pallas_call(body, in_specs=[VMEM] * len(args), out_specs=[VMEM] * len(...]
    all_to_all x3 -> x0, starting transfers between devices: 14.9 us -> none  [the longest x1 5.78 us: shards(): lax.all_to_all(observed, 'zg', split_axis=1, concat_axis=0, tiled=True)]
    all_to_all x5 -> x0, local copies, waits for them, and re-layouts: 10.7 us -> none  [the longest x2 4.17 us: shards(): lax.all_to_all(smeared, 'zg', split_axis=1, concat_axis=0, tiled=True)]
  transfers between devices with their start and end apart: 11 -> 34, of which waited for: 4 -> 12; matrix products, arithmetic and copies ran while one was open for 65% -> 0% of each run, Pallas kernels for 0% -> 18%
where the time goes in v3:
time: 138 us; the launch traced here: 135 us
  waiting for transfers between devices  76.6 us (56%)
  Pallas kernels  32.4 us (23%)
  starting transfers between devices  23.7 us (17%)
  local copies, waits for them, and re-layouts  1.61 us (1%)
    ppermute x34, waiting for transfers between devices, send(): return lax.ppermute(v, AXES, pairs)  76.6 us
    ppermute x34, starting transfers between devices, send(): return lax.ppermute(v, AXES, pairs)  23.7 us
    pallas_call x16, Pallas kernels, conv_z(): pl.pallas_call(body, in_specs=[VMEM] * len(args), out_specs=[VMEM] * len(...  12.2 us
    pallas_call x16, Pallas kernels, conv_x(): pl.pallas_call(body, in_specs=[VMEM] * len(args), out_specs=VMEM, out_sha...  6.61 us
    pallas_call x2, Pallas kernels, put_half(): pl.pallas_call(body, in_specs=[SMEM, VMEM] + ([] if whole is None else [H...  3.06 us
  transfers between devices with their start and end apart: 34, of which 12 were waited for; matrix products, arithmetic and copies ran while one was open for 0% of the time, Pallas kernels for 18%

profile of v3, /device:TPU:25, one launch (start us, length us, event | category | flops | bytes accessed | tf_op | source)
XLA Modules:
  0.0 134.8 jit_solution(18110533047909187051)
XLA Ops:
  0.1 1.6 %copy-done = f32[32,64,256]{2,1,0:T(8,128)S(1)} copy-done((f32[32,64,256]{2,1,0:T(8,128)S(1)}, f32[32,64,256]{2,1,0:T(8,128)}, u32[]{:S(2)}) %copy-start) | copy-done | bytes 2097176
  3.8 2.0 %matrices_y.1 = (bf16[256,256]{1,0:T(8,128)(2,1)S(1)}, bf16[256,256]{1,0:T(8,128)(2,1)S(1)}, bf16[256,256]{1,0:T(8,128)(2,1)S(1)}, bf16[256,256]{1,0:T(8,128)(2,1)S(1)}) custom-call(f32[33]{0:T(128)S(1)} %copy-done.1), custom_call_target="tpu_custom_call" | custom-call | tf_op jit(solution)/shard_map/matrices_y/pallas_call | solution.py:98
  5.8 1.6 %first_y.1 = (f32[2,32,32,128]{3,2,1,0:T(8,128)S(1)}, f32[2,32,32,128]{3,2,1,0:T(8,128)S(1)}, f32[32,16,128]{2,1,0:T(8,128)S(1)}, f32[32,16,128]{2,1,0:T(8,128)S...) custom-call(s32[3]{0:T(128)S(1)} %pad_add_fusion.ids_ref, ...), custom_call_target="tpu_custom_call" | custom-call | tf_op jit(solution)/shard_map/first_y/pallas_call | solution.py:262
  7.5 1.3 collective-permute-start.9
  8.8 1.8 %collective-permute-start.1 = (f32[32,16,128]{2,1,0:T(8,128)S(1)}, f32[32,16,128]{2,1,0:T(8,128)S(1)}, u32[]{:S(2)}, u32[]{:S(2)}) collective-permute-start(f32[32,16,128]{2,1,0:T(8,128)S(1)} %get-tuple-element.51.e_ref), channel_id=1, source_target_pairs={{8,1},{1,8},{9,2},{2,9},{10,3},{3,10},{11,4},{4,11},{12,5},{5,12},... | collective-permute-start | bytes 786440 | tf_op jit(solution)/shard_map/ppermute | solution.py:52
  11.7 8.9 %collective-permute-done.1.outer_ref = f32[32,16,128]{2,1,0:T(8,128)S(1)} collective-permute-done((f32[32,16,128]{2,1,0:T(8,128)S(1)}, f32[32,16,128]{2,1,0:T(8,128)S(1)}, u32[]{:S(2)}, u32[]{:S(2)}) %collective-permute-start.1) | collective-permute-done | bytes 262176 | tf_op jit(solution)/shard_map/ppermute | solution.py:52
  23.4 2.1 %collective-permute-start.10 = (f32[32,16,128]{2,1,0:T(8,128)S(1)}, f32[32,16,128]{2,1,0:T(8,128)S(1)}, u32[]{:S(2)}, u32[]{:S(2)}) collective-permute-start(f32[32,16,128]{2,1,0:T(8,128)S(1)} %get-tuple-element.60.e_ref), channel_id=1, source_target_pairs={{8,1},{1,8},{9,2},{2,9},{10,3},{3,10},{11,4},{4,11},{12,5},{5,12},... | collective-permute-start | bytes 786440 | tf_op jit(solution)/shard_map/ppermute | solution.py:52
  25.9 6.7 %collective-permute-done.4.refs_2_ = f32[32,32,128]{2,1,0:T(8,128)S(1)} collective-permute-done((f32[32,32,128]{2,1,0:T(8,128)S(1)}, f32[32,32,128]{2,1,0:T(8,128)S(1)}, u32[]{:S(2)}, u32[]{:S(2)}) %collective-permute-start.4) | collective-permute-done | bytes 524320 | tf_op jit(solution)/shard_map/ppermute | solution.py:52
  33.7 1.5 %collective-permute-done.10.outer_ref = f32[32,16,128]{2,1,0:T(8,128)S(1)} collective-permute-done((f32[32,16,128]{2,1,0:T(8,128)S(1)}, f32[32,16,128]{2,1,0:T(8,128)S(1)}, u32[]{:S(2)}, u32[]{:S(2)}) %collective-permute-start.10) | collective-permute-done | bytes 262176 | tf_op jit(solution)/shard_map/ppermute | solution.py:52
  35.5 1.3 collective-permute-start.13
  38.3 1.3 collective-permute-start.7
  40.0 9.1 %collective-permute-done.5.outer_ref = f32[32,16,128]{2,1,0:T(8,128)S(1)} collective-permute-done((f32[32,16,128]{2,1,0:T(8,128)S(1)}, f32[32,16,128]{2,1,0:T(8,128)S(1)}, u32[]{:S(2)}, u32[]{:S(2)}) %collective-permute-start.5) | collective-permute-done | bytes 262176 | tf_op jit(solution)/shard_map/ppermute | solution.py:52
  51.7 1.4 %collective-permute-start.16 = (f32[32,16,128]{2,1,0:T(8,128)S(1)}, f32[32,16,128]{2,1,0:T(8,128)S(1)}, u32[]{:S(2)}, u32[]{:S(2)}) collective-permute-start(f32[32,16,128]{2,1,0:T(8,128)S(1)} %get-tuple-element.63.e_ref), channel_id=1, source_target_pairs={{8,1},{1,8},{9,2},{2,9},{10,3},{3,10},{11,4},{4,11},{12,5},{5,12},... | collective-permute-start | bytes 786440 | tf_op jit(solution)/shard_map/ppermute | solution.py:52
  53.5 6.8 %collective-permute-done.8.refs_2_ = f32[32,32,128]{2,1,0:T(8,128)S(1)} collective-permute-done((f32[32,32,128]{2,1,0:T(8,128)S(1)}, f32[32,32,128]{2,1,0:T(8,128)S(1)}, u32[]{:S(2)}, u32[]{:S(2)}) %collective-permute-start.8) | collective-permute-done | bytes 524320 | tf_op jit(solution)/shard_map/ppermute | solution.py:52
  61.0 4.6 %collective-permute-done.16.outer_ref = f32[32,16,128]{2,1,0:T(8,128)S(1)} collective-permute-done((f32[32,16,128]{2,1,0:T(8,128)S(1)}, f32[32,16,128]{2,1,0:T(8,128)S(1)}, u32[]{:S(2)}, u32[]{:S(2)}) %collective-permute-start.16) | collective-permute-done | bytes 262176 | tf_op jit(solution)/shard_map/ppermute | solution.py:52
  67.1 2.2 %update_y.1 = (f32[2,32,32,128]{3,2,1,0:T(8,128)S(1)}, f32[2,32,32,128]{3,2,1,0:T(8,128)S(1)}, f32[32,16,128]{2,1,0:T(8,128)S(1)}, f32[32,16,128]{2,1,0:T(8,128)...) custom-call(f32[2,32,32,128]{3,2,1,0:T(8,128)S(1)} %get-tuple-element.45.refs_3_.refs_0_, ...), custom_call_target="tpu_custom_call" | custom-call | tf_op jit(solution)/shard_map/update_y/pallas_call | solution.py:284
  69.4 1.3 collective-permute-start.25
  70.7 1.0 collective-permute-start.17
  72.5 10.0 %collective-permute-done.17.outer_ref = f32[32,16,128]{2,1,0:T(8,128)S(1)} collective-permute-done((f32[32,16,128]{2,1,0:T(8,128)S(1)}, f32[32,16,128]{2,1,0:T(8,128)S(1)}, u32[]{:S(2)}, u32[]{:S(2)}) %collective-permute-start.17) | collective-permute-done | bytes 262176 | tf_op jit(solution)/shard_map/ppermute | solution.py:52
  86.1 1.1 collective-permute-start.28
  87.5 7.1 %collective-permute-done.20.refs_2_ = f32[32,32,128]{2,1,0:T(8,128)S(1)} collective-permute-done((f32[32,32,128]{2,1,0:T(8,128)S(1)}, f32[32,32,128]{2,1,0:T(8,128)S(1)}, u32[]{:S(2)}, u32[]{:S(2)}) %collective-permute-start.20) | collective-permute-done | bytes 524320 | tf_op jit(solution)/shard_map/ppermute | solution.py:52
  95.7 1.1 collective-permute-done.26.outer_ref
  97.2 1.3 collective-permute-start.29
  99.7 1.5 %collective-permute-start.23 = (f32[32,16,128]{2,1,0:T(8,128)S(1)}, f32[32,16,128]{2,1,0:T(8,128)S(1)}, u32[]{:S(2)}, u32[]{:S(2)}) collective-permute-start(f32[32,16,128]{2,1,0:T(8,128)S(1)} %get-tuple-element.72.e_ref), channel_id=1, source_target_pairs={{8,1},{1,8},{9,2},{2,9},{10,3},{3,10},{11,4},{4,11},{12,5},{5,12},... | collective-permute-start | bytes 786440 | tf_op jit(solution)/shard_map/ppermute | solution.py:52
  101.7 9.4 %collective-permute-done.21.outer_ref = f32[32,16,128]{2,1,0:T(8,128)S(1)} collective-permute-done((f32[32,16,128]{2,1,0:T(8,128)S(1)}, f32[32,16,128]{2,1,0:T(8,128)S(1)}, u32[]{:S(2)}, u32[]{:S(2)}) %collective-permute-start.21) | collective-permute-done | bytes 262176 | tf_op jit(solution)/shard_map/ppermute | solution.py:52
  113.4 1.7 %collective-permute-start.32 = (f32[32,16,128]{2,1,0:T(8,128)S(1)}, f32[32,16,128]{2,1,0:T(8,128)S(1)}, u32[]{:S(2)}, u32[]{:S(2)}) collective-permute-start(f32[32,16,128]{2,1,0:T(8,128)S(1)} %get-tuple-element.80.e_ref), channel_id=1, source_target_pairs={{8,1},{1,8},{9,2},{2,9},{10,3},{3,10},{11,4},{4,11},{12,5},{5,12},... | collective-permute-start | bytes 786440 | tf_op jit(solution)/shard_map/ppermute | solution.py:52
  115.5 6.8 %collective-permute-done.24.refs_2_ = f32[32,32,128]{2,1,0:T(8,128)S(1)} collective-permute-done((f32[32,32,128]{2,1,0:T(8,128)S(1)}, f32[32,32,128]{2,1,0:T(8,128)S(1)}, u32[]{:S(2)}, u32[]{:S(2)}) %collective-permute-start.24) | collective-permute-done | bytes 524320 | tf_op jit(solution)/shard_map/ppermute | solution.py:52
  123.0 4.6 %collective-permute-done.32.outer_ref = f32[32,16,128]{2,1,0:T(8,128)S(1)} collective-permute-done((f32[32,16,128]{2,1,0:T(8,128)S(1)}, f32[32,16,128]{2,1,0:T(8,128)S(1)}, u32[]{:S(2)}, u32[]{:S(2)}) %collective-permute-start.32) | collective-permute-done | bytes 262176 | tf_op jit(solution)/shard_map/ppermute | solution.py:52
  129.1 1.2 last_slab.2
  130.4 1.2 last_slab.3.src_ref
  131.6 1.5 %put_half.2.refs_0_ = f32[32,64,256]{2,1,0:T(8,128)} custom-call(s32[3]{0:T(128)S(1)} %pad_add_fusion.ids_ref, f32[32,32,256]{2,1,0:T(8,128)S(1)} %last_slab.3.src_ref), custom_call_target="tpu_custom_call" | custom-call | tf_op jit(solution)/shard_map/put_half/pallas_call | solution.py:369
  133.1 1.5 %put_half.3 = f32[32,64,256]{2,1,0:T(8,128)} custom-call(s32[3]{0:T(128)S(1)} %pad_add_fusion.ids_ref, f32[32,32,256]{2,1,0:T(8,128)S(1)} %collective-permute-done.33.src_ref, f32[32,64,256]{2,1,0:T(8,128)} %put_half.2.refs_0_), custom_call_target="tpu_custom_call", output_to_operand_aliasing={{}: (2, {})} | custom-call | tf_op jit(solution)/shard_map/put_half/pallas_call | solution.py:369
  (87 shorter events, 27.8 us)
Async XLA Ops:
  7.4 13.2 %collective-permute-start.2 = (f32[64,16,128]{2,1,0:T(8,128)S(1)}, f32[64,16,128]{2,1,0:T(8,128)S(1)}, u32[]{:S(2)}, u32[]{:S(2)}) collective-permute-start(f32[64,16,128]{2,1,0:T(8,128)S(1)} %get-tuple-element.52.i_ref), channel_id=1, source_target_pairs={{0,8},{8,0},{1,9},{9,1},{2,10},{10,2},{3,11},{11,3},{4,12},{12,4},... | collective-permute-start | bytes 1572872 | tf_op jit(solution)/shard_map/ppermute | solution.py:52
  7.5 13.7 %collective-permute-start.9 = (f32[32,32,128]{2,1,0:T(8,128)S(1)}, f32[32,32,128]{2,1,0:T(8,128)S(1)}, u32[]{:S(2)}, u32[]{:S(2)}) collective-permute-start(f32[32,32,128]{2,1,0:T(8,128)S(1)} %get-tuple-element.58.refs_0_), channel_id=1, source_target_pairs={{0,16},{16,0},{1,17},{17,1},{2,18},{18,2},{3,19},{19,3},{4,20},{20... | collective-permute-start | bytes 1572872 | tf_op jit(solution)/shard_map/ppermute | solution.py:52
  8.8 11.8 %collective-permute-start.1 = (f32[32,16,128]{2,1,0:T(8,128)S(1)}, f32[32,16,128]{2,1,0:T(8,128)S(1)}, u32[]{:S(2)}, u32[]{:S(2)}) collective-permute-start(f32[32,16,128]{2,1,0:T(8,128)S(1)} %get-tuple-element.51.e_ref), channel_id=1, source_target_pairs={{8,1},{1,8},{9,2},{2,9},{10,3},{3,10},{11,4},{4,11},{12,5},{5,12},... | collective-permute-start | bytes 786440 | tf_op jit(solution)/shard_map/ppermute | solution.py:52
  11.6 14.0 %collective-permute-start.3 = (f32[32,16,128]{2,1,0:T(8,128)S(1)}, f32[32,16,128]{2,1,0:T(8,128)S(1)}, u32[]{:S(2)}, u32[]{:S(2)}) collective-permute-start(f32[32,16,128]{2,1,0:T(8,128)S(1)} %get-tuple-element.53.e_ref), channel_id=1, source_target_pairs={{8,1},{1,8},{9,2},{2,9},{10,3},{3,10},{11,4},{4,11},{12,5},{5,12},... | collective-permute-start | bytes 786440 | tf_op jit(solution)/shard_map/ppermute | solution.py:52
  21.0 11.7 %collective-permute-start.4 = (f32[32,32,128]{2,1,0:T(8,128)S(1)}, f32[32,32,128]{2,1,0:T(8,128)S(1)}, u32[]{:S(2)}, u32[]{:S(2)}) collective-permute-start(f32[32,32,128]{2,1,0:T(8,128)S(1)} %conv_x.16.refs_0_), channel_id=1, source_target_pairs={{0,16},{16,0},{1,17},{17,1},{2,18},{18,2},{3,19},{19,3},{4,20},{20... | collective-permute-start | bytes 1572872 | tf_op jit(solution)/shard_map/ppermute | solution.py:52
  22.0 13.1 %collective-permute-start.11 = (f32[64,16,128]{2,1,0:T(8,128)S(1)}, f32[64,16,128]{2,1,0:T(8,128)S(1)}, u32[]{:S(2)}, u32[]{:S(2)}) collective-permute-start(f32[64,16,128]{2,1,0:T(8,128)S(1)} %conv_z.21.i_ref), channel_id=1, source_target_pairs={{0,8},{8,0},{1,9},{9,1},{2,10},{10,2},{3,11},{11,3},{4,12},{12,4},... | collective-permute-start | bytes 1572872 | tf_op jit(solution)/shard_map/ppermute | solution.py:52
  23.4 11.7 %collective-permute-start.10 = (f32[32,16,128]{2,1,0:T(8,128)S(1)}, f32[32,16,128]{2,1,0:T(8,128)S(1)}, u32[]{:S(2)}, u32[]{:S(2)}) collective-permute-start(f32[32,16,128]{2,1,0:T(8,128)S(1)} %get-tuple-element.60.e_ref), channel_id=1, source_target_pairs={{8,1},{1,8},{9,2},{2,9},{10,3},{3,10},{11,4},{4,11},{12,5},{5,12},... | collective-permute-start | bytes 786440 | tf_op jit(solution)/shard_map/ppermute | solution.py:52
  25.5 14.1 %collective-permute-start.12 = (f32[32,16,128]{2,1,0:T(8,128)S(1)}, f32[32,16,128]{2,1,0:T(8,128)S(1)}, u32[]{:S(2)}, u32[]{:S(2)}) collective-permute-start(f32[32,16,128]{2,1,0:T(8,128)S(1)} %get-tuple-element.61.e_ref), channel_id=1, source_target_pairs={{8,1},{1,8},{9,2},{2,9},{10,3},{3,10},{11,4},{4,11},{12,5},{5,12},... | collective-permute-start | bytes 786440 | tf_op jit(solution)/shard_map/ppermute | solution.py:52
  33.6 15.5 %collective-permute-start.6 = (f32[64,16,128]{2,1,0:T(8,128)S(1)}, f32[64,16,128]{2,1,0:T(8,128)S(1)}, u32[]{:S(2)}, u32[]{:S(2)}) collective-permute-start(f32[64,16,128]{2,1,0:T(8,128)S(1)} %conv_z.17.i_ref), channel_id=1, source_target_pairs={{0,8},{8,0},{1,9},{9,1},{2,10},{10,2},{3,11},{11,3},{4,12},{12,4},... | collective-permute-start | bytes 1572872 | tf_op jit(solution)/shard_map/ppermute | solution.py:52
  35.5 14.2 %collective-permute-start.13 = (f32[32,32,128]{2,1,0:T(8,128)S(1)}, f32[32,32,128]{2,1,0:T(8,128)S(1)}, u32[]{:S(2)}, u32[]{:S(2)}) collective-permute-start(f32[32,32,128]{2,1,0:T(8,128)S(1)} %conv_x.20.refs_0_), channel_id=1, source_target_pairs={{0,16},{16,0},{1,17},{17,1},{2,18},{18,2},{3,19},{19,3},{4,20},{20... | collective-permute-start | bytes 1572872 | tf_op jit(solution)/shard_map/ppermute | solution.py:52
  37.8 11.3 %collective-permute-start.5 = (f32[32,16,128]{2,1,0:T(8,128)S(1)}, f32[32,16,128]{2,1,0:T(8,128)S(1)}, u32[]{:S(2)}, u32[]{:S(2)}) collective-permute-start(f32[32,16,128]{2,1,0:T(8,128)S(1)} %get-tuple-element.54.e_ref), channel_id=1, source_target_pairs={{8,1},{1,8},{9,2},{2,9},{10,3},{3,10},{11,4},{4,11},{12,5},{5,12},... | collective-permute-start | bytes 786440 | tf_op jit(solution)/shard_map/ppermute | solution.py:52
  38.3 14.8 %collective-permute-start.7 = (f32[32,16,128]{2,1,0:T(8,128)S(1)}, f32[32,16,128]{2,1,0:T(8,128)S(1)}, u32[]{:S(2)}, u32[]{:S(2)}) collective-permute-start(f32[32,16,128]{2,1,0:T(8,128)S(1)} %get-tuple-element.55.e_ref), channel_id=1, source_target_pairs={{8,1},{1,8},{9,2},{2,9},{10,3},{3,10},{11,4},{4,11},{12,5},{5,12},... | collective-permute-start | bytes 786440 | tf_op jit(solution)/shard_map/ppermute | solution.py:52
  49.5 10.8 %collective-permute-start.8 = (f32[32,32,128]{2,1,0:T(8,128)S(1)}, f32[32,32,128]{2,1,0:T(8,128)S(1)}, u32[]{:S(2)}, u32[]{:S(2)}) collective-permute-start(f32[32,32,128]{2,1,0:T(8,128)S(1)} %conv_x.18.refs_0_), channel_id=1, source_target_pairs={{0,16},{16,0},{1,17},{17,1},{2,18},{18,2},{3,19},{19,3},{4,20},{20... | collective-permute-start | bytes 1572872 | tf_op jit(solution)/shard_map/ppermute | solution.py:52
  50.5 15.1 %collective-permute-start.15 = (f32[64,16,128]{2,1,0:T(8,128)S(1)}, f32[64,16,128]{2,1,0:T(8,128)S(1)}, u32[]{:S(2)}, u32[]{:S(2)}) collective-permute-start(f32[64,16,128]{2,1,0:T(8,128)S(1)} %conv_z.23.i_ref), channel_id=1, source_target_pairs={{0,8},{8,0},{1,9},{9,1},{2,10},{10,2},{3,11},{11,3},{4,12},{12,4},... | collective-permute-start | bytes 1572872 | tf_op jit(solution)/shard_map/ppermute | solution.py:52
  51.3 15.4 %collective-permute-start.14 = (f32[32,16,128]{2,1,0:T(8,128)S(1)}, f32[32,16,128]{2,1,0:T(8,128)S(1)}, u32[]{:S(2)}, u32[]{:S(2)}) collective-permute-start(f32[32,16,128]{2,1,0:T(8,128)S(1)} %get-tuple-element.62.e_ref), channel_id=1, source_target_pairs={{8,1},{1,8},{9,2},{2,9},{10,3},{3,10},{11,4},{4,11},{12,5},{5,12},... | collective-permute-start | bytes 786440 | tf_op jit(solution)/shard_map/ppermute | solution.py:52
  51.7 13.9 %collective-permute-start.16 = (f32[32,16,128]{2,1,0:T(8,128)S(1)}, f32[32,16,128]{2,1,0:T(8,128)S(1)}, u32[]{:S(2)}, u32[]{:S(2)}) collective-permute-start(f32[32,16,128]{2,1,0:T(8,128)S(1)} %get-tuple-element.63.e_ref), channel_id=1, source_target_pairs={{8,1},{1,8},{9,2},{2,9},{10,3},{3,10},{11,4},{4,11},{12,5},{5,12},... | collective-permute-start | bytes 786440 | tf_op jit(solution)/shard_map/ppermute | solution.py:52
  69.3 13.1 %collective-permute-start.18 = (f32[64,16,128]{2,1,0:T(8,128)S(1)}, f32[64,16,128]{2,1,0:T(8,128)S(1)}, u32[]{:S(2)}, u32[]{:S(2)}) collective-permute-start(f32[64,16,128]{2,1,0:T(8,128)S(1)} %get-tuple-element.69.i_ref), channel_id=1, source_target_pairs={{0,8},{8,0},{1,9},{9,1},{2,10},{10,2},{3,11},{11,3},{4,12},{12,4},... | collective-permute-start | bytes 1572872 | tf_op jit(solution)/shard_map/ppermute | solution.py:52
  69.4 13.9 %collective-permute-start.25 = (f32[32,32,128]{2,1,0:T(8,128)S(1)}, f32[32,32,128]{2,1,0:T(8,128)S(1)}, u32[]{:S(2)}, u32[]{:S(2)}) collective-permute-start(f32[32,32,128]{2,1,0:T(8,128)S(1)} %get-tuple-element.75.refs_0_), channel_id=1, source_target_pairs={{0,16},{16,0},{1,17},{17,1},{2,18},{18,2},{3,19},{19,3},{4,20},{20... | collective-permute-start | bytes 1572872 | tf_op jit(solution)/shard_map/ppermute | solution.py:52
  70.7 11.7 %collective-permute-start.17 = (f32[32,16,128]{2,1,0:T(8,128)S(1)}, f32[32,16,128]{2,1,0:T(8,128)S(1)}, u32[]{:S(2)}, u32[]{:S(2)}) collective-permute-start(f32[32,16,128]{2,1,0:T(8,128)S(1)} %get-tuple-element.68.e_ref), channel_id=1, source_target_pairs={{8,1},{1,8},{9,2},{2,9},{10,3},{3,10},{11,4},{4,11},{12,5},{5,12},... | collective-permute-start | bytes 786440 | tf_op jit(solution)/shard_map/ppermute | solution.py:52
  71.7 15.4 %collective-permute-start.19 = (f32[32,16,128]{2,1,0:T(8,128)S(1)}, f32[32,16,128]{2,1,0:T(8,128)S(1)}, u32[]{:S(2)}, u32[]{:S(2)}) collective-permute-start(f32[32,16,128]{2,1,0:T(8,128)S(1)} %get-tuple-element.70.e_ref), channel_id=1, source_target_pairs={{8,1},{1,8},{9,2},{2,9},{10,3},{3,10},{11,4},{4,11},{12,5},{5,12},... | collective-permute-start | bytes 786440 | tf_op jit(solution)/shard_map/ppermute | solution.py:52
  83.0 11.7 %collective-permute-start.20 = (f32[32,32,128]{2,1,0:T(8,128)S(1)}, f32[32,32,128]{2,1,0:T(8,128)S(1)}, u32[]{:S(2)}, u32[]{:S(2)}) collective-permute-start(f32[32,32,128]{2,1,0:T(8,128)S(1)} %conv_x.24.refs_0_), channel_id=1, source_target_pairs={{0,16},{16,0},{1,17},{17,1},{2,18},{18,2},{3,19},{19,3},{4,20},{20... | collective-permute-start | bytes 1572872 | tf_op jit(solution)/shard_map/ppermute | solution.py:52
  84.0 12.8 %collective-permute-start.27 = (f32[64,16,128]{2,1,0:T(8,128)S(1)}, f32[64,16,128]{2,1,0:T(8,128)S(1)}, u32[]{:S(2)}, u32[]{:S(2)}) collective-permute-start(f32[64,16,128]{2,1,0:T(8,128)S(1)} %conv_z.29.i_ref), channel_id=1, source_target_pairs={{0,8},{8,0},{1,9},{9,1},{2,10},{10,2},{3,11},{11,3},{4,12},{12,4},... | collective-permute-start | bytes 1572872 | tf_op jit(solution)/shard_map/ppermute | solution.py:52
  85.3 11.5 %collective-permute-start.26 = (f32[32,16,128]{2,1,0:T(8,128)S(1)}, f32[32,16,128]{2,1,0:T(8,128)S(1)}, u32[]{:S(2)}, u32[]{:S(2)}) collective-permute-start(f32[32,16,128]{2,1,0:T(8,128)S(1)} %get-tuple-element.77.e_ref), channel_id=1, source_target_pairs={{8,1},{1,8},{9,2},{2,9},{10,3},{3,10},{11,4},{4,11},{12,5},{5,12},... | collective-permute-start | bytes 786440 | tf_op jit(solution)/shard_map/ppermute | solution.py:52
  86.1 15.2 %collective-permute-start.28 = (f32[32,16,128]{2,1,0:T(8,128)S(1)}, f32[32,16,128]{2,1,0:T(8,128)S(1)}, u32[]{:S(2)}, u32[]{:S(2)}) collective-permute-start(f32[32,16,128]{2,1,0:T(8,128)S(1)} %get-tuple-element.78.e_ref), channel_id=1, source_target_pairs={{8,1},{1,8},{9,2},{2,9},{10,3},{3,10},{11,4},{4,11},{12,5},{5,12},... | collective-permute-start | bytes 786440 | tf_op jit(solution)/shard_map/ppermute | solution.py:52
  95.6 15.5 %collective-permute-start.22 = (f32[64,16,128]{2,1,0:T(8,128)S(1)}, f32[64,16,128]{2,1,0:T(8,128)S(1)}, u32[]{:S(2)}, u32[]{:S(2)}) collective-permute-start(f32[64,16,128]{2,1,0:T(8,128)S(1)} %conv_z.25.i_ref), channel_id=1, source_target_pairs={{0,8},{8,0},{1,9},{9,1},{2,10},{10,2},{3,11},{11,3},{4,12},{12,4},... | collective-permute-start | bytes 1572872 | tf_op jit(solution)/shard_map/ppermute | solution.py:52
  97.2 14.6 %collective-permute-start.29 = (f32[32,32,128]{2,1,0:T(8,128)S(1)}, f32[32,32,128]{2,1,0:T(8,128)S(1)}, u32[]{:S(2)}, u32[]{:S(2)}) collective-permute-start(f32[32,32,128]{2,1,0:T(8,128)S(1)} %conv_x.28.refs_0_), channel_id=1, source_target_pairs={{0,16},{16,0},{1,17},{17,1},{2,18},{18,2},{3,19},{19,3},{4,20},{20... | collective-permute-start | bytes 1572872 | tf_op jit(solution)/shard_map/ppermute | solution.py:52
  99.5 11.6 %collective-permute-start.21 = (f32[32,16,128]{2,1,0:T(8,128)S(1)}, f32[32,16,128]{2,1,0:T(8,128)S(1)}, u32[]{:S(2)}, u32[]{:S(2)}) collective-permute-start(f32[32,16,128]{2,1,0:T(8,128)S(1)} %get-tuple-element.71.e_ref), channel_id=1, source_target_pairs={{8,1},{1,8},{9,2},{2,9},{10,3},{3,10},{11,4},{4,11},{12,5},{5,12},... | collective-permute-start | bytes 786440 | tf_op jit(solution)/shard_map/ppermute | solution.py:52
  99.7 15.4 %collective-permute-start.23 = (f32[32,16,128]{2,1,0:T(8,128)S(1)}, f32[32,16,128]{2,1,0:T(8,128)S(1)}, u32[]{:S(2)}, u32[]{:S(2)}) collective-permute-start(f32[32,16,128]{2,1,0:T(8,128)S(1)} %get-tuple-element.72.e_ref), channel_id=1, source_target_pairs={{8,1},{1,8},{9,2},{2,9},{10,3},{3,10},{11,4},{4,11},{12,5},{5,12},... | collective-permute-start | bytes 786440 | tf_op jit(solution)/shard_map/ppermute | solution.py:52
  111.5 10.8 %collective-permute-start.24 = (f32[32,32,128]{2,1,0:T(8,128)S(1)}, f32[32,32,128]{2,1,0:T(8,128)S(1)}, u32[]{:S(2)}, u32[]{:S(2)}) collective-permute-start(f32[32,32,128]{2,1,0:T(8,128)S(1)} %conv_x.26.refs_0_), channel_id=1, source_target_pairs={{0,16},{16,0},{1,17},{17,1},{2,18},{18,2},{3,19},{19,3},{4,20},{20... | collective-permute-start | bytes 1572872 | tf_op jit(solution)/shard_map/ppermute | solution.py:52
  112.5 15.1 %collective-permute-start.31 = (f32[64,16,128]{2,1,0:T(8,128)S(1)}, f32[64,16,128]{2,1,0:T(8,128)S(1)}, u32[]{:S(2)}, u32[]{:S(2)}) collective-permute-start(f32[64,16,128]{2,1,0:T(8,128)S(1)} %conv_z.31.i_ref), channel_id=1, source_target_pairs={{0,8},{8,0},{1,9},{9,1},{2,10},{10,2},{3,11},{11,3},{4,12},{12,4},... | collective-permute-start | bytes 1572872 | tf_op jit(solution)/shard_map/ppermute | solution.py:52
  113.3 15.4 %collective-permute-start.30 = (f32[32,16,128]{2,1,0:T(8,128)S(1)}, f32[32,16,128]{2,1,0:T(8,128)S(1)}, u32[]{:S(2)}, u32[]{:S(2)}) collective-permute-start(f32[32,16,128]{2,1,0:T(8,128)S(1)} %get-tuple-element.79.e_ref), channel_id=1, source_target_pairs={{8,1},{1,8},{9,2},{2,9},{10,3},{3,10},{11,4},{4,11},{12,5},{5,12},... | collective-permute-start | bytes 786440 | tf_op jit(solution)/shard_map/ppermute | solution.py:52
  113.4 14.2 %collective-permute-start.32 = (f32[32,16,128]{2,1,0:T(8,128)S(1)}, f32[32,16,128]{2,1,0:T(8,128)S(1)}, u32[]{:S(2)}, u32[]{:S(2)}) collective-permute-start(f32[32,16,128]{2,1,0:T(8,128)S(1)} %get-tuple-element.80.e_ref), channel_id=1, source_target_pairs={{8,1},{1,8},{9,2},{2,9},{10,3},{3,10},{11,4},{4,11},{12,5},{5,12},... | collective-permute-start | bytes 786440 | tf_op jit(solution)/shard_map/ppermute | solution.py:52
  (6 other events, 25.7 us)

commit v4 on v3

--- a/solution.py
+++ b/solution.py
@@ -6,7 +6,7 @@
 from jax.sharding import PartitionSpec as P
 
 ITERS = 2
-COST = 30
+COST_X, COST_Z = 45, 30
 AXES = ("zg", "gx")
 F32 = jnp.float32
 BF16 = jnp.bfloat16
@@ -17,8 +17,8 @@
     return pltpu.CompilerParams(vmem_limit_bytes=VMEM_LIMIT)
 
 
-def cost(flops, data):
-    return pl.CostEstimate(flops=int(COST * flops), bytes_accessed=int(COST * data), transcendentals=0)
+def cost(scale, flops, data):
+    return pl.CostEstimate(flops=int(scale * flops), bytes_accessed=int(scale * data), transcendentals=0)
 
 
 def shape(*dims, dtype=F32):
@@ -141,11 +141,14 @@
     return (fx, fz), (ax, az)
 
 
-def conv_x(mat, s, outer, e, i, inner, over):
+def conv_x(mat, s, outer, e, i, inner, over, later=None):
     slab, group, lanes = e.shape
+    n_out = 1 if later is None else 2
 
     def body(m_ref, outer_ref, e_ref, i_ref, inner_ref, *rest):
-        out_ref = rest[-1]
+        out_ref = rest[-n_out]
+        if later is not None:
+            rest[-1][...] = rest[-n_out - 1][...]
         m = m_ref[...]
         at = s * slab
         for z in range(0, slab, 2):
@@ -160,13 +163,13 @@
                     v = rest[0][s, z + n] / v
                 out_ref[z + n] = v
 
-    args = [mat, outer, e, i, inner] + ([] if over is None else [over])
+    args = [mat, outer, e, i, inner] + ([] if over is None else [over]) + ([] if later is None else [later])
     return pl.pallas_call(
         body,
         in_specs=[VMEM] * len(args),
-        out_specs=VMEM,
-        out_shape=shape(slab, 2 * group, lanes),
-        cost_estimate=cost(2 * slab * lanes * mat.size, 4 * 6 * slab * group * lanes),
+        out_specs=[VMEM] * n_out,
+        out_shape=[shape(slab, 2 * group, lanes)] + ([] if later is None else [shape(*later.shape)]),
+        cost_estimate=cost(COST_X, 2 * slab * lanes * mat.size, 4 * 6 * slab * group * lanes),
         compiler_params=params(),
         name="conv_x",
     )(*args)
@@ -203,7 +206,7 @@
         in_specs=[VMEM] * len(args),
         out_specs=[VMEM] * len(outs),
         out_shape=outs,
-        cost_estimate=cost(3 * group * lanes * mat.size, 4 * (n + 3) * slab * group * lanes),
+        cost_estimate=cost(COST_Z, 3 * group * lanes * mat.size, 4 * (n + 3) * slab * group * lanes),
         compiler_params=params(),
         name="conv_z",
     )(*args)
@@ -378,6 +381,68 @@
     )(*args)
 
 
+class Chunk:
+    def __init__(self, links, mats, over, parts):
+        self.links, self.mats, self.over = links, mats, over
+        self.parts, self.op, self.out = list(parts), 0, []
+
+    def mat(self, dim):
+        return self.mats[self.op // 2][dim]
+
+    def numerator(self):
+        return self.over if self.op == 1 else None
+
+    def send_x(self, *which):
+        for n in which:
+            self.halos[n] = send(self.parts[n], self.links.inner if n == 2 else self.links.x)
+
+    def send_z(self, s, slab):
+        pairs = (self.links.z_even, self.links.z_odd)[s]
+        if pairs:
+            self.halos.append(send(slab, pairs))
+
+    def x(self, s, later=None):
+        (e, i), (outer, inner) = ((v[s], v[2]) for v in (self.parts, self.halos))
+        out, *late = conv_x(self.mat(0), s, outer, e, i, inner, self.numerator(), later)
+        self.out.append(out)
+        if s == 1:
+            self.turn([])
+            self.send_z(0, self.parts[0])
+            self.send_z(1, self.parts[1])
+        return late[0] if late else None
+
+    def z(self, g):
+        self.out += conv_z(self.mat(1), g, [*self.parts, *self.halos], self.numerator())
+
+    def turn(self, halos):
+        self.parts, self.out, self.halos = self.out, [], halos
+        self.op += 1
+
+
+def iteration(links, mats, obs, parts):
+    left, right = Chunk(links, mats, obs[0], parts[:3]), Chunk(links, mats, obs[1], parts[3:])
+    left.halos, right.halos = [None] * 3, []
+    left.send_x(2, 0)
+    right.send_z(0, parts[3])
+    right.send_z(1, parts[4])
+    left.send_x(1)
+    left.x(0)
+    for half in range(4):
+        c, other = (right, left) if half % 2 == 0 else (left, right)
+        c.z(0)
+        c.z(1)
+        if half == 3:
+            c.turn([])
+            other.x(1)
+            break
+        late = other.x(1, c.out[1])
+        c.turn([None] * 3)
+        c.parts[1] = late
+        c.send_x(0, 2, 1)
+        c.x(0)
+    return [*left.parts, *right.parts]
+
+
 def shards(observed, kernel_x, kernel_y, kernel_z):
     n_zg, n_gx = lax.axis_size("zg"), lax.axis_size("gx")
     links = Links(n_zg, n_gx)
@@ -396,24 +461,10 @@
     fwd_y, adj_y = matrices_y(kernel_y, size_y)
     fwd, adj = matrices_xz(ids, kernel_x, kernel_z, slab, group, n_pieces)
 
-    def x_pass(mats, parts, over=None):
-        e, i = parts[:2], parts[2]
-        outer, inner = [send(v, links.x) for v in e], send(i, links.inner)
-        return [conv_x(mats[0], s, outer[s], e[s], i, inner, over) for s in (0, 1)]
-
-    def z_pass(mats, parts, over=None):
-        halos = [send(v, pairs) for v, pairs in zip(parts, (links.z_even, links.z_odd)) if pairs]
-        return [v for g in (0, 1) for v in conv_z(mats[1], g, [*parts, *halos], over)]
-
     obs, parts = first_y(ids, own, received, fwd_y)
     estimate = obs
     for step in range(ITERS):
-        left, right = parts[:3], parts[3:]
-        left, right = x_pass(fwd, left), z_pass(fwd, right)
-        left, right = z_pass(fwd, left, obs[0]), x_pass(fwd, right, obs[1])
-        left, right = x_pass(adj, left), z_pass(adj, right)
-        left, right = z_pass(adj, left), x_pass(adj, right)
-        parts = [*left, *right]
+        parts = iteration(links, (fwd, adj), obs, parts)
         if step < ITERS - 1:
             estimate, parts = update_y(estimate, parts, adj_y, fwd_y)
     received = send(last_slab(ids, estimate, parts, adj_y, False), links.inner)

time: 138 us -> 132 us (0.957)
  waiting for transfers between devices: 76.6 us -> 71.7 us
    ppermute x34, waiting for transfers between devices: 76.6 us -> 71.7 us  [send(): return lax.ppermute(v, AXES, pairs)]
  transfers between devices with their start and end apart: 34 -> 34, of which waited for: 12 -> 15; matrix products, arithmetic and copies ran while one was open for 0% -> 0% of each run, Pallas kernels for 18% -> 19%
where the time goes in v4:
time: 132 us; the launch traced here: 130 us
  waiting for transfers between devices  71.7 us (54%)
  Pallas kernels  32.5 us (25%)
  starting transfers between devices  23.5 us (18%)
  local copies, waits for them, and re-layouts  1.61 us (1%)
    ppermute x34, waiting for transfers between devices, send(): return lax.ppermute(v, AXES, pairs)  71.7 us
    ppermute x34, starting transfers between devices, send(): return lax.ppermute(v, AXES, pairs)  23.5 us
    pallas_call x16, Pallas kernels, conv_z(): pl.pallas_call(body, in_specs=[VMEM] * len(args), out_specs=[VMEM] * len(...  12.2 us
    pallas_call x16, Pallas kernels, conv_x(): pl.pallas_call(body, in_specs=[VMEM] * len(args), out_specs=[VMEM] * n_ou...  6.75 us
    pallas_call x2, Pallas kernels, put_half(): pl.pallas_call(body, in_specs=[SMEM, VMEM] + ([] if whole is None else [H...  3.06 us
  transfers between devices with their start and end apart: 34, of which 15 were waited for; matrix products, arithmetic and copies ran while one was open for 0% of the time, Pallas kernels for 19%

profile of v4, /device:TPU:25, one launch (start us, length us, event | category | flops | bytes accessed | tf_op | source)
XLA Modules:
  0.0 129.9 jit_solution(9672311421418669208)
XLA Ops:
  0.1 1.6 %copy-done = f32[32,64,256]{2,1,0:T(8,128)S(1)} copy-done((f32[32,64,256]{2,1,0:T(8,128)S(1)}, f32[32,64,256]{2,1,0:T(8,128)}, u32[]{:S(2)}) %copy-start) | copy-done | bytes 2097176
  3.8 2.0 %matrices_y.1 = (bf16[256,256]{1,0:T(8,128)(2,1)S(1)}, bf16[256,256]{1,0:T(8,128)(2,1)S(1)}, bf16[256,256]{1,0:T(8,128)(2,1)S(1)}, bf16[256,256]{1,0:T(8,128)(2,1)S(1)}) custom-call(f32[33]{0:T(128)S(1)} %copy-done.1), custom_call_target="tpu_custom_call" | custom-call | tf_op jit(solution)/shard_map/matrices_y/pallas_call | solution.py:98
  5.8 1.6 %first_y.1 = (f32[2,32,32,128]{3,2,1,0:T(8,128)S(1)}, f32[2,32,32,128]{3,2,1,0:T(8,128)S(1)}, f32[32,16,128]{2,1,0:T(8,128)S(1)}, f32[32,16,128]{2,1,0:T(8,128)S...) custom-call(s32[3]{0:T(128)S(1)} %pad_add_fusion.ids_ref, ...), custom_call_target="tpu_custom_call" | custom-call | tf_op jit(solution)/shard_map/first_y/pallas_call | solution.py:265
  7.5 1.3 collective-permute-start.4
  8.8 1.8 %collective-permute-start.1 = (f32[32,16,128]{2,1,0:T(8,128)S(1)}, f32[32,16,128]{2,1,0:T(8,128)S(1)}, u32[]{:S(2)}, u32[]{:S(2)}) collective-permute-start(f32[32,16,128]{2,1,0:T(8,128)S(1)} %get-tuple-element.63.e_ref), channel_id=1, source_target_pairs={{8,1},{1,8},{9,2},{2,9},{10,3},{3,10},{11,4},{4,11},{12,5},{5,12},... | collective-permute-start | bytes 786440 | tf_op jit(solution)/shard_map/ppermute | solution.py:52
  11.7 8.9 %collective-permute-done.1.outer_ref = f32[32,16,128]{2,1,0:T(8,128)S(1)} collective-permute-done((f32[32,16,128]{2,1,0:T(8,128)S(1)}, f32[32,16,128]{2,1,0:T(8,128)S(1)}, u32[]{:S(2)}, u32[]{:S(2)}) %collective-permute-start.1) | collective-permute-done | bytes 262176 | tf_op jit(solution)/shard_map/ppermute | solution.py:52
  23.4 2.1 %collective-permute-start.11 = (f32[32,16,128]{2,1,0:T(8,128)S(1)}, f32[32,16,128]{2,1,0:T(8,128)S(1)}, u32[]{:S(2)}, u32[]{:S(2)}) collective-permute-start(f32[32,16,128]{2,1,0:T(8,128)S(1)} %get-tuple-element.74.e_ref), channel_id=1, source_target_pairs={{8,1},{1,8},{9,2},{2,9},{10,3},{3,10},{11,4},{4,11},{12,5},{5,12},... | collective-permute-start | bytes 786440 | tf_op jit(solution)/shard_map/ppermute | solution.py:52
  26.0 6.7 %collective-permute-done.5.refs_2_ = f32[32,32,128]{2,1,0:T(8,128)S(1)} collective-permute-done((f32[32,32,128]{2,1,0:T(8,128)S(1)}, f32[32,32,128]{2,1,0:T(8,128)S(1)}, u32[]{:S(2)}, u32[]{:S(2)}) %collective-permute-start.5) | collective-permute-done | bytes 524320 | tf_op jit(solution)/shard_map/ppermute | solution.py:52
  33.7 1.5 %collective-permute-done.11.outer_ref = f32[32,16,128]{2,1,0:T(8,128)S(1)} collective-permute-done((f32[32,16,128]{2,1,0:T(8,128)S(1)}, f32[32,16,128]{2,1,0:T(8,128)S(1)}, u32[]{:S(2)}, u32[]{:S(2)}) %collective-permute-start.11) | collective-permute-done | bytes 262176 | tf_op jit(solution)/shard_map/ppermute | solution.py:52
  35.5 1.3 %collective-permute-start.12 = (f32[32,32,128]{2,1,0:T(8,128)S(1)}, f32[32,32,128]{2,1,0:T(8,128)S(1)}, u32[]{:S(2)}, u32[]{:S(2)}) collective-permute-start(f32[32,32,128]{2,1,0:T(8,128)S(1)} %conv_x.20.refs_0_), channel_id=1, source_target_pairs={{0,16},{16,0},{1,17},{17,1},{2,18},{18,2},{3,19},{19,3},{4,20},{20... | collective-permute-start | bytes 1572872 | tf_op jit(solution)/shard_map/ppermute | solution.py:52
  38.7 1.5 %collective-permute-start.10 = (f32[32,16,128]{2,1,0:T(8,128)S(1)}, f32[32,16,128]{2,1,0:T(8,128)S(1)}, u32[]{:S(2)}, u32[]{:S(2)}) collective-permute-start(f32[32,16,128]{2,1,0:T(8,128)S(1)} %get-tuple-element.73.e_ref), channel_id=1, source_target_pairs={{8,1},{1,8},{9,2},{2,9},{10,3},{3,10},{11,4},{4,11},{12,5},{5,12},... | collective-permute-start | bytes 786440 | tf_op jit(solution)/shard_map/ppermute | solution.py:52
  40.2 8.9 %collective-permute-done.6.outer_ref = f32[32,16,128]{2,1,0:T(8,128)S(1)} collective-permute-done((f32[32,16,128]{2,1,0:T(8,128)S(1)}, f32[32,16,128]{2,1,0:T(8,128)S(1)}, u32[]{:S(2)}, u32[]{:S(2)}) %collective-permute-start.6) | collective-permute-done | bytes 262176 | tf_op jit(solution)/shard_map/ppermute | solution.py:52
  52.3 1.3 collective-permute-start.16
  53.6 6.4 %collective-permute-done.13.refs_2_ = f32[32,32,128]{2,1,0:T(8,128)S(1)} collective-permute-done((f32[32,32,128]{2,1,0:T(8,128)S(1)}, f32[32,32,128]{2,1,0:T(8,128)S(1)}, u32[]{:S(2)}, u32[]{:S(2)}) %collective-permute-start.13) | collective-permute-done | bytes 524320 | tf_op jit(solution)/shard_map/ppermute | solution.py:52
  61.9 2.4 %collective-permute-done.16.outer_ref = f32[32,16,128]{2,1,0:T(8,128)S(1)} collective-permute-done((f32[32,16,128]{2,1,0:T(8,128)S(1)}, f32[32,16,128]{2,1,0:T(8,128)S(1)}, u32[]{:S(2)}, u32[]{:S(2)}) %collective-permute-start.16) | collective-permute-done | bytes 262176 | tf_op jit(solution)/shard_map/ppermute | solution.py:52
  64.7 2.2 %update_y.1 = (f32[2,32,32,128]{3,2,1,0:T(8,128)S(1)}, f32[2,32,32,128]{3,2,1,0:T(8,128)S(1)}, f32[32,16,128]{2,1,0:T(8,128)S(1)}, f32[32,16,128]{2,1,0:T(8,128)...) custom-call(f32[2,32,32,128]{3,2,1,0:T(8,128)S(1)} %get-tuple-element.57.refs_3_.refs_0_, ...), custom_call_target="tpu_custom_call" | custom-call | tf_op jit(solution)/shard_map/update_y/pallas_call | solution.py:287
  66.9 1.3 %collective-permute-start.20 = (f32[32,32,128]{2,1,0:T(8,128)S(1)}, f32[32,32,128]{2,1,0:T(8,128)S(1)}, u32[]{:S(2)}, u32[]{:S(2)}) collective-permute-start(f32[32,32,128]{2,1,0:T(8,128)S(1)} %get-tuple-element.89.refs_0_), channel_id=1, source_target_pairs={{0,16},{16,0},{1,17},{17,1},{2,18},{18,2},{3,19},{19,3},{4,20},{20... | collective-permute-start | bytes 1572872 | tf_op jit(solution)/shard_map/ppermute | solution.py:52
  68.2 1.5 %collective-permute-start.17 = (f32[32,16,128]{2,1,0:T(8,128)S(1)}, f32[32,16,128]{2,1,0:T(8,128)S(1)}, u32[]{:S(2)}, u32[]{:S(2)}) collective-permute-start(f32[32,16,128]{2,1,0:T(8,128)S(1)} %get-tuple-element.86.e_ref), channel_id=1, source_target_pairs={{8,1},{1,8},{9,2},{2,9},{10,3},{3,10},{11,4},{4,11},{12,5},{5,12},... | collective-permute-start | bytes 786440 | tf_op jit(solution)/shard_map/ppermute | solution.py:52
  70.0 10.0 %collective-permute-done.17.outer_ref = f32[32,16,128]{2,1,0:T(8,128)S(1)} collective-permute-done((f32[32,16,128]{2,1,0:T(8,128)S(1)}, f32[32,16,128]{2,1,0:T(8,128)S(1)}, u32[]{:S(2)}, u32[]{:S(2)}) %collective-permute-start.17) | collective-permute-done | bytes 262176 | tf_op jit(solution)/shard_map/ppermute | solution.py:52
  82.8 1.3 collective-permute-start.27
  85.1 7.0 %collective-permute-done.21.refs_2_ = f32[32,32,128]{2,1,0:T(8,128)S(1)} collective-permute-done((f32[32,32,128]{2,1,0:T(8,128)S(1)}, f32[32,32,128]{2,1,0:T(8,128)S(1)}, u32[]{:S(2)}, u32[]{:S(2)}) %collective-permute-start.21) | collective-permute-done | bytes 524320 | tf_op jit(solution)/shard_map/ppermute | solution.py:52
  93.1 1.2 collective-permute-done.27.outer_ref
  94.7 1.3 %collective-permute-start.28 = (f32[32,32,128]{2,1,0:T(8,128)S(1)}, f32[32,32,128]{2,1,0:T(8,128)S(1)}, u32[]{:S(2)}, u32[]{:S(2)}) collective-permute-start(f32[32,32,128]{2,1,0:T(8,128)S(1)} %conv_x.28.refs_0_), channel_id=1, source_target_pairs={{0,16},{16,0},{1,17},{17,1},{2,18},{18,2},{3,19},{19,3},{4,20},{20... | collective-permute-start | bytes 1572872 | tf_op jit(solution)/shard_map/ppermute | solution.py:52
  98.3 1.1 collective-permute-start.26
  99.3 9.2 %collective-permute-done.22.outer_ref = f32[32,16,128]{2,1,0:T(8,128)S(1)} collective-permute-done((f32[32,16,128]{2,1,0:T(8,128)S(1)}, f32[32,16,128]{2,1,0:T(8,128)S(1)}, u32[]{:S(2)}, u32[]{:S(2)}) %collective-permute-start.22) | collective-permute-done | bytes 262176 | tf_op jit(solution)/shard_map/ppermute | solution.py:52
  111.8 1.4 %collective-permute-start.32 = (f32[32,16,128]{2,1,0:T(8,128)S(1)}, f32[32,16,128]{2,1,0:T(8,128)S(1)}, u32[]{:S(2)}, u32[]{:S(2)}) collective-permute-start(f32[32,16,128]{2,1,0:T(8,128)S(1)} %get-tuple-element.104.e_ref), channel_id=1, source_target_pairs={{8,1},{1,8},{9,2},{2,9},{10,3},{3,10},{11,4},{4,11},{12,5},{5,12},... | collective-permute-start | bytes 786440 | tf_op jit(solution)/shard_map/ppermute | solution.py:52
  113.1 6.3 %collective-permute-done.29.refs_2_ = f32[32,32,128]{2,1,0:T(8,128)S(1)} collective-permute-done((f32[32,32,128]{2,1,0:T(8,128)S(1)}, f32[32,32,128]{2,1,0:T(8,128)S(1)}, u32[]{:S(2)}, u32[]{:S(2)}) %collective-permute-start.29) | collective-permute-done | bytes 524320 | tf_op jit(solution)/shard_map/ppermute | solution.py:52
  121.4 2.4 %collective-permute-done.32.outer_ref = f32[32,16,128]{2,1,0:T(8,128)S(1)} collective-permute-done((f32[32,16,128]{2,1,0:T(8,128)S(1)}, f32[32,16,128]{2,1,0:T(8,128)S(1)}, u32[]{:S(2)}, u32[]{:S(2)}) %collective-permute-start.32) | collective-permute-done | bytes 262176 | tf_op jit(solution)/shard_map/ppermute | solution.py:52
  124.2 1.2 last_slab.2
  125.5 1.2 last_slab.3.src_ref
  126.6 1.5 %put_half.2.refs_0_ = f32[32,64,256]{2,1,0:T(8,128)} custom-call(s32[3]{0:T(128)S(1)} %pad_add_fusion.ids_ref, f32[32,32,256]{2,1,0:T(8,128)S(1)} %last_slab.3.src_ref), custom_call_target="tpu_custom_call" | custom-call | tf_op jit(solution)/shard_map/put_half/pallas_call | solution.py:372
  128.2 1.5 %put_half.3 = f32[32,64,256]{2,1,0:T(8,128)} custom-call(s32[3]{0:T(128)S(1)} %pad_add_fusion.ids_ref, f32[32,32,256]{2,1,0:T(8,128)S(1)} %collective-permute-done.33.src_ref, f32[32,64,256]{2,1,0:T(8,128)} %put_half.2.refs_0_), custom_call_target="tpu_custom_call", output_to_operand_aliasing={{}: (2, {})} | custom-call | tf_op jit(solution)/shard_map/put_half/pallas_call | solution.py:372
  (87 shorter events, 28.7 us)
Async XLA Ops:
  7.4 13.2 %collective-permute-start.2 = (f32[64,16,128]{2,1,0:T(8,128)S(1)}, f32[64,16,128]{2,1,0:T(8,128)S(1)}, u32[]{:S(2)}, u32[]{:S(2)}) collective-permute-start(f32[64,16,128]{2,1,0:T(8,128)S(1)} %get-tuple-element.64.i_ref), channel_id=1, source_target_pairs={{0,8},{8,0},{1,9},{9,1},{2,10},{10,2},{3,11},{11,3},{4,12},{12,4},... | collective-permute-start | bytes 1572872 | tf_op jit(solution)/shard_map/ppermute | solution.py:52
  7.5 13.7 %collective-permute-start.4 = (f32[32,32,128]{2,1,0:T(8,128)S(1)}, f32[32,32,128]{2,1,0:T(8,128)S(1)}, u32[]{:S(2)}, u32[]{:S(2)}) collective-permute-start(f32[32,32,128]{2,1,0:T(8,128)S(1)} %get-tuple-element.66.refs_0_), channel_id=1, source_target_pairs={{0,16},{16,0},{1,17},{17,1},{2,18},{18,2},{3,19},{19,3},{4,20},{20... | collective-permute-start | bytes 1572872 | tf_op jit(solution)/shard_map/ppermute | solution.py:52
  8.8 11.8 %collective-permute-start.1 = (f32[32,16,128]{2,1,0:T(8,128)S(1)}, f32[32,16,128]{2,1,0:T(8,128)S(1)}, u32[]{:S(2)}, u32[]{:S(2)}) collective-permute-start(f32[32,16,128]{2,1,0:T(8,128)S(1)} %get-tuple-element.63.e_ref), channel_id=1, source_target_pairs={{8,1},{1,8},{9,2},{2,9},{10,3},{3,10},{11,4},{4,11},{12,5},{5,12},... | collective-permute-start | bytes 786440 | tf_op jit(solution)/shard_map/ppermute | solution.py:52
  11.6 13.9 %collective-permute-start.3 = (f32[32,16,128]{2,1,0:T(8,128)S(1)}, f32[32,16,128]{2,1,0:T(8,128)S(1)}, u32[]{:S(2)}, u32[]{:S(2)}) collective-permute-start(f32[32,16,128]{2,1,0:T(8,128)S(1)} %get-tuple-element.65.e_ref), channel_id=1, source_target_pairs={{8,1},{1,8},{9,2},{2,9},{10,3},{3,10},{11,4},{4,11},{12,5},{5,12},... | collective-permute-start | bytes 786440 | tf_op jit(solution)/shard_map/ppermute | solution.py:52
  21.0 11.7 %collective-permute-start.5 = (f32[32,32,128]{2,1,0:T(8,128)S(1)}, f32[32,32,128]{2,1,0:T(8,128)S(1)}, u32[]{:S(2)}, u32[]{:S(2)}) collective-permute-start(f32[32,32,128]{2,1,0:T(8,128)S(1)} %conv_x.16.refs_0_), channel_id=1, source_target_pairs={{0,16},{16,0},{1,17},{17,1},{2,18},{18,2},{3,19},{19,3},{4,20},{20... | collective-permute-start | bytes 1572872 | tf_op jit(solution)/shard_map/ppermute | solution.py:52
  22.0 13.1 %collective-permute-start.9 = (f32[64,16,128]{2,1,0:T(8,128)S(1)}, f32[64,16,128]{2,1,0:T(8,128)S(1)}, u32[]{:S(2)}, u32[]{:S(2)}) collective-permute-start(f32[64,16,128]{2,1,0:T(8,128)S(1)} %conv_z.19.i_ref), channel_id=1, source_target_pairs={{0,8},{8,0},{1,9},{9,1},{2,10},{10,2},{3,11},{11,3},{4,12},{12,4},... | collective-permute-start | bytes 1572872 | tf_op jit(solution)/shard_map/ppermute | solution.py:52
  23.4 11.7 %collective-permute-start.11 = (f32[32,16,128]{2,1,0:T(8,128)S(1)}, f32[32,16,128]{2,1,0:T(8,128)S(1)}, u32[]{:S(2)}, u32[]{:S(2)}) collective-permute-start(f32[32,16,128]{2,1,0:T(8,128)S(1)} %get-tuple-element.74.e_ref), channel_id=1, source_target_pairs={{8,1},{1,8},{9,2},{2,9},{10,3},{3,10},{11,4},{4,11},{12,5},{5,12},... | collective-permute-start | bytes 786440 | tf_op jit(solution)/shard_map/ppermute | solution.py:52
  25.9 12.4 %collective-permute-start.8 = (f32[32,16,128]{2,1,0:T(8,128)S(1)}, f32[32,16,128]{2,1,0:T(8,128)S(1)}, u32[]{:S(2)}, u32[]{:S(2)}) collective-permute-start(f32[32,16,128]{2,1,0:T(8,128)S(1)} %get-tuple-element.71.e_ref), channel_id=1, source_target_pairs={{8,1},{1,8},{9,2},{2,9},{10,3},{3,10},{11,4},{4,11},{12,5},{5,12},... | collective-permute-start | bytes 786440 | tf_op jit(solution)/shard_map/ppermute | solution.py:52
  33.6 15.5 %collective-permute-start.7 = (f32[64,16,128]{2,1,0:T(8,128)S(1)}, f32[64,16,128]{2,1,0:T(8,128)S(1)}, u32[]{:S(2)}, u32[]{:S(2)}) collective-permute-start(f32[64,16,128]{2,1,0:T(8,128)S(1)} %conv_z.18.i_ref), channel_id=1, source_target_pairs={{0,8},{8,0},{1,9},{9,1},{2,10},{10,2},{3,11},{11,3},{4,12},{12,4},... | collective-permute-start | bytes 1572872 | tf_op jit(solution)/shard_map/ppermute | solution.py:52
  35.5 14.2 %collective-permute-start.12 = (f32[32,32,128]{2,1,0:T(8,128)S(1)}, f32[32,32,128]{2,1,0:T(8,128)S(1)}, u32[]{:S(2)}, u32[]{:S(2)}) collective-permute-start(f32[32,32,128]{2,1,0:T(8,128)S(1)} %conv_x.20.refs_0_), channel_id=1, source_target_pairs={{0,16},{16,0},{1,17},{17,1},{2,18},{18,2},{3,19},{19,3},{4,20},{20... | collective-permute-start | bytes 1572872 | tf_op jit(solution)/shard_map/ppermute | solution.py:52
  37.8 11.3 %collective-permute-start.6 = (f32[32,16,128]{2,1,0:T(8,128)S(1)}, f32[32,16,128]{2,1,0:T(8,128)S(1)}, u32[]{:S(2)}, u32[]{:S(2)}) collective-permute-start(f32[32,16,128]{2,1,0:T(8,128)S(1)} %get-tuple-element.70.e_ref), channel_id=1, source_target_pairs={{8,1},{1,8},{9,2},{2,9},{10,3},{3,10},{11,4},{4,11},{12,5},{5,12},... | collective-permute-start | bytes 786440 | tf_op jit(solution)/shard_map/ppermute | solution.py:52
  38.7 13.2 %collective-permute-start.10 = (f32[32,16,128]{2,1,0:T(8,128)S(1)}, f32[32,16,128]{2,1,0:T(8,128)S(1)}, u32[]{:S(2)}, u32[]{:S(2)}) collective-permute-start(f32[32,16,128]{2,1,0:T(8,128)S(1)} %get-tuple-element.73.e_ref), channel_id=1, source_target_pairs={{8,1},{1,8},{9,2},{2,9},{10,3},{3,10},{11,4},{4,11},{12,5},{5,12},... | collective-permute-start | bytes 786440 | tf_op jit(solution)/shard_map/ppermute | solution.py:52
  49.5 10.5 %collective-permute-start.13 = (f32[32,32,128]{2,1,0:T(8,128)S(1)}, f32[32,32,128]{2,1,0:T(8,128)S(1)}, u32[]{:S(2)}, u32[]{:S(2)}) collective-permute-start(f32[32,32,128]{2,1,0:T(8,128)S(1)} %conv_x.18.refs_0_), channel_id=1, source_target_pairs={{0,16},{16,0},{1,17},{17,1},{2,18},{18,2},{3,19},{19,3},{4,20},{20... | collective-permute-start | bytes 1572872 | tf_op jit(solution)/shard_map/ppermute | solution.py:52
  50.5 10.9 %collective-permute-start.14 = (f32[32,16,128]{2,1,0:T(8,128)S(1)}, f32[32,16,128]{2,1,0:T(8,128)S(1)}, u32[]{:S(2)}, u32[]{:S(2)}) collective-permute-start(f32[32,16,128]{2,1,0:T(8,128)S(1)} %get-tuple-element.80.e_ref), channel_id=1, source_target_pairs={{8,1},{1,8},{9,2},{2,9},{10,3},{3,10},{11,4},{4,11},{12,5},{5,12},... | collective-permute-start | bytes 786440 | tf_op jit(solution)/shard_map/ppermute | solution.py:52
  51.6 9.9 %collective-permute-start.15 = (f32[64,16,128]{2,1,0:T(8,128)S(1)}, f32[64,16,128]{2,1,0:T(8,128)S(1)}, u32[]{:S(2)}, u32[]{:S(2)}) collective-permute-start(f32[64,16,128]{2,1,0:T(8,128)S(1)} %conv_z.23.i_ref), channel_id=1, source_target_pairs={{0,8},{8,0},{1,9},{9,1},{2,10},{10,2},{3,11},{11,3},{4,12},{12,4},... | collective-permute-start | bytes 1572872 | tf_op jit(solution)/shard_map/ppermute | solution.py:52
  52.3 11.9 %collective-permute-start.16 = (f32[32,16,128]{2,1,0:T(8,128)S(1)}, f32[32,16,128]{2,1,0:T(8,128)S(1)}, u32[]{:S(2)}, u32[]{:S(2)}) collective-permute-start(f32[32,16,128]{2,1,0:T(8,128)S(1)} %get-tuple-element.81.e_ref), channel_id=1, source_target_pairs={{8,1},{1,8},{9,2},{2,9},{10,3},{3,10},{11,4},{4,11},{12,5},{5,12},... | collective-permute-start | bytes 786440 | tf_op jit(solution)/shard_map/ppermute | solution.py:52
  66.8 13.1 %collective-permute-start.18 = (f32[64,16,128]{2,1,0:T(8,128)S(1)}, f32[64,16,128]{2,1,0:T(8,128)S(1)}, u32[]{:S(2)}, u32[]{:S(2)}) collective-permute-start(f32[64,16,128]{2,1,0:T(8,128)S(1)} %get-tuple-element.87.i_ref), channel_id=1, source_target_pairs={{0,8},{8,0},{1,9},{9,1},{2,10},{10,2},{3,11},{11,3},{4,12},{12,4},... | collective-permute-start | bytes 1572872 | tf_op jit(solution)/shard_map/ppermute | solution.py:52
  66.9 13.9 %collective-permute-start.20 = (f32[32,32,128]{2,1,0:T(8,128)S(1)}, f32[32,32,128]{2,1,0:T(8,128)S(1)}, u32[]{:S(2)}, u32[]{:S(2)}) collective-permute-start(f32[32,32,128]{2,1,0:T(8,128)S(1)} %get-tuple-element.89.refs_0_), channel_id=1, source_target_pairs={{0,16},{16,0},{1,17},{17,1},{2,18},{18,2},{3,19},{19,3},{4,20},{20... | collective-permute-start | bytes 1572872 | tf_op jit(solution)/shard_map/ppermute | solution.py:52
  68.2 11.7 %collective-permute-start.17 = (f32[32,16,128]{2,1,0:T(8,128)S(1)}, f32[32,16,128]{2,1,0:T(8,128)S(1)}, u32[]{:S(2)}, u32[]{:S(2)}) collective-permute-start(f32[32,16,128]{2,1,0:T(8,128)S(1)} %get-tuple-element.86.e_ref), channel_id=1, source_target_pairs={{8,1},{1,8},{9,2},{2,9},{10,3},{3,10},{11,4},{4,11},{12,5},{5,12},... | collective-permute-start | bytes 786440 | tf_op jit(solution)/shard_map/ppermute | solution.py:52
  69.8 14.4 %collective-permute-start.19 = (f32[32,16,128]{2,1,0:T(8,128)S(1)}, f32[32,16,128]{2,1,0:T(8,128)S(1)}, u32[]{:S(2)}, u32[]{:S(2)}) collective-permute-start(f32[32,16,128]{2,1,0:T(8,128)S(1)} %get-tuple-element.88.e_ref), channel_id=1, source_target_pairs={{8,1},{1,8},{9,2},{2,9},{10,3},{3,10},{11,4},{4,11},{12,5},{5,12},... | collective-permute-start | bytes 786440 | tf_op jit(solution)/shard_map/ppermute | solution.py:52
  80.5 11.6 %collective-permute-start.21 = (f32[32,32,128]{2,1,0:T(8,128)S(1)}, f32[32,32,128]{2,1,0:T(8,128)S(1)}, u32[]{:S(2)}, u32[]{:S(2)}) collective-permute-start(f32[32,32,128]{2,1,0:T(8,128)S(1)} %conv_x.24.refs_0_), channel_id=1, source_target_pairs={{0,16},{16,0},{1,17},{17,1},{2,18},{18,2},{3,19},{19,3},{4,20},{20... | collective-permute-start | bytes 1572872 | tf_op jit(solution)/shard_map/ppermute | solution.py:52
  81.5 12.8 %collective-permute-start.25 = (f32[64,16,128]{2,1,0:T(8,128)S(1)}, f32[64,16,128]{2,1,0:T(8,128)S(1)}, u32[]{:S(2)}, u32[]{:S(2)}) collective-permute-start(f32[64,16,128]{2,1,0:T(8,128)S(1)} %conv_z.27.i_ref), channel_id=1, source_target_pairs={{0,8},{8,0},{1,9},{9,1},{2,10},{10,2},{3,11},{11,3},{4,12},{12,4},... | collective-permute-start | bytes 1572872 | tf_op jit(solution)/shard_map/ppermute | solution.py:52
  82.8 11.5 %collective-permute-start.27 = (f32[32,16,128]{2,1,0:T(8,128)S(1)}, f32[32,16,128]{2,1,0:T(8,128)S(1)}, u32[]{:S(2)}, u32[]{:S(2)}) collective-permute-start(f32[32,16,128]{2,1,0:T(8,128)S(1)} %get-tuple-element.97.e_ref), channel_id=1, source_target_pairs={{8,1},{1,8},{9,2},{2,9},{10,3},{3,10},{11,4},{4,11},{12,5},{5,12},... | collective-permute-start | bytes 786440 | tf_op jit(solution)/shard_map/ppermute | solution.py:52
  84.5 13.3 %collective-permute-start.24 = (f32[32,16,128]{2,1,0:T(8,128)S(1)}, f32[32,16,128]{2,1,0:T(8,128)S(1)}, u32[]{:S(2)}, u32[]{:S(2)}) collective-permute-start(f32[32,16,128]{2,1,0:T(8,128)S(1)} %get-tuple-element.94.e_ref), channel_id=1, source_target_pairs={{8,1},{1,8},{9,2},{2,9},{10,3},{3,10},{11,4},{4,11},{12,5},{5,12},... | collective-permute-start | bytes 786440 | tf_op jit(solution)/shard_map/ppermute | solution.py:52
  93.0 15.5 %collective-permute-start.23 = (f32[64,16,128]{2,1,0:T(8,128)S(1)}, f32[64,16,128]{2,1,0:T(8,128)S(1)}, u32[]{:S(2)}, u32[]{:S(2)}) collective-permute-start(f32[64,16,128]{2,1,0:T(8,128)S(1)} %conv_z.26.i_ref), channel_id=1, source_target_pairs={{0,8},{8,0},{1,9},{9,1},{2,10},{10,2},{3,11},{11,3},{4,12},{12,4},... | collective-permute-start | bytes 1572872 | tf_op jit(solution)/shard_map/ppermute | solution.py:52
  94.7 14.5 %collective-permute-start.28 = (f32[32,32,128]{2,1,0:T(8,128)S(1)}, f32[32,32,128]{2,1,0:T(8,128)S(1)}, u32[]{:S(2)}, u32[]{:S(2)}) collective-permute-start(f32[32,32,128]{2,1,0:T(8,128)S(1)} %conv_x.28.refs_0_), channel_id=1, source_target_pairs={{0,16},{16,0},{1,17},{17,1},{2,18},{18,2},{3,19},{19,3},{4,20},{20... | collective-permute-start | bytes 1572872 | tf_op jit(solution)/shard_map/ppermute | solution.py:52
  97.0 11.5 %collective-permute-start.22 = (f32[32,16,128]{2,1,0:T(8,128)S(1)}, f32[32,16,128]{2,1,0:T(8,128)S(1)}, u32[]{:S(2)}, u32[]{:S(2)}) collective-permute-start(f32[32,16,128]{2,1,0:T(8,128)S(1)} %get-tuple-element.93.e_ref), channel_id=1, source_target_pairs={{8,1},{1,8},{9,2},{2,9},{10,3},{3,10},{11,4},{4,11},{12,5},{5,12},... | collective-permute-start | bytes 786440 | tf_op jit(solution)/shard_map/ppermute | solution.py:52
  98.3 13.1 %collective-permute-start.26 = (f32[32,16,128]{2,1,0:T(8,128)S(1)}, f32[32,16,128]{2,1,0:T(8,128)S(1)}, u32[]{:S(2)}, u32[]{:S(2)}) collective-permute-start(f32[32,16,128]{2,1,0:T(8,128)S(1)} %get-tuple-element.96.e_ref), channel_id=1, source_target_pairs={{8,1},{1,8},{9,2},{2,9},{10,3},{3,10},{11,4},{4,11},{12,5},{5,12},... | collective-permute-start | bytes 786440 | tf_op jit(solution)/shard_map/ppermute | solution.py:52
  108.9 10.5 %collective-permute-start.29 = (f32[32,32,128]{2,1,0:T(8,128)S(1)}, f32[32,32,128]{2,1,0:T(8,128)S(1)}, u32[]{:S(2)}, u32[]{:S(2)}) collective-permute-start(f32[32,32,128]{2,1,0:T(8,128)S(1)} %conv_x.26.refs_0_), channel_id=1, source_target_pairs={{0,16},{16,0},{1,17},{17,1},{2,18},{18,2},{3,19},{19,3},{4,20},{20... | collective-permute-start | bytes 1572872 | tf_op jit(solution)/shard_map/ppermute | solution.py:52
  109.9 11.1 %collective-permute-start.30 = (f32[32,16,128]{2,1,0:T(8,128)S(1)}, f32[32,16,128]{2,1,0:T(8,128)S(1)}, u32[]{:S(2)}, u32[]{:S(2)}) collective-permute-start(f32[32,16,128]{2,1,0:T(8,128)S(1)} %get-tuple-element.103.e_ref), channel_id=1, source_target_pairs={{8,1},{1,8},{9,2},{2,9},{10,3},{3,10},{11,4},{4,11},{12,5},{5,12},... | collective-permute-start | bytes 786440 | tf_op jit(solution)/shard_map/ppermute | solution.py:52
  110.9 10.1 %collective-permute-start.31 = (f32[64,16,128]{2,1,0:T(8,128)S(1)}, f32[64,16,128]{2,1,0:T(8,128)S(1)}, u32[]{:S(2)}, u32[]{:S(2)}) collective-permute-start(f32[64,16,128]{2,1,0:T(8,128)S(1)} %conv_z.31.i_ref), channel_id=1, source_target_pairs={{0,8},{8,0},{1,9},{9,1},{2,10},{10,2},{3,11},{11,3},{4,12},{12,4},... | collective-permute-start | bytes 1572872 | tf_op jit(solution)/shard_map/ppermute | solution.py:52
  111.8 12.1 %collective-permute-start.32 = (f32[32,16,128]{2,1,0:T(8,128)S(1)}, f32[32,16,128]{2,1,0:T(8,128)S(1)}, u32[]{:S(2)}, u32[]{:S(2)}) collective-permute-start(f32[32,16,128]{2,1,0:T(8,128)S(1)} %get-tuple-element.104.e_ref), channel_id=1, source_target_pairs={{8,1},{1,8},{9,2},{2,9},{10,3},{3,10},{11,4},{4,11},{12,5},{5,12},... | collective-permute-start | bytes 786440 | tf_op jit(solution)/shard_map/ppermute | solution.py:52
  (6 other events, 25.7 us)

commit v5 on v4

--- a/solution.py
+++ b/solution.py
@@ -6,7 +6,7 @@
 from jax.sharding import PartitionSpec as P
 
 ITERS = 2
-COST_X, COST_Z = 45, 30
+COST_X, COST_Z, COST_Y = 45, 30, 0
 AXES = ("zg", "gx")
 F32 = jnp.float32
 BF16 = jnp.bfloat16
@@ -23,6 +23,15 @@
 
 def shape(*dims, dtype=F32):
     return jax.ShapeDtypeStruct(dims, dtype)
+
+
+def call(body, args, in_specs, after=None, **options):
+    if after is not None:
+        n = len(args)
+        inner = body
+        body = lambda *refs: inner(*refs[:n], *refs[n + 1 :])
+        args, in_specs = [*args, after], [*in_specs, pl.BlockSpec(memory_space=pl.ANY)]
+    return pl.pallas_call(body, in_specs=in_specs, **options)(*args)
 
 
 VMEM = pl.BlockSpec(memory_space=pltpu.VMEM)
@@ -80,20 +89,22 @@
     return place
 
 
-def matrices_y(kernel_y, size_y, rows_per=64):
+def matrices_y(kernel_y, size_y):
     taps = kernel_y.shape[0]
+    half = (taps - 1) // 2
 
     def body(ref, fh_ref, fl_ref, ah_ref, al_ref):
-        dims = (rows_per, size_y)
-
-        @pl.loop(0, size_y // rows_per)
-        def _(k):
-            at = pl.multiple_of(k * rows_per, rows_per)
-            rows = pl.ds(at, rows_per)
-            diff = at + lax.broadcasted_iota(jnp.int32, dims, 0) - lax.broadcasted_iota(jnp.int32, dims, 1) + (taps - 1) // 2
-            fwd, adj = band(ref, taps, diff)
-            fh_ref[rows, :], fl_ref[rows, :] = split(fwd)
-            ah_ref[rows, :], al_ref[rows, :] = split(adj)
+        lane = lax.broadcasted_iota(jnp.int32, (1, size_y), 1)
+        row, reverse, total = jnp.zeros((1, size_y), F32), jnp.zeros((1, size_y), F32), jnp.float32(0.0)
+        for t in range(taps):
+            tap = ref[t]
+            row, reverse, total = jnp.where(lane == t, tap, row), jnp.where(lane == taps - 1 - t, tap, reverse), total + tap
+        dims = (size_y, size_y)
+        offset = lax.broadcasted_iota(jnp.int32, dims, 1) - lax.broadcasted_iota(jnp.int32, dims, 0)
+        inside = jnp.abs(offset) <= half
+        for v, hi_ref, lo_ref in ((reverse, fh_ref, fl_ref), (row, ah_ref, al_ref)):
+            mat = pltpu.roll(jnp.broadcast_to(v / total, dims), size_y - half, 1, stride=1, stride_axis=0)
+            hi_ref[...], lo_ref[...] = split(jnp.where(inside, mat, 0.0))
 
     out = pl.pallas_call(
         body,
@@ -141,7 +152,7 @@
     return (fx, fz), (ax, az)
 
 
-def conv_x(mat, s, outer, e, i, inner, over, later=None):
+def conv_x(mat, s, outer, e, i, inner, over, later=None, after=None):
     slab, group, lanes = e.shape
     n_out = 1 if later is None else 2
 
@@ -150,7 +161,7 @@
         if later is not None:
             rest[-1][...] = rest[-n_out - 1][...]
         m = m_ref[...]
-        at = s * slab
+        at = s * slab if i.shape[0] > slab else 0
         for z in range(0, slab, 2):
             cols = [
                 jnp.concatenate([outer_ref[k], e_ref[k], i_ref[at + k], inner_ref[at + k]], axis=0) for k in (z, z + 1)
@@ -160,19 +171,21 @@
             for n in (0, 1):
                 v = res[:, n * lanes : (n + 1) * lanes]
                 if over is not None:
-                    v = rest[0][s, z + n] / v
+                    v = rest[0][z + n] / v
                 out_ref[z + n] = v
 
     args = [mat, outer, e, i, inner] + ([] if over is None else [over]) + ([] if later is None else [later])
-    return pl.pallas_call(
-        body,
-        in_specs=[VMEM] * len(args),
+    return call(
+        body,
+        args,
+        [VMEM] * len(args),
+        after,
         out_specs=[VMEM] * n_out,
         out_shape=[shape(slab, 2 * group, lanes)] + ([] if later is None else [shape(*later.shape)]),
         cost_estimate=cost(COST_X, 2 * slab * lanes * mat.size, 4 * 6 * slab * group * lanes),
         compiler_params=params(),
         name="conv_x",
-    )(*args)
+    )
 
 
 def conv_z(mat, g, pieces, over):
@@ -196,11 +209,12 @@
             for j in (0, 1):
                 v = res[:, j * lanes : (j + 1) * lanes]
                 if over is not None:
-                    v = refs[n].reshape(m_z * width, lanes)[pl.ds(g * group + x + j, m_z, stride=width), :] / v
+                    at = pl.ds(g * group + x + j, slab, stride=width)
+                    v = jnp.concatenate([r.reshape(slab * width, lanes)[at, :] for r in refs[n : n + 2]], axis=0) / v
                 for r, part in zip(out, jnp.split(v, len(out), axis=0)):
                     r[pl.ds(x + j, part.shape[0], stride=group), :] = part
 
-    args = [mat, *pieces] + ([] if over is None else [over])
+    args = [mat, *pieces] + list(over or ())
     return pl.pallas_call(
         body,
         in_specs=[VMEM] * len(args),
@@ -219,102 +233,106 @@
 
 
 def take(refs, s, z, block):
-    slab = refs[0].shape[0]
-    left = jnp.concatenate([refs[s][z : z + block], refs[2][s * slab + z : s * slab + z + block]], axis=1)
-    return jnp.concatenate([left, refs[3 + s][z : z + block]], axis=2)
-
-
-def put(refs, s, z, v):
-    slab, group, lanes = refs[0].shape
-    block = v.shape[0]
-    refs[s][z : z + block] = v[:, :group, :lanes]
-    refs[2][s * slab + z : s * slab + z + block] = v[:, group:, :lanes]
-    refs[3 + s][z : z + block] = v[:, :, lanes:]
-
-
-def rows(pair, s, z, block):
-    return jnp.concatenate([r[s, z : z + block] for r in pair], axis=2)
-
-
-def put_rows(pair, s, z, v):
+    e_ref, i_ref, slab_ref = refs
+    at = s * e_ref.shape[0] + z
+    left = jnp.concatenate([e_ref[z : z + block], i_ref[at : at + block]], axis=1)
+    return jnp.concatenate([left, slab_ref[z : z + block]], axis=2)
+
+
+def put(refs, z, v):
+    e_ref, i_ref, slab_ref = refs
+    block, group, lanes = v.shape[0], e_ref.shape[1], e_ref.shape[2]
+    e_ref[z : z + block] = v[:, :group, :lanes]
+    i_ref[z : z + block] = v[:, group:, :lanes]
+    slab_ref[z : z + block] = v[:, :, lanes:]
+
+
+def rows(pair, z, block):
+    return jnp.concatenate([r[z : z + block] for r in pair], axis=2)
+
+
+def put_rows(pair, z, v):
     for r, part in zip(pair, jnp.split(v, 2, axis=2)):
-        r[s, z : z + v.shape[0]] = part
-
-
-def piece_shapes(slab, group, size_y):
+        r[z : z + v.shape[0]] = part
+
+
+def slab_shapes(slab, width, size_y):
     half = size_y // 2
-    return [shape(slab, group, half)] * 2 + [shape(2 * slab, group, half)] + [shape(slab, 2 * group, half)] * 2
+    return [shape(slab, width, half)] * 2 + [shape(slab, width // 2, half)] * 2 + [shape(slab, width, half)]
 
 
 def own_is_a(ids_ref):
     return ids_ref[0] != ids_ref[1]
 
 
-def first_y(ids, own, received, mat, block=16):
+def first_y(ids, s, own, received, mat, block=16):
     slab, width, size_y = own.shape
 
     def body(ids_ref, own_ref, got_ref, h_ref, l_ref, *refs):
         obs, outs = refs[:2], refs[2:]
-        for s in (0, 1):
-            mine = own_is_a(ids_ref) == (s == 0)
-            for z in range(0, slab, block):
-                v = jnp.where(mine, own_ref[z : z + block], got_ref[z : z + block])
-                put_rows(obs, s, z, v)
-                put(outs, s, z, mul_y(v, h_ref, l_ref))
+        mine = own_is_a(ids_ref) == (s == 0)
+        for z in range(0, slab, block):
+            v = jnp.where(mine, own_ref[z : z + block], got_ref[z : z + block])
+            put_rows(obs, z, v)
+            put(outs, z, mul_y(v, h_ref, l_ref))
 
     out = pl.pallas_call(
         body,
         in_specs=[SMEM] + [VMEM] * 4,
-        out_specs=[VMEM] * 7,
-        out_shape=[shape(2, slab, width, size_y // 2)] * 2 + piece_shapes(slab, width // 2, size_y),
+        out_specs=[VMEM] * 5,
+        out_shape=slab_shapes(slab, width, size_y),
+        cost_estimate=cost(COST_Y, 6 * slab * width * size_y * size_y, 4 * 4 * slab * width * size_y),
         compiler_params=params(),
         name="first_y",
     )(ids, own, received, *mat)
     return out[:2], out[2:]
 
 
-def update_y(estimate, parts, adj, fwd, block=16):
-    _, slab, width, half = estimate[0].shape
+def update_y(s, estimate, parts, adj, fwd, after=None, block=16):
+    slab, width, half = estimate[0].shape
 
     def body(*refs):
-        est, ins, (ah_ref, al_ref, fh_ref, fl_ref), new_est, outs = refs[:2], refs[2:7], refs[7:11], refs[11:13], refs[13:]
-        for s in (0, 1):
-            for z in range(0, slab, block):
-                new = rows(est, s, z, block) * mul_y(take(ins, s, z, block), ah_ref, al_ref)
-                put_rows(new_est, s, z, new)
-                put(outs, s, z, mul_y(new, fh_ref, fl_ref))
-
-    out = pl.pallas_call(
-        body,
-        in_specs=[VMEM] * 11,
-        out_specs=[VMEM] * 7,
-        out_shape=[shape(2, slab, width, half)] * 2 + piece_shapes(slab, width // 2, 2 * half),
+        est, ins, (ah_ref, al_ref, fh_ref, fl_ref), new_est, outs = refs[:2], refs[2:5], refs[5:9], refs[9:11], refs[11:]
+        for z in range(0, slab, block):
+            new = rows(est, z, block) * mul_y(take(ins, s, z, block), ah_ref, al_ref)
+            put_rows(new_est, z, new)
+            put(outs, z, mul_y(new, fh_ref, fl_ref))
+
+    out = call(
+        body,
+        [*estimate, *parts, *adj, *fwd],
+        [VMEM] * 9,
+        after,
+        out_specs=[VMEM] * 5,
+        out_shape=slab_shapes(slab, width, 2 * half),
+        cost_estimate=cost(COST_Y, 24 * slab * width * half * half, 4 * 8 * slab * width * half),
         compiler_params=params(),
         name="update_y",
-    )(*estimate, *parts, *adj, *fwd)
+    )
     return out[:2], out[2:]
 
 
 def last_slab(ids, estimate, parts, adj, mine, block=16):
-    _, slab, width, half = estimate[0].shape
+    slab, width, half = estimate[0][0].shape
 
     def body(ids_ref, *refs):
-        est, ins, (ah_ref, al_ref, out_ref) = refs[:2], refs[2:7], refs[7:]
+        est, (e0, e1, i, a, b), (ah_ref, al_ref, out_ref) = (refs[:2], refs[2:4]), refs[4:9], refs[9:]
+        ins = ((e0, i, a), (e1, i, b))
         for s in (0, 1):
 
             @pl.when(own_is_a(ids_ref) == ((s == 0) == mine))
             def _(s=s):
                 for z in range(0, slab, block):
-                    out_ref[z : z + block] = rows(est, s, z, block) * mul_y(take(ins, s, z, block), ah_ref, al_ref)
+                    out_ref[z : z + block] = rows(est[s], z, block) * mul_y(take(ins[s], s, z, block), ah_ref, al_ref)
 
     return pl.pallas_call(
         body,
-        in_specs=[SMEM] + [VMEM] * 9,
+        in_specs=[SMEM] + [VMEM] * 11,
         out_specs=VMEM,
         out_shape=shape(slab, width, 2 * half),
         compiler_params=params(),
         name="last_slab",
-    )(ids, *estimate, *parts, *adj)
+    )(ids, *estimate[0], *estimate[1], *parts, *adj)
 
 
 def outward(core, g, group):
@@ -389,12 +407,15 @@
     def mat(self, dim):
         return self.mats[self.op // 2][dim]
 
-    def numerator(self):
-        return self.over if self.op == 1 else None
+    def numerator(self, s=slice(None)):
+        return self.over[s] if self.op == 1 else None
 
     def send_x(self, *which):
         for n in which:
-            self.halos[n] = send(self.parts[n], self.links.inner if n == 2 else self.links.x)
+            if n == 3 and self.parts[3] is self.parts[2]:
+                self.halos[3] = self.halos[2]
+            else:
+                self.halos[n] = send(self.parts[n], self.links.inner if n >= 2 else self.links.x)
 
     def send_z(self, s, slab):
         pairs = (self.links.z_even, self.links.z_odd)[s]
@@ -402,17 +423,20 @@
             self.halos.append(send(slab, pairs))
 
     def x(self, s, later=None):
-        (e, i), (outer, inner) = ((v[s], v[2]) for v in (self.parts, self.halos))
-        out, *late = conv_x(self.mat(0), s, outer, e, i, inner, self.numerator(), later)
+        after = self.out[0] if s == 1 else None
+        (e, i), (outer, inner) = ((v[s], v[2 + s]) for v in (self.parts, self.halos))
+        out, *late = conv_x(self.mat(0), s, outer, e, i, inner, self.numerator(s), later, after)
         self.out.append(out)
         if s == 1:
             self.turn([])
-            self.send_z(0, self.parts[0])
-            self.send_z(1, self.parts[1])
+            if self.op < 4:
+                self.send_z(0, self.parts[0])
+                self.send_z(1, self.parts[1])
         return late[0] if late else None
 
     def z(self, g):
-        self.out += conv_z(self.mat(1), g, [*self.parts, *self.halos], self.numerator())
+        out = conv_z(self.mat(1), g, [*self.parts, *self.halos], self.numerator())
+        self.out += out if g == 0 else [out[0], out[0]]
 
     def turn(self, halos):
         self.parts, self.out, self.halos = self.out, [], halos
@@ -420,12 +444,13 @@
 
 
 def iteration(links, mats, obs, parts):
-    left, right = Chunk(links, mats, obs[0], parts[:3]), Chunk(links, mats, obs[1], parts[3:])
-    left.halos, right.halos = [None] * 3, []
+    (e0, i0, a), (e1, i1, b) = parts
+    left, right = (Chunk(links, mats, [v[side] for v in obs], p) for side, p in enumerate(([e0, e1, i0, i1], [a, b])))
+    left.halos, right.halos = [None] * 4, []
     left.send_x(2, 0)
-    right.send_z(0, parts[3])
-    right.send_z(1, parts[4])
-    left.send_x(1)
+    right.send_z(0, a)
+    right.send_z(1, b)
+    left.send_x(3, 1)
     left.x(0)
     for half in range(4):
         c, other = (right, left) if half % 2 == 0 else (left, right)
@@ -436,11 +461,11 @@
             other.x(1)
             break
         late = other.x(1, c.out[1])
-        c.turn([None] * 3)
+        c.turn([None] * 4)
         c.parts[1] = late
-        c.send_x(0, 2, 1)
+        c.send_x(0, 2, 3, 1)
         c.x(0)
-    return [*left.parts, *right.parts]
+    return [*left.parts[:3], *right.parts]
 
 
 def shards(observed, kernel_x, kernel_y, kernel_z):
@@ -461,12 +486,16 @@
     fwd_y, adj_y = matrices_y(kernel_y, size_y)
     fwd, adj = matrices_xz(ids, kernel_x, kernel_z, slab, group, n_pieces)
 
-    obs, parts = first_y(ids, own, received, fwd_y)
+    obs, parts = zip(*(first_y(ids, s, own, received, fwd_y) for s in (0, 1)))
     estimate = obs
     for step in range(ITERS):
-        parts = iteration(links, (fwd, adj), obs, parts)
+        e0, e1, i, a, b = iteration(links, (fwd, adj), obs, parts)
         if step < ITERS - 1:
-            estimate, parts = update_y(estimate, parts, adj_y, fwd_y)
+            slabs = ((e0, i, a), (e1, i, b))
+            first = update_y(0, estimate[0], slabs[0], adj_y, fwd_y)
+            second = update_y(1, estimate[1], slabs[1], adj_y, fwd_y, first[0][0])
+            estimate, parts = zip(first, second)
+    parts = [e0, e1, i, a, b]
     received = send(last_slab(ids, estimate, parts, adj_y, False), links.inner)
     whole = put_half(ids, last_slab(ids, estimate, parts, adj_y, True), True)
     return put_half(ids, received, False, whole)

time: 132 us -> 126 us (0.955)
  waiting for transfers between devices: 71.7 us -> 63.8 us
  starting transfers between devices: 23.5 us -> 26.7 us
    ppermute x34 -> x36, waiting for transfers between devices: 71.7 us -> 63.8 us  [send(): return lax.ppermute(v, AXES, pairs)]
    ppermute x34 -> x36, starting transfers between devices: 23.5 us -> 26.7 us  [send(): return lax.ppermute(v, AXES, pairs)]
    pallas_call x20 -> x22, Pallas kernels: 12.9 us -> 14.1 us  [the longest x18 9.53 us: call(): return pl.pallas_call(body, in_specs=in_specs, **options)(*args)]
  transfers between devices with their start and end apart: 34 -> 36, of which waited for: 15 -> 16; matrix products, arithmetic and copies ran while one was open for 0% -> 0% of each run, Pallas kernels for 19% -> 22%
where the time goes in v5:
time: 126 us; the launch traced here: 125 us
  waiting for transfers between devices  63.8 us (51%)
  Pallas kernels  32.4 us (26%)
  starting transfers between devices  26.7 us (21%)
  local copies, waits for them, and re-layouts  1.61 us (1%)
    ppermute x36, waiting for transfers between devices, send(): return lax.ppermute(v, AXES, pairs)  63.8 us
    ppermute x36, starting transfers between devices, send(): return lax.ppermute(v, AXES, pairs)  26.7 us
    pallas_call x16, Pallas kernels, conv_z(): pl.pallas_call(body, in_specs=[VMEM] * len(args), out_specs=[VMEM] * len(...  12.3 us
    pallas_call x18, Pallas kernels, call(): return pl.pallas_call(body, in_specs=in_specs, **options)(*args)  9.53 us
    pallas_call x2, Pallas kernels, put_half(): pl.pallas_call(body, in_specs=[SMEM, VMEM] + ([] if whole is None else [H...  3.06 us
  transfers between devices with their start and end apart: 36, of which 16 were waited for; matrix products, arithmetic and copies ran while one was open for 0% of the time, Pallas kernels for 22%

profile of v5, /device:TPU:25, one launch (start us, length us, event | category | flops | bytes accessed | tf_op | source)
XLA Modules:
  0.0 125.2 jit_solution(15703696602342726061)
XLA Ops:
  0.1 1.6 %copy-done = f32[32,64,256]{2,1,0:T(8,128)S(1)} copy-done((f32[32,64,256]{2,1,0:T(8,128)S(1)}, f32[32,64,256]{2,1,0:T(8,128)}, u32[]{:S(2)}) %copy-start) | copy-done | bytes 2097176
  6.5 1.3 %collective-permute-start.5 = (f32[32,32,128]{2,1,0:T(8,128)S(1)}, f32[32,32,128]{2,1,0:T(8,128)S(1)}, u32[]{:S(2)}, u32[]{:S(2)}) collective-permute-start(f32[32,32,128]{2,1,0:T(8,128)S(1)} %get-tuple-element.73.refs_0_), channel_id=1, source_target_pairs={{0,16},{16,0},{1,17},{17,1},{2,18},{18,2},{3,19},{19,3},{4,20},{20... | collective-permute-start | bytes 1572872 | tf_op jit(solution)/shard_map/ppermute | solution.py:61
  7.8 1.8 %collective-permute-start.1 = (f32[32,16,128]{2,1,0:T(8,128)S(1)}, f32[32,16,128]{2,1,0:T(8,128)S(1)}, u32[]{:S(2)}, u32[]{:S(2)}) collective-permute-start(f32[32,16,128]{2,1,0:T(8,128)S(1)} %get-tuple-element.69.e_ref), channel_id=1, source_target_pairs={{8,1},{1,8},{9,2},{2,9},{10,3},{3,10},{11,4},{4,11},{12,5},{5,12},... | collective-permute-start | bytes 786440 | tf_op jit(solution)/shard_map/ppermute | solution.py:61
  12.0 1.2 collective-permute-start.4
  13.3 6.3 %collective-permute-done.1.outer_ref = f32[32,16,128]{2,1,0:T(8,128)S(1)} collective-permute-done((f32[32,16,128]{2,1,0:T(8,128)S(1)}, f32[32,16,128]{2,1,0:T(8,128)S(1)}, u32[]{:S(2)}, u32[]{:S(2)}) %collective-permute-start.1) | collective-permute-done | bytes 262176 | tf_op jit(solution)/shard_map/ppermute | solution.py:61
  22.4 2.0 %collective-permute-start.11 = (f32[32,16,128]{2,1,0:T(8,128)S(1)}, f32[32,16,128]{2,1,0:T(8,128)S(1)}, u32[]{:S(2)}, u32[]{:S(2)}) collective-permute-start(f32[32,16,128]{2,1,0:T(8,128)S(1)} %get-tuple-element.82.e_ref), channel_id=1, source_target_pairs={{8,1},{1,8},{9,2},{2,9},{10,3},{3,10},{11,4},{4,11},{12,5},{5,12},... | collective-permute-start | bytes 786440 | tf_op jit(solution)/shard_map/ppermute | solution.py:61
  24.9 6.8 %collective-permute-done.6.refs_2_ = f32[32,32,128]{2,1,0:T(8,128)S(1)} collective-permute-done((f32[32,32,128]{2,1,0:T(8,128)S(1)}, f32[32,32,128]{2,1,0:T(8,128)S(1)}, u32[]{:S(2)}, u32[]{:S(2)}) %collective-permute-start.6) | collective-permute-done | bytes 524320 | tf_op jit(solution)/shard_map/ppermute | solution.py:61
  32.7 1.4 %collective-permute-done.11.outer_ref = f32[32,16,128]{2,1,0:T(8,128)S(1)} collective-permute-done((f32[32,16,128]{2,1,0:T(8,128)S(1)}, f32[32,16,128]{2,1,0:T(8,128)S(1)}, u32[]{:S(2)}, u32[]{:S(2)}) %collective-permute-start.11) | collective-permute-done | bytes 262176 | tf_op jit(solution)/shard_map/ppermute | solution.py:61
  34.5 1.3 %collective-permute-start.13 = (f32[32,32,128]{2,1,0:T(8,128)S(1)}, f32[32,32,128]{2,1,0:T(8,128)S(1)}, u32[]{:S(2)}, u32[]{:S(2)}) collective-permute-start(f32[32,32,128]{2,1,0:T(8,128)S(1)} %conv_x.19.refs_7_.refs_0_), channel_id=1, source_target_pairs={{0,16},{16,0},{1,17},{17,1},{2,18},{18,2},{3,19},{19,3},{4,20},{20... | collective-permute-start | bytes 1572872 | tf_op jit(solution)/shard_map/ppermute | solution.py:61
  37.8 1.4 %collective-permute-start.12 = (f32[32,16,128]{2,1,0:T(8,128)S(1)}, f32[32,16,128]{2,1,0:T(8,128)S(1)}, u32[]{:S(2)}, u32[]{:S(2)}) collective-permute-start(f32[32,16,128]{2,1,0:T(8,128)S(1)} %get-tuple-element.83.refs_2_), channel_id=1, source_target_pairs={{8,1},{1,8},{9,2},{2,9},{10,3},{3,10},{11,4},{4,11},{12,5},{5,12},... | collective-permute-start | bytes 786440 | tf_op jit(solution)/shard_map/ppermute | solution.py:61
  39.2 9.0 %collective-permute-done.7.outer_ref = f32[32,16,128]{2,1,0:T(8,128)S(1)} collective-permute-done((f32[32,16,128]{2,1,0:T(8,128)S(1)}, f32[32,16,128]{2,1,0:T(8,128)S(1)}, u32[]{:S(2)}, u32[]{:S(2)}) %collective-permute-start.7) | collective-permute-done | bytes 262176 | tf_op jit(solution)/shard_map/ppermute | solution.py:61
  51.4 1.3 %collective-permute-start.17 = (f32[32,16,128]{2,1,0:T(8,128)S(1)}, f32[32,16,128]{2,1,0:T(8,128)S(1)}, u32[]{:S(2)}, u32[]{:S(2)}) collective-permute-start(f32[32,16,128]{2,1,0:T(8,128)S(1)} %get-tuple-element.94.refs_2_), channel_id=1, source_target_pairs={{8,1},{1,8},{9,2},{2,9},{10,3},{3,10},{11,4},{4,11},{12,5},{5,12},... | collective-permute-start | bytes 786440 | tf_op jit(solution)/shard_map/ppermute | solution.py:61
  52.6 6.7 %collective-permute-done.14.refs_2_ = f32[32,32,128]{2,1,0:T(8,128)S(1)} collective-permute-done((f32[32,32,128]{2,1,0:T(8,128)S(1)}, f32[32,32,128]{2,1,0:T(8,128)S(1)}, u32[]{:S(2)}, u32[]{:S(2)}) %collective-permute-start.14) | collective-permute-done | bytes 524320 | tf_op jit(solution)/shard_map/ppermute | solution.py:61
  62.2 1.4 %update_y.2 = (f32[32,32,128]{2,1,0:T(8,128)S(1)}, f32[32,32,128]{2,1,0:T(8,128)S(1)}, f32[32,16,128]{2,1,0:T(8,128)S(1)}, f32[32,16,128]{2,1,0:T(8,128)S(1)}, f32[32,32,128]{2,1,0:T(8,128)S(1)}) custom-call(f32[32,32,128]{2,1,0:T(8,128)S(1)} %get-tuple-element.63.refs_3_.refs_0_, f32[32,32,128]{2,1,0:T(8,128)S(1)} %get-tuple-element.64.rest_0_.refs_1_, ...), custom_call_target="tpu_custom_call" | custom-call | tf_op jit(solution)/shard_map/update_y/pallas_call | solution.py:34
  63.6 1.3 %collective-permute-start.22 = (f32[32,32,128]{2,1,0:T(8,128)S(1)}, f32[32,32,128]{2,1,0:T(8,128)S(1)}, u32[]{:S(2)}, u32[]{:S(2)}) collective-permute-start(f32[32,32,128]{2,1,0:T(8,128)S(1)} %get-tuple-element.101.refs_0_), channel_id=1, source_target_pairs={{0,16},{16,0},{1,17},{17,1},{2,18},{18,2},{3,19},{19,3},{4,20},{20... | collective-permute-start | bytes 1572872 | tf_op jit(solution)/shard_map/ppermute | solution.py:61
  65.6 1.6 %update_y.3 = (f32[32,32,128]{2,1,0:T(8,128)S(1)}, f32[32,32,128]{2,1,0:T(8,128)S(1)}, f32[32,16,128]{2,1,0:T(8,128)S(1)}, f32[32,16,128]{2,1,0:T(8,128)S(1)}, f32[32,32,128]{2,1,0:T(8,128)S(1)}) custom-call(f32[32,32,128]{2,1,0:T(8,128)S(1)} %get-tuple-element.77.refs_4_.refs_0_, f32[32,32,128]{2,1,0:T(8,128)S(1)} %get-tuple-element.80.refs_5_.refs_1_, ...), custom_call_target="tpu_custom_call" | custom-call | tf_op jit(solution)/shard_map/update_y/pallas_call | solution.py:34
  67.1 1.6 %collective-permute-start.20 = (f32[32,16,128]{2,1,0:T(8,128)S(1)}, f32[32,16,128]{2,1,0:T(8,128)S(1)}, u32[]{:S(2)}, u32[]{:S(2)}) collective-permute-start(f32[32,16,128]{2,1,0:T(8,128)S(1)} %get-tuple-element.99.refs_2_), channel_id=1, source_target_pairs={{8,1},{1,8},{9,2},{2,9},{10,3},{3,10},{11,4},{4,11},{12,5},{5,12},... | collective-permute-start | bytes 786440 | tf_op jit(solution)/shard_map/ppermute | solution.py:61
  68.7 1.3 %collective-permute-start.21 = (f32[32,16,128]{2,1,0:T(8,128)S(1)}, f32[32,16,128]{2,1,0:T(8,128)S(1)}, u32[]{:S(2)}, u32[]{:S(2)}) collective-permute-start(f32[32,16,128]{2,1,0:T(8,128)S(1)} %get-tuple-element.100.refs_3_), channel_id=1, source_target_pairs={{0,8},{8,0},{1,9},{9,1},{2,10},{10,2},{3,11},{11,3},{4,12},{12,4},... | collective-permute-start | bytes 786440 | tf_op jit(solution)/shard_map/ppermute | solution.py:61
  70.0 4.2 %collective-permute-done.18.outer_ref = f32[32,16,128]{2,1,0:T(8,128)S(1)} collective-permute-done((f32[32,16,128]{2,1,0:T(8,128)S(1)}, f32[32,16,128]{2,1,0:T(8,128)S(1)}, u32[]{:S(2)}, u32[]{:S(2)}) %collective-permute-start.18) | collective-permute-done | bytes 262176 | tf_op jit(solution)/shard_map/ppermute | solution.py:61
  78.4 1.5 %collective-permute-start.26 = (f32[32,16,128]{2,1,0:T(8,128)S(1)}, f32[32,16,128]{2,1,0:T(8,128)S(1)}, u32[]{:S(2)}, u32[]{:S(2)}) collective-permute-start(f32[32,16,128]{2,1,0:T(8,128)S(1)} %get-tuple-element.106.refs_2_), channel_id=1, source_target_pairs={{8,1},{1,8},{9,2},{2,9},{10,3},{3,10},{11,4},{4,11},{12,5},{5,12},... | collective-permute-start | bytes 786440 | tf_op jit(solution)/shard_map/ppermute | solution.py:61
  79.9 6.0 %collective-permute-done.23.refs_2_ = f32[32,32,128]{2,1,0:T(8,128)S(1)} collective-permute-done((f32[32,32,128]{2,1,0:T(8,128)S(1)}, f32[32,32,128]{2,1,0:T(8,128)S(1)}, u32[]{:S(2)}, u32[]{:S(2)}) %collective-permute-start.23) | collective-permute-done | bytes 524320 | tf_op jit(solution)/shard_map/ppermute | solution.py:61
  86.9 1.7 %collective-permute-done.28.outer_ref = f32[32,16,128]{2,1,0:T(8,128)S(1)} collective-permute-done((f32[32,16,128]{2,1,0:T(8,128)S(1)}, f32[32,16,128]{2,1,0:T(8,128)S(1)}, u32[]{:S(2)}, u32[]{:S(2)}) %collective-permute-start.28) | collective-permute-done | bytes 262176 | tf_op jit(solution)/shard_map/ppermute | solution.py:61
  89.0 1.9 %collective-permute-start.30 = (f32[32,32,128]{2,1,0:T(8,128)S(1)}, f32[32,32,128]{2,1,0:T(8,128)S(1)}, u32[]{:S(2)}, u32[]{:S(2)}) collective-permute-start(f32[32,32,128]{2,1,0:T(8,128)S(1)} %conv_x.27.refs_7_.refs_0_), channel_id=1, source_target_pairs={{0,16},{16,0},{1,17},{17,1},{2,18},{18,2},{3,19},{19,3},{4,20},{20... | collective-permute-start | bytes 1572872 | tf_op jit(solution)/shard_map/ppermute | solution.py:61
  92.6 1.7 %collective-permute-start.29 = (f32[32,16,128]{2,1,0:T(8,128)S(1)}, f32[32,16,128]{2,1,0:T(8,128)S(1)}, u32[]{:S(2)}, u32[]{:S(2)}) collective-permute-start(f32[32,16,128]{2,1,0:T(8,128)S(1)} %get-tuple-element.109.refs_2_), channel_id=1, source_target_pairs={{8,1},{1,8},{9,2},{2,9},{10,3},{3,10},{11,4},{4,11},{12,5},{5,12},... | collective-permute-start | bytes 786440 | tf_op jit(solution)/shard_map/ppermute | solution.py:61
  94.3 8.6 %collective-permute-done.24.outer_ref = f32[32,16,128]{2,1,0:T(8,128)S(1)} collective-permute-done((f32[32,16,128]{2,1,0:T(8,128)S(1)}, f32[32,16,128]{2,1,0:T(8,128)S(1)}, u32[]{:S(2)}, u32[]{:S(2)}) %collective-permute-start.24) | collective-permute-done | bytes 262176 | tf_op jit(solution)/shard_map/ppermute | solution.py:61
  107.1 6.4 %collective-permute-done.31.refs_2_ = f32[32,32,128]{2,1,0:T(8,128)S(1)} collective-permute-done((f32[32,32,128]{2,1,0:T(8,128)S(1)}, f32[32,32,128]{2,1,0:T(8,128)S(1)}, u32[]{:S(2)}, u32[]{:S(2)}) %collective-permute-start.31) | collective-permute-done | bytes 524320 | tf_op jit(solution)/shard_map/ppermute | solution.py:61
  115.0 1.3 %collective-permute-done.32.outer_ref = f32[32,16,128]{2,1,0:T(8,128)S(1)} collective-permute-done((f32[32,16,128]{2,1,0:T(8,128)S(1)}, f32[32,16,128]{2,1,0:T(8,128)S(1)}, u32[]{:S(2)}, u32[]{:S(2)}) %collective-permute-start.32) | collective-permute-done | bytes 262176 | tf_op jit(solution)/shard_map/ppermute | solution.py:61
  116.7 2.4 %collective-permute-done.34.refs_1_ = f32[32,16,128]{2,1,0:T(8,128)S(1)} collective-permute-done((f32[32,16,128]{2,1,0:T(8,128)S(1)}, f32[32,16,128]{2,1,0:T(8,128)S(1)}, u32[]{:S(2)}, u32[]{:S(2)}) %collective-permute-start.34) | collective-permute-done | bytes 262176 | tf_op jit(solution)/shard_map/ppermute | solution.py:61
  119.5 1.2 last_slab.2
  120.8 1.1 last_slab.3.src_ref
  121.9 1.5 %put_half.2.refs_0_ = f32[32,64,256]{2,1,0:T(8,128)} custom-call(s32[3]{0:T(128)S(1)} %pad_add_fusion.ids_ref, f32[32,32,256]{2,1,0:T(8,128)S(1)} %last_slab.3.src_ref), custom_call_target="tpu_custom_call" | custom-call | tf_op jit(solution)/shard_map/put_half/pallas_call | solution.py:390
  123.5 1.5 %put_half.3 = f32[32,64,256]{2,1,0:T(8,128)} custom-call(s32[3]{0:T(128)S(1)} %pad_add_fusion.ids_ref, f32[32,32,256]{2,1,0:T(8,128)S(1)} %collective-permute-done.35.src_ref, f32[32,64,256]{2,1,0:T(8,128)} %put_half.2.refs_0_), custom_call_target="tpu_custom_call", output_to_operand_aliasing={{}: (2, {})} | custom-call | tf_op jit(solution)/shard_map/put_half/pallas_call | solution.py:390
  (93 shorter events, 34.5 us)
Async XLA Ops:
  6.5 13.7 %collective-permute-start.5 = (f32[32,32,128]{2,1,0:T(8,128)S(1)}, f32[32,32,128]{2,1,0:T(8,128)S(1)}, u32[]{:S(2)}, u32[]{:S(2)}) collective-permute-start(f32[32,32,128]{2,1,0:T(8,128)S(1)} %get-tuple-element.73.refs_0_), channel_id=1, source_target_pairs={{0,16},{16,0},{1,17},{17,1},{2,18},{18,2},{3,19},{19,3},{4,20},{20... | collective-permute-start | bytes 1572872 | tf_op jit(solution)/shard_map/ppermute | solution.py:61
  7.8 11.7 %collective-permute-start.1 = (f32[32,16,128]{2,1,0:T(8,128)S(1)}, f32[32,16,128]{2,1,0:T(8,128)S(1)}, u32[]{:S(2)}, u32[]{:S(2)}) collective-permute-start(f32[32,16,128]{2,1,0:T(8,128)S(1)} %get-tuple-element.69.e_ref), channel_id=1, source_target_pairs={{8,1},{1,8},{9,2},{2,9},{10,3},{3,10},{11,4},{4,11},{12,5},{5,12},... | collective-permute-start | bytes 786440 | tf_op jit(solution)/shard_map/ppermute | solution.py:61
  9.6 10.0 %collective-permute-start.2 = (f32[32,16,128]{2,1,0:T(8,128)S(1)}, f32[32,16,128]{2,1,0:T(8,128)S(1)}, u32[]{:S(2)}, u32[]{:S(2)}) collective-permute-start(f32[32,16,128]{2,1,0:T(8,128)S(1)} %get-tuple-element.70.i_ref), channel_id=1, source_target_pairs={{0,8},{8,0},{1,9},{9,1},{2,10},{10,2},{3,11},{11,3},{4,12},{12,4},... | collective-permute-start | bytes 786440 | tf_op jit(solution)/shard_map/ppermute | solution.py:61
  11.7 12.7 %collective-permute-start.3 = (f32[32,16,128]{2,1,0:T(8,128)S(1)}, f32[32,16,128]{2,1,0:T(8,128)S(1)}, u32[]{:S(2)}, u32[]{:S(2)}) collective-permute-start(f32[32,16,128]{2,1,0:T(8,128)S(1)} %get-tuple-element.71.refs_2_), channel_id=1, source_target_pairs={{8,1},{1,8},{9,2},{2,9},{10,3},{3,10},{11,4},{4,11},{12,5},{5,12},... | collective-permute-start | bytes 786440 | tf_op jit(solution)/shard_map/ppermute | solution.py:61
  12.0 12.4 %collective-permute-start.4 = (f32[32,16,128]{2,1,0:T(8,128)S(1)}, f32[32,16,128]{2,1,0:T(8,128)S(1)}, u32[]{:S(2)}, u32[]{:S(2)}) collective-permute-start(f32[32,16,128]{2,1,0:T(8,128)S(1)} %get-tuple-element.72.refs_3_), channel_id=1, source_target_pairs={{0,8},{8,0},{1,9},{9,1},{2,10},{10,2},{3,11},{11,3},{4,12},{12,4},... | collective-permute-start | bytes 786440 | tf_op jit(solution)/shard_map/ppermute | solution.py:61
  19.9 11.7 %collective-permute-start.6 = (f32[32,32,128]{2,1,0:T(8,128)S(1)}, f32[32,32,128]{2,1,0:T(8,128)S(1)}, u32[]{:S(2)}, u32[]{:S(2)}) collective-permute-start(f32[32,32,128]{2,1,0:T(8,128)S(1)} %conv_x.16.refs_6_.refs_0_), channel_id=1, source_target_pairs={{0,16},{16,0},{1,17},{17,1},{2,18},{18,2},{3,19},{19,3},{4,20},{20... | collective-permute-start | bytes 1572872 | tf_op jit(solution)/shard_map/ppermute | solution.py:61
  20.9 13.2 %collective-permute-start.10 = (f32[64,16,128]{2,1,0:T(8,128)S(1)}, f32[64,16,128]{2,1,0:T(8,128)S(1)}, u32[]{:S(2)}, u32[]{:S(2)}) collective-permute-start(f32[64,16,128]{2,1,0:T(8,128)S(1)} %conv_z.19.i_ref.refs_3_), channel_id=1, source_target_pairs={{0,8},{8,0},{1,9},{9,1},{2,10},{10,2},{3,11},{11,3},{4,12},{12,4},... | collective-permute-start | bytes 1572872 | tf_op jit(solution)/shard_map/ppermute | solution.py:61
  22.4 11.7 %collective-permute-start.11 = (f32[32,16,128]{2,1,0:T(8,128)S(1)}, f32[32,16,128]{2,1,0:T(8,128)S(1)}, u32[]{:S(2)}, u32[]{:S(2)}) collective-permute-start(f32[32,16,128]{2,1,0:T(8,128)S(1)} %get-tuple-element.82.e_ref), channel_id=1, source_target_pairs={{8,1},{1,8},{9,2},{2,9},{10,3},{3,10},{11,4},{4,11},{12,5},{5,12},... | collective-permute-start | bytes 786440 | tf_op jit(solution)/shard_map/ppermute | solution.py:61
  24.8 12.5 %collective-permute-start.9 = (f32[32,16,128]{2,1,0:T(8,128)S(1)}, f32[32,16,128]{2,1,0:T(8,128)S(1)}, u32[]{:S(2)}, u32[]{:S(2)}) collective-permute-start(f32[32,16,128]{2,1,0:T(8,128)S(1)} %get-tuple-element.79.refs_2_), channel_id=1, source_target_pairs={{8,1},{1,8},{9,2},{2,9},{10,3},{3,10},{11,4},{4,11},{12,5},{5,12},... | collective-permute-start | bytes 786440 | tf_op jit(solution)/shard_map/ppermute | solution.py:61
  32.6 15.5 %collective-permute-start.8 = (f32[64,16,128]{2,1,0:T(8,128)S(1)}, f32[64,16,128]{2,1,0:T(8,128)S(1)}, u32[]{:S(2)}, u32[]{:S(2)}) collective-permute-start(f32[64,16,128]{2,1,0:T(8,128)S(1)} %conv_z.18.i_ref.refs_3_), channel_id=1, source_target_pairs={{0,8},{8,0},{1,9},{9,1},{2,10},{10,2},{3,11},{11,3},{4,12},{12,4},... | collective-permute-start | bytes 1572872 | tf_op jit(solution)/shard_map/ppermute | solution.py:61
  34.5 14.3 %collective-permute-start.13 = (f32[32,32,128]{2,1,0:T(8,128)S(1)}, f32[32,32,128]{2,1,0:T(8,128)S(1)}, u32[]{:S(2)}, u32[]{:S(2)}) collective-permute-start(f32[32,32,128]{2,1,0:T(8,128)S(1)} %conv_x.19.refs_7_.refs_0_), channel_id=1, source_target_pairs={{0,16},{16,0},{1,17},{17,1},{2,18},{18,2},{3,19},{19,3},{4,20},{20... | collective-permute-start | bytes 1572872 | tf_op jit(solution)/shard_map/ppermute | solution.py:61
  36.8 11.4 %collective-permute-start.7 = (f32[32,16,128]{2,1,0:T(8,128)S(1)}, f32[32,16,128]{2,1,0:T(8,128)S(1)}, u32[]{:S(2)}, u32[]{:S(2)}) collective-permute-start(f32[32,16,128]{2,1,0:T(8,128)S(1)} %get-tuple-element.78.e_ref), channel_id=1, source_target_pairs={{8,1},{1,8},{9,2},{2,9},{10,3},{3,10},{11,4},{4,11},{12,5},{5,12},... | collective-permute-start | bytes 786440 | tf_op jit(solution)/shard_map/ppermute | solution.py:61
  37.8 13.2 %collective-permute-start.12 = (f32[32,16,128]{2,1,0:T(8,128)S(1)}, f32[32,16,128]{2,1,0:T(8,128)S(1)}, u32[]{:S(2)}, u32[]{:S(2)}) collective-permute-start(f32[32,16,128]{2,1,0:T(8,128)S(1)} %get-tuple-element.83.refs_2_), channel_id=1, source_target_pairs={{8,1},{1,8},{9,2},{2,9},{10,3},{3,10},{11,4},{4,11},{12,5},{5,12},... | collective-permute-start | bytes 786440 | tf_op jit(solution)/shard_map/ppermute | solution.py:61
  48.5 10.8 %collective-permute-start.14 = (f32[32,32,128]{2,1,0:T(8,128)S(1)}, f32[32,32,128]{2,1,0:T(8,128)S(1)}, u32[]{:S(2)}, u32[]{:S(2)}) collective-permute-start(f32[32,32,128]{2,1,0:T(8,128)S(1)} %conv_x.18.refs_6_.refs_0_), channel_id=1, source_target_pairs={{0,16},{16,0},{1,17},{17,1},{2,18},{18,2},{3,19},{19,3},{4,20},{20... | collective-permute-start | bytes 1572872 | tf_op jit(solution)/shard_map/ppermute | solution.py:61
  49.5 12.3 %collective-permute-start.16 = (f32[64,16,128]{2,1,0:T(8,128)S(1)}, f32[64,16,128]{2,1,0:T(8,128)S(1)}, u32[]{:S(2)}, u32[]{:S(2)}) collective-permute-start(f32[64,16,128]{2,1,0:T(8,128)S(1)} %conv_z.23.i_ref.refs_3_), channel_id=1, source_target_pairs={{0,8},{8,0},{1,9},{9,1},{2,10},{10,2},{3,11},{11,3},{4,12},{12,4},... | collective-permute-start | bytes 1572872 | tf_op jit(solution)/shard_map/ppermute | solution.py:61
  50.4 11.5 %collective-permute-start.15 = (f32[32,16,128]{2,1,0:T(8,128)S(1)}, f32[32,16,128]{2,1,0:T(8,128)S(1)}, u32[]{:S(2)}, u32[]{:S(2)}) collective-permute-start(f32[32,16,128]{2,1,0:T(8,128)S(1)} %get-tuple-element.88.e_ref), channel_id=1, source_target_pairs={{8,1},{1,8},{9,2},{2,9},{10,3},{3,10},{11,4},{4,11},{12,5},{5,12},... | collective-permute-start | bytes 786440 | tf_op jit(solution)/shard_map/ppermute | solution.py:61
  51.4 13.8 %collective-permute-start.17 = (f32[32,16,128]{2,1,0:T(8,128)S(1)}, f32[32,16,128]{2,1,0:T(8,128)S(1)}, u32[]{:S(2)}, u32[]{:S(2)}) collective-permute-start(f32[32,16,128]{2,1,0:T(8,128)S(1)} %get-tuple-element.94.refs_2_), channel_id=1, source_target_pairs={{8,1},{1,8},{9,2},{2,9},{10,3},{3,10},{11,4},{4,11},{12,5},{5,12},... | collective-permute-start | bytes 786440 | tf_op jit(solution)/shard_map/ppermute | solution.py:61
  63.6 12.0 %collective-permute-start.22 = (f32[32,32,128]{2,1,0:T(8,128)S(1)}, f32[32,32,128]{2,1,0:T(8,128)S(1)}, u32[]{:S(2)}, u32[]{:S(2)}) collective-permute-start(f32[32,32,128]{2,1,0:T(8,128)S(1)} %get-tuple-element.101.refs_0_), channel_id=1, source_target_pairs={{0,16},{16,0},{1,17},{17,1},{2,18},{18,2},{3,19},{19,3},{4,20},{20... | collective-permute-start | bytes 1572872 | tf_op jit(solution)/shard_map/ppermute | solution.py:61
  64.9 9.3 %collective-permute-start.18 = (f32[32,16,128]{2,1,0:T(8,128)S(1)}, f32[32,16,128]{2,1,0:T(8,128)S(1)}, u32[]{:S(2)}, u32[]{:S(2)}) collective-permute-start(f32[32,16,128]{2,1,0:T(8,128)S(1)} %get-tuple-element.97.e_ref), channel_id=1, source_target_pairs={{8,1},{1,8},{9,2},{2,9},{10,3},{3,10},{11,4},{4,11},{12,5},{5,12},... | collective-permute-start | bytes 786440 | tf_op jit(solution)/shard_map/ppermute | solution.py:61
  67.1 10.8 %collective-permute-start.20 = (f32[32,16,128]{2,1,0:T(8,128)S(1)}, f32[32,16,128]{2,1,0:T(8,128)S(1)}, u32[]{:S(2)}, u32[]{:S(2)}) collective-permute-start(f32[32,16,128]{2,1,0:T(8,128)S(1)} %get-tuple-element.99.refs_2_), channel_id=1, source_target_pairs={{8,1},{1,8},{9,2},{2,9},{10,3},{3,10},{11,4},{4,11},{12,5},{5,12},... | collective-permute-start | bytes 786440 | tf_op jit(solution)/shard_map/ppermute | solution.py:61
  74.6 11.3 %collective-permute-start.23 = (f32[32,32,128]{2,1,0:T(8,128)S(1)}, f32[32,32,128]{2,1,0:T(8,128)S(1)}, u32[]{:S(2)}, u32[]{:S(2)}) collective-permute-start(f32[32,32,128]{2,1,0:T(8,128)S(1)} %conv_x.24.refs_6_.refs_0_), channel_id=1, source_target_pairs={{0,16},{16,0},{1,17},{17,1},{2,18},{18,2},{3,19},{19,3},{4,20},{20... | collective-permute-start | bytes 1572872 | tf_op jit(solution)/shard_map/ppermute | solution.py:61
  76.3 12.3 %collective-permute-start.27 = (f32[64,16,128]{2,1,0:T(8,128)S(1)}, f32[64,16,128]{2,1,0:T(8,128)S(1)}, u32[]{:S(2)}, u32[]{:S(2)}) collective-permute-start(f32[64,16,128]{2,1,0:T(8,128)S(1)} %conv_z.27.i_ref.refs_3_), channel_id=1, source_target_pairs={{0,8},{8,0},{1,9},{9,1},{2,10},{10,2},{3,11},{11,3},{4,12},{12,4},... | collective-permute-start | bytes 1572872 | tf_op jit(solution)/shard_map/ppermute | solution.py:61
  77.1 11.5 %collective-permute-start.28 = (f32[32,16,128]{2,1,0:T(8,128)S(1)}, f32[32,16,128]{2,1,0:T(8,128)S(1)}, u32[]{:S(2)}, u32[]{:S(2)}) collective-permute-start(f32[32,16,128]{2,1,0:T(8,128)S(1)} %get-tuple-element.108.e_ref), channel_id=1, source_target_pairs={{8,1},{1,8},{9,2},{2,9},{10,3},{3,10},{11,4},{4,11},{12,5},{5,12},... | collective-permute-start | bytes 786440 | tf_op jit(solution)/shard_map/ppermute | solution.py:61
  78.4 13.8 %collective-permute-start.26 = (f32[32,16,128]{2,1,0:T(8,128)S(1)}, f32[32,16,128]{2,1,0:T(8,128)S(1)}, u32[]{:S(2)}, u32[]{:S(2)}) collective-permute-start(f32[32,16,128]{2,1,0:T(8,128)S(1)} %get-tuple-element.106.refs_2_), channel_id=1, source_target_pairs={{8,1},{1,8},{9,2},{2,9},{10,3},{3,10},{11,4},{4,11},{12,5},{5,12},... | collective-permute-start | bytes 786440 | tf_op jit(solution)/shard_map/ppermute | solution.py:61
  86.8 16.0 %collective-permute-start.25 = (f32[64,16,128]{2,1,0:T(8,128)S(1)}, f32[64,16,128]{2,1,0:T(8,128)S(1)}, u32[]{:S(2)}, u32[]{:S(2)}) collective-permute-start(f32[64,16,128]{2,1,0:T(8,128)S(1)} %conv_z.26.i_ref.refs_3_), channel_id=1, source_target_pairs={{0,8},{8,0},{1,9},{9,1},{2,10},{10,2},{3,11},{11,3},{4,12},{12,4},... | collective-permute-start | bytes 1572872 | tf_op jit(solution)/shard_map/ppermute | solution.py:61
  89.0 14.3 %collective-permute-start.30 = (f32[32,32,128]{2,1,0:T(8,128)S(1)}, f32[32,32,128]{2,1,0:T(8,128)S(1)}, u32[]{:S(2)}, u32[]{:S(2)}) collective-permute-start(f32[32,32,128]{2,1,0:T(8,128)S(1)} %conv_x.27.refs_7_.refs_0_), channel_id=1, source_target_pairs={{0,16},{16,0},{1,17},{17,1},{2,18},{18,2},{3,19},{19,3},{4,20},{20... | collective-permute-start | bytes 1572872 | tf_op jit(solution)/shard_map/ppermute | solution.py:61
  91.9 10.9 %collective-permute-start.24 = (f32[32,16,128]{2,1,0:T(8,128)S(1)}, f32[32,16,128]{2,1,0:T(8,128)S(1)}, u32[]{:S(2)}, u32[]{:S(2)}) collective-permute-start(f32[32,16,128]{2,1,0:T(8,128)S(1)} %get-tuple-element.105.e_ref), channel_id=1, source_target_pairs={{8,1},{1,8},{9,2},{2,9},{10,3},{3,10},{11,4},{4,11},{12,5},{5,12},... | collective-permute-start | bytes 786440 | tf_op jit(solution)/shard_map/ppermute | solution.py:61
  92.6 13.2 %collective-permute-start.29 = (f32[32,16,128]{2,1,0:T(8,128)S(1)}, f32[32,16,128]{2,1,0:T(8,128)S(1)}, u32[]{:S(2)}, u32[]{:S(2)}) collective-permute-start(f32[32,16,128]{2,1,0:T(8,128)S(1)} %get-tuple-element.109.refs_2_), channel_id=1, source_target_pairs={{8,1},{1,8},{9,2},{2,9},{10,3},{3,10},{11,4},{4,11},{12,5},{5,12},... | collective-permute-start | bytes 786440 | tf_op jit(solution)/shard_map/ppermute | solution.py:61
  103.3 10.3 %collective-permute-start.31 = (f32[32,32,128]{2,1,0:T(8,128)S(1)}, f32[32,32,128]{2,1,0:T(8,128)S(1)}, u32[]{:S(2)}, u32[]{:S(2)}) collective-permute-start(f32[32,32,128]{2,1,0:T(8,128)S(1)} %conv_x.26.refs_6_.refs_0_), channel_id=1, source_target_pairs={{0,16},{16,0},{1,17},{17,1},{2,18},{18,2},{3,19},{19,3},{4,20},{20... | collective-permute-start | bytes 1572872 | tf_op jit(solution)/shard_map/ppermute | solution.py:61
  104.0 12.3 %collective-permute-start.33 = (f32[64,16,128]{2,1,0:T(8,128)S(1)}, f32[64,16,128]{2,1,0:T(8,128)S(1)}, u32[]{:S(2)}, u32[]{:S(2)}) collective-permute-start(f32[64,16,128]{2,1,0:T(8,128)S(1)} %conv_z.31.i_ref.refs_3_), channel_id=1, source_target_pairs={{0,8},{8,0},{1,9},{9,1},{2,10},{10,2},{3,11},{11,3},{4,12},{12,4},... | collective-permute-start | bytes 1572872 | tf_op jit(solution)/shard_map/ppermute | solution.py:61
  104.8 11.5 %collective-permute-start.32 = (f32[32,16,128]{2,1,0:T(8,128)S(1)}, f32[32,16,128]{2,1,0:T(8,128)S(1)}, u32[]{:S(2)}, u32[]{:S(2)}) collective-permute-start(f32[32,16,128]{2,1,0:T(8,128)S(1)} %get-tuple-element.115.e_ref), channel_id=1, source_target_pairs={{8,1},{1,8},{9,2},{2,9},{10,3},{3,10},{11,4},{4,11},{12,5},{5,12},... | collective-permute-start | bytes 786440 | tf_op jit(solution)/shard_map/ppermute | solution.py:61
  106.2 13.0 %collective-permute-start.34 = (f32[32,16,128]{2,1,0:T(8,128)S(1)}, f32[32,16,128]{2,1,0:T(8,128)S(1)}, u32[]{:S(2)}, u32[]{:S(2)}) collective-permute-start(f32[32,16,128]{2,1,0:T(8,128)S(1)} %get-tuple-element.116.refs_2_), channel_id=1, source_target_pairs={{8,1},{1,8},{9,2},{2,9},{10,3},{3,10},{11,4},{4,11},{12,5},{5,12},... | collective-permute-start | bytes 786440 | tf_op jit(solution)/shard_map/ppermute | solution.py:61
  (8 other events, 41.4 us)

commit v6 on v5

--- a/solution.py
+++ b/solution.py
@@ -312,7 +312,7 @@
     return out[:2], out[2:]
 
 
-def last_slab(ids, estimate, parts, adj, mine, block=16):
+def last_give(ids, estimate, parts, adj, block=16):
     slab, width, half = estimate[0][0].shape
 
     def body(ids_ref, *refs):
@@ -320,7 +320,7 @@
         ins = ((e0, i, a), (e1, i, b))
         for s in (0, 1):
 
-            @pl.when(own_is_a(ids_ref) == ((s == 0) == mine))
+            @pl.when(own_is_a(ids_ref) != (s == 0))
             def _(s=s):
                 for z in range(0, slab, block):
                     out_ref[z : z + block] = rows(est[s], z, block) * mul_y(take(ins[s], s, z, block), ah_ref, al_ref)
@@ -331,7 +331,49 @@
         out_specs=VMEM,
         out_shape=shape(slab, width, 2 * half),
         compiler_params=params(),
-        name="last_slab",
+        name="last_give",
+    )(ids, *estimate[0], *estimate[1], *parts, *adj)
+
+
+def last_own(ids, estimate, parts, adj, block=16):
+    slab, width, half = estimate[0][0].shape
+    group = width // 2
+
+    def body(ids_ref, *refs):
+        est, (e0, e1, i, a, b), (ah_ref, al_ref, out_ref, new_ref, sems) = (refs[:2], refs[2:4]), refs[4:9], refs[9:]
+        ins = ((e0, i, a), (e1, i, b))
+        copies = [
+            [
+                pltpu.make_async_copy(
+                    new_ref.at[z : z + block, g * group : (g + 1) * group, :],
+                    out_ref.at[z : z + block, outward(ids_ref[0], g, group), :],
+                    sems.at[z // block, g],
+                )
+                for g in (0, 1)
+            ]
+            for z in range(0, slab, block)
+        ]
+        for s in (0, 1):
+
+            @pl.when(own_is_a(ids_ref) == (s == 0))
+            def _(s=s):
+                for z in range(0, slab, block):
+                    new_ref[z : z + block] = rows(est[s], z, block) * mul_y(take(ins[s], s, z, block), ah_ref, al_ref)
+                    for c in copies[z // block]:
+                        c.start()
+
+        for pair in copies:
+            for c in pair:
+                c.wait()
+
+    return pl.pallas_call(
+        body,
+        in_specs=[SMEM] + [VMEM] * 11,
+        out_specs=HBM,
+        out_shape=shape(slab, 2 * width, 2 * half),
+        scratch_shapes=[pltpu.VMEM((slab, width, 2 * half), F32), pltpu.SemaphoreType.DMA((slab // block, 2))],
+        compiler_params=params(),
+        name="last_own",
     )(ids, *estimate[0], *estimate[1], *parts, *adj)
 
 
@@ -368,16 +410,16 @@
     )(ids, volume)
 
 
-def put_half(ids, half, mine, whole=None):
-    slab, width, size_y = half.shape
+def put_half(ids, part, whole):
+    _, width, _ = part.shape
     group = width // 2
 
-    def body(ids_ref, src_ref, *refs):
-        out_ref, sems = refs[-2:]
-        core = ids_ref[0] if mine else 1 - ids_ref[0]
+    def body(ids_ref, src_ref, _, out_ref, sems):
         copies = [
             pltpu.make_async_copy(
-                src_ref.at[:, g * group : (g + 1) * group, :], out_ref.at[:, outward(core, g, group), :], sems.at[g]
+                src_ref.at[:, g * group : (g + 1) * group, :],
+                out_ref.at[:, outward(1 - ids_ref[0], g, group), :],
+                sems.at[g],
             )
             for g in (0, 1)
         ]
@@ -386,17 +428,16 @@
         for c in copies:
             c.wait()
 
-    args = [ids, half] + ([] if whole is None else [whole])
     return pl.pallas_call(
         body,
-        in_specs=[SMEM, VMEM] + ([] if whole is None else [HBM]),
+        in_specs=[SMEM, VMEM, HBM],
         out_specs=HBM,
-        out_shape=shape(slab, 2 * width, size_y),
+        out_shape=shape(*whole.shape),
         scratch_shapes=[pltpu.SemaphoreType.DMA((2,))],
-        input_output_aliases={} if whole is None else {2: 0},
+        input_output_aliases={2: 0},
         compiler_params=params(),
         name="put_half",
-    )(*args)
+    )(ids, part, whole)
 
 
 class Chunk:
@@ -447,10 +488,9 @@
     (e0, i0, a), (e1, i1, b) = parts
     left, right = (Chunk(links, mats, [v[side] for v in obs], p) for side, p in enumerate(([e0, e1, i0, i1], [a, b])))
     left.halos, right.halos = [None] * 4, []
-    left.send_x(2, 0)
     right.send_z(0, a)
     right.send_z(1, b)
-    left.send_x(3, 1)
+    left.send_x(0, 2, 3, 1)
     left.x(0)
     for half in range(4):
         c, other = (right, left) if half % 2 == 0 else (left, right)
@@ -496,9 +536,8 @@
             second = update_y(1, estimate[1], slabs[1], adj_y, fwd_y, first[0][0])
             estimate, parts = zip(first, second)
     parts = [e0, e1, i, a, b]
-    received = send(last_slab(ids, estimate, parts, adj_y, False), links.inner)
-    whole = put_half(ids, last_slab(ids, estimate, parts, adj_y, True), True)
-    return put_half(ids, received, False, whole)
+    received = send(last_give(ids, estimate, parts, adj_y), links.inner)
+    return put_half(ids, received, last_own(ids, estimate, parts, adj_y))
 
 
 def solution(mesh):

time: 126 us -> 126 us (level)
    pallas_call x4 -> x3, Pallas kernels: 5.37 us -> 4.85 us  [the longest x1 2.16 us: last_own(): pl.pallas_call(body, in_specs=[SMEM] + [VMEM] * 11, out_specs=HBM, out_sh...]
  transfers between devices with their start and end apart: 36 -> 36, of which waited for: 16 -> 17; matrix products, arithmetic and copies ran while one was open for 0% -> 0% of each run, Pallas kernels for 22% -> 22%
where the time goes in v6:
time: 126 us; the launch traced here: 125 us
  waiting for transfers between devices  64.3 us (51%)
  Pallas kernels  31.9 us (25%)
  starting transfers between devices  26.7 us (21%)
  local copies, waits for them, and re-layouts  1.61 us (1%)
    ppermute x36, waiting for transfers between devices, send(): return lax.ppermute(v, AXES, pairs)  64.3 us
    ppermute x36, starting transfers between devices, send(): return lax.ppermute(v, AXES, pairs)  26.7 us
    pallas_call x16, Pallas kernels, conv_z(): pl.pallas_call(body, in_specs=[VMEM] * len(args), out_specs=[VMEM] * len(...  12.3 us
    pallas_call x18, Pallas kernels, call(): return pl.pallas_call(body, in_specs=in_specs, **options)(*args)  9.53 us
  transfers between devices with their start and end apart: 36, of which 17 were waited for; matrix products, arithmetic and copies ran while one was open for 0% of the time, Pallas kernels for 22%

profile of v6, /device:TPU:25, one launch (start us, length us, event | category | flops | bytes accessed | tf_op | source)
XLA Modules:
  0.0 125.1 jit_solution(5682297039983211)
XLA Ops:
  0.1 1.6 %copy-done = f32[32,64,256]{2,1,0:T(8,128)S(1)} copy-done((f32[32,64,256]{2,1,0:T(8,128)S(1)}, f32[32,64,256]{2,1,0:T(8,128)}, u32[]{:S(2)}) %copy-start) | copy-done | bytes 2097176
  5.4 1.1 first_y.2
  6.5 1.3 %collective-permute-start.5 = (f32[32,32,128]{2,1,0:T(8,128)S(1)}, f32[32,32,128]{2,1,0:T(8,128)S(1)}, u32[]{:S(2)}, u32[]{:S(2)}) collective-permute-start(f32[32,32,128]{2,1,0:T(8,128)S(1)} %get-tuple-element.73.refs_0_), channel_id=1, source_target_pairs={{0,16},{16,0},{1,17},{17,1},{2,18},{18,2},{3,19},{19,3},{4,20},{20... | collective-permute-start | bytes 1572872 | tf_op jit(solution)/shard_map/ppermute | solution.py:61
  7.8 1.8 %collective-permute-start.1 = (f32[32,16,128]{2,1,0:T(8,128)S(1)}, f32[32,16,128]{2,1,0:T(8,128)S(1)}, u32[]{:S(2)}, u32[]{:S(2)}) collective-permute-start(f32[32,16,128]{2,1,0:T(8,128)S(1)} %get-tuple-element.69.e_ref), channel_id=1, source_target_pairs={{8,1},{1,8},{9,2},{2,9},{10,3},{3,10},{11,4},{4,11},{12,5},{5,12},... | collective-permute-start | bytes 786440 | tf_op jit(solution)/shard_map/ppermute | solution.py:61
  12.0 1.2 collective-permute-start.4
  13.3 6.3 %collective-permute-done.1.outer_ref = f32[32,16,128]{2,1,0:T(8,128)S(1)} collective-permute-done((f32[32,16,128]{2,1,0:T(8,128)S(1)}, f32[32,16,128]{2,1,0:T(8,128)S(1)}, u32[]{:S(2)}, u32[]{:S(2)}) %collective-permute-start.1) | collective-permute-done | bytes 262176 | tf_op jit(solution)/shard_map/ppermute | solution.py:61
  22.4 2.0 %collective-permute-start.11 = (f32[32,16,128]{2,1,0:T(8,128)S(1)}, f32[32,16,128]{2,1,0:T(8,128)S(1)}, u32[]{:S(2)}, u32[]{:S(2)}) collective-permute-start(f32[32,16,128]{2,1,0:T(8,128)S(1)} %get-tuple-element.82.e_ref), channel_id=1, source_target_pairs={{8,1},{1,8},{9,2},{2,9},{10,3},{3,10},{11,4},{4,11},{12,5},{5,12},... | collective-permute-start | bytes 786440 | tf_op jit(solution)/shard_map/ppermute | solution.py:61
  24.9 6.8 %collective-permute-done.6.refs_2_ = f32[32,32,128]{2,1,0:T(8,128)S(1)} collective-permute-done((f32[32,32,128]{2,1,0:T(8,128)S(1)}, f32[32,32,128]{2,1,0:T(8,128)S(1)}, u32[]{:S(2)}, u32[]{:S(2)}) %collective-permute-start.6) | collective-permute-done | bytes 524320 | tf_op jit(solution)/shard_map/ppermute | solution.py:61
  32.7 1.4 %collective-permute-done.11.outer_ref = f32[32,16,128]{2,1,0:T(8,128)S(1)} collective-permute-done((f32[32,16,128]{2,1,0:T(8,128)S(1)}, f32[32,16,128]{2,1,0:T(8,128)S(1)}, u32[]{:S(2)}, u32[]{:S(2)}) %collective-permute-start.11) | collective-permute-done | bytes 262176 | tf_op jit(solution)/shard_map/ppermute | solution.py:61
  34.5 1.3 %collective-permute-start.13 = (f32[32,32,128]{2,1,0:T(8,128)S(1)}, f32[32,32,128]{2,1,0:T(8,128)S(1)}, u32[]{:S(2)}, u32[]{:S(2)}) collective-permute-start(f32[32,32,128]{2,1,0:T(8,128)S(1)} %conv_x.19.refs_7_.refs_0_), channel_id=1, source_target_pairs={{0,16},{16,0},{1,17},{17,1},{2,18},{18,2},{3,19},{19,3},{4,20},{20... | collective-permute-start | bytes 1572872 | tf_op jit(solution)/shard_map/ppermute | solution.py:61
  37.8 1.4 %collective-permute-start.12 = (f32[32,16,128]{2,1,0:T(8,128)S(1)}, f32[32,16,128]{2,1,0:T(8,128)S(1)}, u32[]{:S(2)}, u32[]{:S(2)}) collective-permute-start(f32[32,16,128]{2,1,0:T(8,128)S(1)} %get-tuple-element.83.refs_2_), channel_id=1, source_target_pairs={{8,1},{1,8},{9,2},{2,9},{10,3},{3,10},{11,4},{4,11},{12,5},{5,12},... | collective-permute-start | bytes 786440 | tf_op jit(solution)/shard_map/ppermute | solution.py:61
  39.2 9.0 %collective-permute-done.7.outer_ref = f32[32,16,128]{2,1,0:T(8,128)S(1)} collective-permute-done((f32[32,16,128]{2,1,0:T(8,128)S(1)}, f32[32,16,128]{2,1,0:T(8,128)S(1)}, u32[]{:S(2)}, u32[]{:S(2)}) %collective-permute-start.7) | collective-permute-done | bytes 262176 | tf_op jit(solution)/shard_map/ppermute | solution.py:61
  51.4 1.3 %collective-permute-start.17 = (f32[32,16,128]{2,1,0:T(8,128)S(1)}, f32[32,16,128]{2,1,0:T(8,128)S(1)}, u32[]{:S(2)}, u32[]{:S(2)}) collective-permute-start(f32[32,16,128]{2,1,0:T(8,128)S(1)} %get-tuple-element.94.refs_2_), channel_id=1, source_target_pairs={{8,1},{1,8},{9,2},{2,9},{10,3},{3,10},{11,4},{4,11},{12,5},{5,12},... | collective-permute-start | bytes 786440 | tf_op jit(solution)/shard_map/ppermute | solution.py:61
  52.6 6.7 %collective-permute-done.14.refs_2_ = f32[32,32,128]{2,1,0:T(8,128)S(1)} collective-permute-done((f32[32,32,128]{2,1,0:T(8,128)S(1)}, f32[32,32,128]{2,1,0:T(8,128)S(1)}, u32[]{:S(2)}, u32[]{:S(2)}) %collective-permute-start.14) | collective-permute-done | bytes 524320 | tf_op jit(solution)/shard_map/ppermute | solution.py:61
  62.2 1.4 %update_y.2 = (f32[32,32,128]{2,1,0:T(8,128)S(1)}, f32[32,32,128]{2,1,0:T(8,128)S(1)}, f32[32,16,128]{2,1,0:T(8,128)S(1)}, f32[32,16,128]{2,1,0:T(8,128)S(1)}, f32[32,32,128]{2,1,0:T(8,128)S(1)}) custom-call(f32[32,32,128]{2,1,0:T(8,128)S(1)} %get-tuple-element.63.refs_3_.refs_0_, f32[32,32,128]{2,1,0:T(8,128)S(1)} %get-tuple-element.64.rest_0_.refs_1_, ...), custom_call_target="tpu_custom_call" | custom-call | tf_op jit(solution)/shard_map/update_y/pallas_call | solution.py:34
  63.6 1.3 %collective-permute-start.22 = (f32[32,32,128]{2,1,0:T(8,128)S(1)}, f32[32,32,128]{2,1,0:T(8,128)S(1)}, u32[]{:S(2)}, u32[]{:S(2)}) collective-permute-start(f32[32,32,128]{2,1,0:T(8,128)S(1)} %get-tuple-element.101.refs_0_), channel_id=1, source_target_pairs={{0,16},{16,0},{1,17},{17,1},{2,18},{18,2},{3,19},{19,3},{4,20},{20... | collective-permute-start | bytes 1572872 | tf_op jit(solution)/shard_map/ppermute | solution.py:61
  65.6 1.6 %update_y.3 = (f32[32,32,128]{2,1,0:T(8,128)S(1)}, f32[32,32,128]{2,1,0:T(8,128)S(1)}, f32[32,16,128]{2,1,0:T(8,128)S(1)}, f32[32,16,128]{2,1,0:T(8,128)S(1)}, f32[32,32,128]{2,1,0:T(8,128)S(1)}) custom-call(f32[32,32,128]{2,1,0:T(8,128)S(1)} %get-tuple-element.77.refs_4_.refs_0_, f32[32,32,128]{2,1,0:T(8,128)S(1)} %get-tuple-element.80.refs_5_.refs_1_, ...), custom_call_target="tpu_custom_call" | custom-call | tf_op jit(solution)/shard_map/update_y/pallas_call | solution.py:34
  67.1 1.6 %collective-permute-start.20 = (f32[32,16,128]{2,1,0:T(8,128)S(1)}, f32[32,16,128]{2,1,0:T(8,128)S(1)}, u32[]{:S(2)}, u32[]{:S(2)}) collective-permute-start(f32[32,16,128]{2,1,0:T(8,128)S(1)} %get-tuple-element.99.refs_2_), channel_id=1, source_target_pairs={{8,1},{1,8},{9,2},{2,9},{10,3},{3,10},{11,4},{4,11},{12,5},{5,12},... | collective-permute-start | bytes 786440 | tf_op jit(solution)/shard_map/ppermute | solution.py:61
  68.7 1.3 %collective-permute-start.21 = (f32[32,16,128]{2,1,0:T(8,128)S(1)}, f32[32,16,128]{2,1,0:T(8,128)S(1)}, u32[]{:S(2)}, u32[]{:S(2)}) collective-permute-start(f32[32,16,128]{2,1,0:T(8,128)S(1)} %get-tuple-element.100.refs_3_), channel_id=1, source_target_pairs={{0,8},{8,0},{1,9},{9,1},{2,10},{10,2},{3,11},{11,3},{4,12},{12,4},... | collective-permute-start | bytes 786440 | tf_op jit(solution)/shard_map/ppermute | solution.py:61
  70.0 4.2 %collective-permute-done.18.outer_ref = f32[32,16,128]{2,1,0:T(8,128)S(1)} collective-permute-done((f32[32,16,128]{2,1,0:T(8,128)S(1)}, f32[32,16,128]{2,1,0:T(8,128)S(1)}, u32[]{:S(2)}, u32[]{:S(2)}) %collective-permute-start.18) | collective-permute-done | bytes 262176 | tf_op jit(solution)/shard_map/ppermute | solution.py:61
  78.4 1.5 %collective-permute-start.26 = (f32[32,16,128]{2,1,0:T(8,128)S(1)}, f32[32,16,128]{2,1,0:T(8,128)S(1)}, u32[]{:S(2)}, u32[]{:S(2)}) collective-permute-start(f32[32,16,128]{2,1,0:T(8,128)S(1)} %get-tuple-element.106.refs_2_), channel_id=1, source_target_pairs={{8,1},{1,8},{9,2},{2,9},{10,3},{3,10},{11,4},{4,11},{12,5},{5,12},... | collective-permute-start | bytes 786440 | tf_op jit(solution)/shard_map/ppermute | solution.py:61
  79.9 6.0 %collective-permute-done.23.refs_2_ = f32[32,32,128]{2,1,0:T(8,128)S(1)} collective-permute-done((f32[32,32,128]{2,1,0:T(8,128)S(1)}, f32[32,32,128]{2,1,0:T(8,128)S(1)}, u32[]{:S(2)}, u32[]{:S(2)}) %collective-permute-start.23) | collective-permute-done | bytes 524320 | tf_op jit(solution)/shard_map/ppermute | solution.py:61
  86.9 1.7 %collective-permute-done.28.outer_ref = f32[32,16,128]{2,1,0:T(8,128)S(1)} collective-permute-done((f32[32,16,128]{2,1,0:T(8,128)S(1)}, f32[32,16,128]{2,1,0:T(8,128)S(1)}, u32[]{:S(2)}, u32[]{:S(2)}) %collective-permute-start.28) | collective-permute-done | bytes 262176 | tf_op jit(solution)/shard_map/ppermute | solution.py:61
  89.0 1.9 %collective-permute-start.30 = (f32[32,32,128]{2,1,0:T(8,128)S(1)}, f32[32,32,128]{2,1,0:T(8,128)S(1)}, u32[]{:S(2)}, u32[]{:S(2)}) collective-permute-start(f32[32,32,128]{2,1,0:T(8,128)S(1)} %conv_x.27.refs_7_.refs_0_), channel_id=1, source_target_pairs={{0,16},{16,0},{1,17},{17,1},{2,18},{18,2},{3,19},{19,3},{4,20},{20... | collective-permute-start | bytes 1572872 | tf_op jit(solution)/shard_map/ppermute | solution.py:61
  92.6 1.7 %collective-permute-start.29 = (f32[32,16,128]{2,1,0:T(8,128)S(1)}, f32[32,16,128]{2,1,0:T(8,128)S(1)}, u32[]{:S(2)}, u32[]{:S(2)}) collective-permute-start(f32[32,16,128]{2,1,0:T(8,128)S(1)} %get-tuple-element.109.refs_2_), channel_id=1, source_target_pairs={{8,1},{1,8},{9,2},{2,9},{10,3},{3,10},{11,4},{4,11},{12,5},{5,12},... | collective-permute-start | bytes 786440 | tf_op jit(solution)/shard_map/ppermute | solution.py:61
  94.3 8.6 %collective-permute-done.24.outer_ref = f32[32,16,128]{2,1,0:T(8,128)S(1)} collective-permute-done((f32[32,16,128]{2,1,0:T(8,128)S(1)}, f32[32,16,128]{2,1,0:T(8,128)S(1)}, u32[]{:S(2)}, u32[]{:S(2)}) %collective-permute-start.24) | collective-permute-done | bytes 262176 | tf_op jit(solution)/shard_map/ppermute | solution.py:61
  107.1 6.4 %collective-permute-done.31.refs_2_ = f32[32,32,128]{2,1,0:T(8,128)S(1)} collective-permute-done((f32[32,32,128]{2,1,0:T(8,128)S(1)}, f32[32,32,128]{2,1,0:T(8,128)S(1)}, u32[]{:S(2)}, u32[]{:S(2)}) %collective-permute-start.31) | collective-permute-done | bytes 524320 | tf_op jit(solution)/shard_map/ppermute | solution.py:61
  115.0 1.3 %collective-permute-done.32.outer_ref = f32[32,16,128]{2,1,0:T(8,128)S(1)} collective-permute-done((f32[32,16,128]{2,1,0:T(8,128)S(1)}, f32[32,16,128]{2,1,0:T(8,128)S(1)}, u32[]{:S(2)}, u32[]{:S(2)}) %collective-permute-start.32) | collective-permute-done | bytes 262176 | tf_op jit(solution)/shard_map/ppermute | solution.py:61
  116.7 2.4 %collective-permute-done.34.refs_1_ = f32[32,16,128]{2,1,0:T(8,128)S(1)} collective-permute-done((f32[32,16,128]{2,1,0:T(8,128)S(1)}, f32[32,16,128]{2,1,0:T(8,128)S(1)}, u32[]{:S(2)}, u32[]{:S(2)}) %collective-permute-start.34) | collective-permute-done | bytes 262176 | tf_op jit(solution)/shard_map/ppermute | solution.py:61
  119.5 1.2 last_give.1
  120.8 2.2 %last_own.1._ = f32[32,64,256]{2,1,0:T(8,128)} custom-call(s32[3]{0:T(128)S(1)} %pad_add_fusion.ids_ref, f32[32,32,128]{2,1,0:T(8,128)S(1)} %get-tuple-element.91.refs_9_.refs_0_, f32[32,32,128]{2,1,0:T(8,128)S(1)} %get-tuple-element.92.refs_1_, f32[32,32,128]{2,1,0:T(8,128)S(1)} %get-tuple-element.95.refs_2_, f32[32,32,128]{2,1,0:T(8,128)S(1)} %get-tuple-element.96.refs_3_, ...), custom_call_target="tpu_custom_call" | custom-call | tf_op jit(solution)/shard_map/last_own/pallas_call | solution.py:369
  123.4 1.5 %put_half.1 = f32[32,64,256]{2,1,0:T(8,128)} custom-call(s32[3]{0:T(128)S(1)} %pad_add_fusion.ids_ref, f32[32,32,256]{2,1,0:T(8,128)S(1)} %collective-permute-done.35.src_ref, f32[32,64,256]{2,1,0:T(8,128)} %last_own.1._), custom_call_target="tpu_custom_call", output_to_operand_aliasing={{}: (2, {})} | custom-call | tf_op jit(solution)/shard_map/put_half/pallas_call | solution.py:431
  (92 shorter events, 33.8 us)
Async XLA Ops:
  6.5 13.7 %collective-permute-start.5 = (f32[32,32,128]{2,1,0:T(8,128)S(1)}, f32[32,32,128]{2,1,0:T(8,128)S(1)}, u32[]{:S(2)}, u32[]{:S(2)}) collective-permute-start(f32[32,32,128]{2,1,0:T(8,128)S(1)} %get-tuple-element.73.refs_0_), channel_id=1, source_target_pairs={{0,16},{16,0},{1,17},{17,1},{2,18},{18,2},{3,19},{19,3},{4,20},{20... | collective-permute-start | bytes 1572872 | tf_op jit(solution)/shard_map/ppermute | solution.py:61
  7.8 11.7 %collective-permute-start.1 = (f32[32,16,128]{2,1,0:T(8,128)S(1)}, f32[32,16,128]{2,1,0:T(8,128)S(1)}, u32[]{:S(2)}, u32[]{:S(2)}) collective-permute-start(f32[32,16,128]{2,1,0:T(8,128)S(1)} %get-tuple-element.69.e_ref), channel_id=1, source_target_pairs={{8,1},{1,8},{9,2},{2,9},{10,3},{3,10},{11,4},{4,11},{12,5},{5,12},... | collective-permute-start | bytes 786440 | tf_op jit(solution)/shard_map/ppermute | solution.py:61
  9.6 10.0 %collective-permute-start.2 = (f32[32,16,128]{2,1,0:T(8,128)S(1)}, f32[32,16,128]{2,1,0:T(8,128)S(1)}, u32[]{:S(2)}, u32[]{:S(2)}) collective-permute-start(f32[32,16,128]{2,1,0:T(8,128)S(1)} %get-tuple-element.70.i_ref), channel_id=1, source_target_pairs={{0,8},{8,0},{1,9},{9,1},{2,10},{10,2},{3,11},{11,3},{4,12},{12,4},... | collective-permute-start | bytes 786440 | tf_op jit(solution)/shard_map/ppermute | solution.py:61
  11.7 12.7 %collective-permute-start.3 = (f32[32,16,128]{2,1,0:T(8,128)S(1)}, f32[32,16,128]{2,1,0:T(8,128)S(1)}, u32[]{:S(2)}, u32[]{:S(2)}) collective-permute-start(f32[32,16,128]{2,1,0:T(8,128)S(1)} %get-tuple-element.71.refs_2_), channel_id=1, source_target_pairs={{8,1},{1,8},{9,2},{2,9},{10,3},{3,10},{11,4},{4,11},{12,5},{5,12},... | collective-permute-start | bytes 786440 | tf_op jit(solution)/shard_map/ppermute | solution.py:61
  12.0 12.4 %collective-permute-start.4 = (f32[32,16,128]{2,1,0:T(8,128)S(1)}, f32[32,16,128]{2,1,0:T(8,128)S(1)}, u32[]{:S(2)}, u32[]{:S(2)}) collective-permute-start(f32[32,16,128]{2,1,0:T(8,128)S(1)} %get-tuple-element.72.refs_3_), channel_id=1, source_target_pairs={{0,8},{8,0},{1,9},{9,1},{2,10},{10,2},{3,11},{11,3},{4,12},{12,4},... | collective-permute-start | bytes 786440 | tf_op jit(solution)/shard_map/ppermute | solution.py:61
  19.9 11.7 %collective-permute-start.6 = (f32[32,32,128]{2,1,0:T(8,128)S(1)}, f32[32,32,128]{2,1,0:T(8,128)S(1)}, u32[]{:S(2)}, u32[]{:S(2)}) collective-permute-start(f32[32,32,128]{2,1,0:T(8,128)S(1)} %conv_x.16.refs_6_.refs_0_), channel_id=1, source_target_pairs={{0,16},{16,0},{1,17},{17,1},{2,18},{18,2},{3,19},{19,3},{4,20},{20... | collective-permute-start | bytes 1572872 | tf_op jit(solution)/shard_map/ppermute | solution.py:61
  20.9 13.2 %collective-permute-start.10 = (f32[64,16,128]{2,1,0:T(8,128)S(1)}, f32[64,16,128]{2,1,0:T(8,128)S(1)}, u32[]{:S(2)}, u32[]{:S(2)}) collective-permute-start(f32[64,16,128]{2,1,0:T(8,128)S(1)} %conv_z.19.i_ref.refs_3_), channel_id=1, source_target_pairs={{0,8},{8,0},{1,9},{9,1},{2,10},{10,2},{3,11},{11,3},{4,12},{12,4},... | collective-permute-start | bytes 1572872 | tf_op jit(solution)/shard_map/ppermute | solution.py:61
  22.4 11.7 %collective-permute-start.11 = (f32[32,16,128]{2,1,0:T(8,128)S(1)}, f32[32,16,128]{2,1,0:T(8,128)S(1)}, u32[]{:S(2)}, u32[]{:S(2)}) collective-permute-start(f32[32,16,128]{2,1,0:T(8,128)S(1)} %get-tuple-element.82.e_ref), channel_id=1, source_target_pairs={{8,1},{1,8},{9,2},{2,9},{10,3},{3,10},{11,4},{4,11},{12,5},{5,12},... | collective-permute-start | bytes 786440 | tf_op jit(solution)/shard_map/ppermute | solution.py:61
  24.8 12.5 %collective-permute-start.9 = (f32[32,16,128]{2,1,0:T(8,128)S(1)}, f32[32,16,128]{2,1,0:T(8,128)S(1)}, u32[]{:S(2)}, u32[]{:S(2)}) collective-permute-start(f32[32,16,128]{2,1,0:T(8,128)S(1)} %get-tuple-element.79.refs_2_), channel_id=1, source_target_pairs={{8,1},{1,8},{9,2},{2,9},{10,3},{3,10},{11,4},{4,11},{12,5},{5,12},... | collective-permute-start | bytes 786440 | tf_op jit(solution)/shard_map/ppermute | solution.py:61
  32.6 15.5 %collective-permute-start.8 = (f32[64,16,128]{2,1,0:T(8,128)S(1)}, f32[64,16,128]{2,1,0:T(8,128)S(1)}, u32[]{:S(2)}, u32[]{:S(2)}) collective-permute-start(f32[64,16,128]{2,1,0:T(8,128)S(1)} %conv_z.18.i_ref.refs_3_), channel_id=1, source_target_pairs={{0,8},{8,0},{1,9},{9,1},{2,10},{10,2},{3,11},{11,3},{4,12},{12,4},... | collective-permute-start | bytes 1572872 | tf_op jit(solution)/shard_map/ppermute | solution.py:61
  34.5 14.3 %collective-permute-start.13 = (f32[32,32,128]{2,1,0:T(8,128)S(1)}, f32[32,32,128]{2,1,0:T(8,128)S(1)}, u32[]{:S(2)}, u32[]{:S(2)}) collective-permute-start(f32[32,32,128]{2,1,0:T(8,128)S(1)} %conv_x.19.refs_7_.refs_0_), channel_id=1, source_target_pairs={{0,16},{16,0},{1,17},{17,1},{2,18},{18,2},{3,19},{19,3},{4,20},{20... | collective-permute-start | bytes 1572872 | tf_op jit(solution)/shard_map/ppermute | solution.py:61
  36.8 11.4 %collective-permute-start.7 = (f32[32,16,128]{2,1,0:T(8,128)S(1)}, f32[32,16,128]{2,1,0:T(8,128)S(1)}, u32[]{:S(2)}, u32[]{:S(2)}) collective-permute-start(f32[32,16,128]{2,1,0:T(8,128)S(1)} %get-tuple-element.78.e_ref), channel_id=1, source_target_pairs={{8,1},{1,8},{9,2},{2,9},{10,3},{3,10},{11,4},{4,11},{12,5},{5,12},... | collective-permute-start | bytes 786440 | tf_op jit(solution)/shard_map/ppermute | solution.py:61
  37.8 13.2 %collective-permute-start.12 = (f32[32,16,128]{2,1,0:T(8,128)S(1)}, f32[32,16,128]{2,1,0:T(8,128)S(1)}, u32[]{:S(2)}, u32[]{:S(2)}) collective-permute-start(f32[32,16,128]{2,1,0:T(8,128)S(1)} %get-tuple-element.83.refs_2_), channel_id=1, source_target_pairs={{8,1},{1,8},{9,2},{2,9},{10,3},{3,10},{11,4},{4,11},{12,5},{5,12},... | collective-permute-start | bytes 786440 | tf_op jit(solution)/shard_map/ppermute | solution.py:61
  48.5 10.8 %collective-permute-start.14 = (f32[32,32,128]{2,1,0:T(8,128)S(1)}, f32[32,32,128]{2,1,0:T(8,128)S(1)}, u32[]{:S(2)}, u32[]{:S(2)}) collective-permute-start(f32[32,32,128]{2,1,0:T(8,128)S(1)} %conv_x.18.refs_6_.refs_0_), channel_id=1, source_target_pairs={{0,16},{16,0},{1,17},{17,1},{2,18},{18,2},{3,19},{19,3},{4,20},{20... | collective-permute-start | bytes 1572872 | tf_op jit(solution)/shard_map/ppermute | solution.py:61
  49.5 12.3 %collective-permute-start.16 = (f32[64,16,128]{2,1,0:T(8,128)S(1)}, f32[64,16,128]{2,1,0:T(8,128)S(1)}, u32[]{:S(2)}, u32[]{:S(2)}) collective-permute-start(f32[64,16,128]{2,1,0:T(8,128)S(1)} %conv_z.23.i_ref.refs_3_), channel_id=1, source_target_pairs={{0,8},{8,0},{1,9},{9,1},{2,10},{10,2},{3,11},{11,3},{4,12},{12,4},... | collective-permute-start | bytes 1572872 | tf_op jit(solution)/shard_map/ppermute | solution.py:61
  50.4 11.5 %collective-permute-start.15 = (f32[32,16,128]{2,1,0:T(8,128)S(1)}, f32[32,16,128]{2,1,0:T(8,128)S(1)}, u32[]{:S(2)}, u32[]{:S(2)}) collective-permute-start(f32[32,16,128]{2,1,0:T(8,128)S(1)} %get-tuple-element.88.e_ref), channel_id=1, source_target_pairs={{8,1},{1,8},{9,2},{2,9},{10,3},{3,10},{11,4},{4,11},{12,5},{5,12},... | collective-permute-start | bytes 786440 | tf_op jit(solution)/shard_map/ppermute | solution.py:61
  51.4 13.8 %collective-permute-start.17 = (f32[32,16,128]{2,1,0:T(8,128)S(1)}, f32[32,16,128]{2,1,0:T(8,128)S(1)}, u32[]{:S(2)}, u32[]{:S(2)}) collective-permute-start(f32[32,16,128]{2,1,0:T(8,128)S(1)} %get-tuple-element.94.refs_2_), channel_id=1, source_target_pairs={{8,1},{1,8},{9,2},{2,9},{10,3},{3,10},{11,4},{4,11},{12,5},{5,12},... | collective-permute-start | bytes 786440 | tf_op jit(solution)/shard_map/ppermute | solution.py:61
  63.6 12.0 %collective-permute-start.22 = (f32[32,32,128]{2,1,0:T(8,128)S(1)}, f32[32,32,128]{2,1,0:T(8,128)S(1)}, u32[]{:S(2)}, u32[]{:S(2)}) collective-permute-start(f32[32,32,128]{2,1,0:T(8,128)S(1)} %get-tuple-element.101.refs_0_), channel_id=1, source_target_pairs={{0,16},{16,0},{1,17},{17,1},{2,18},{18,2},{3,19},{19,3},{4,20},{20... | collective-permute-start | bytes 1572872 | tf_op jit(solution)/shard_map/ppermute | solution.py:61
  64.9 9.3 %collective-permute-start.18 = (f32[32,16,128]{2,1,0:T(8,128)S(1)}, f32[32,16,128]{2,1,0:T(8,128)S(1)}, u32[]{:S(2)}, u32[]{:S(2)}) collective-permute-start(f32[32,16,128]{2,1,0:T(8,128)S(1)} %get-tuple-element.97.e_ref), channel_id=1, source_target_pairs={{8,1},{1,8},{9,2},{2,9},{10,3},{3,10},{11,4},{4,11},{12,5},{5,12},... | collective-permute-start | bytes 786440 | tf_op jit(solution)/shard_map/ppermute | solution.py:61
  67.1 10.8 %collective-permute-start.20 = (f32[32,16,128]{2,1,0:T(8,128)S(1)}, f32[32,16,128]{2,1,0:T(8,128)S(1)}, u32[]{:S(2)}, u32[]{:S(2)}) collective-permute-start(f32[32,16,128]{2,1,0:T(8,128)S(1)} %get-tuple-element.99.refs_2_), channel_id=1, source_target_pairs={{8,1},{1,8},{9,2},{2,9},{10,3},{3,10},{11,4},{4,11},{12,5},{5,12},... | collective-permute-start | bytes 786440 | tf_op jit(solution)/shard_map/ppermute | solution.py:61
  74.6 11.3 %collective-permute-start.23 = (f32[32,32,128]{2,1,0:T(8,128)S(1)}, f32[32,32,128]{2,1,0:T(8,128)S(1)}, u32[]{:S(2)}, u32[]{:S(2)}) collective-permute-start(f32[32,32,128]{2,1,0:T(8,128)S(1)} %conv_x.24.refs_6_.refs_0_), channel_id=1, source_target_pairs={{0,16},{16,0},{1,17},{17,1},{2,18},{18,2},{3,19},{19,3},{4,20},{20... | collective-permute-start | bytes 1572872 | tf_op jit(solution)/shard_map/ppermute | solution.py:61
  76.3 12.3 %collective-permute-start.27 = (f32[64,16,128]{2,1,0:T(8,128)S(1)}, f32[64,16,128]{2,1,0:T(8,128)S(1)}, u32[]{:S(2)}, u32[]{:S(2)}) collective-permute-start(f32[64,16,128]{2,1,0:T(8,128)S(1)} %conv_z.27.i_ref.refs_3_), channel_id=1, source_target_pairs={{0,8},{8,0},{1,9},{9,1},{2,10},{10,2},{3,11},{11,3},{4,12},{12,4},... | collective-permute-start | bytes 1572872 | tf_op jit(solution)/shard_map/ppermute | solution.py:61
  77.1 11.5 %collective-permute-start.28 = (f32[32,16,128]{2,1,0:T(8,128)S(1)}, f32[32,16,128]{2,1,0:T(8,128)S(1)}, u32[]{:S(2)}, u32[]{:S(2)}) collective-permute-start(f32[32,16,128]{2,1,0:T(8,128)S(1)} %get-tuple-element.108.e_ref), channel_id=1, source_target_pairs={{8,1},{1,8},{9,2},{2,9},{10,3},{3,10},{11,4},{4,11},{12,5},{5,12},... | collective-permute-start | bytes 786440 | tf_op jit(solution)/shard_map/ppermute | solution.py:61
  78.4 13.8 %collective-permute-start.26 = (f32[32,16,128]{2,1,0:T(8,128)S(1)}, f32[32,16,128]{2,1,0:T(8,128)S(1)}, u32[]{:S(2)}, u32[]{:S(2)}) collective-permute-start(f32[32,16,128]{2,1,0:T(8,128)S(1)} %get-tuple-element.106.refs_2_), channel_id=1, source_target_pairs={{8,1},{1,8},{9,2},{2,9},{10,3},{3,10},{11,4},{4,11},{12,5},{5,12},... | collective-permute-start | bytes 786440 | tf_op jit(solution)/shard_map/ppermute | solution.py:61
  86.8 16.0 %collective-permute-start.25 = (f32[64,16,128]{2,1,0:T(8,128)S(1)}, f32[64,16,128]{2,1,0:T(8,128)S(1)}, u32[]{:S(2)}, u32[]{:S(2)}) collective-permute-start(f32[64,16,128]{2,1,0:T(8,128)S(1)} %conv_z.26.i_ref.refs_3_), channel_id=1, source_target_pairs={{0,8},{8,0},{1,9},{9,1},{2,10},{10,2},{3,11},{11,3},{4,12},{12,4},... | collective-permute-start | bytes 1572872 | tf_op jit(solution)/shard_map/ppermute | solution.py:61
  89.0 14.3 %collective-permute-start.30 = (f32[32,32,128]{2,1,0:T(8,128)S(1)}, f32[32,32,128]{2,1,0:T(8,128)S(1)}, u32[]{:S(2)}, u32[]{:S(2)}) collective-permute-start(f32[32,32,128]{2,1,0:T(8,128)S(1)} %conv_x.27.refs_7_.refs_0_), channel_id=1, source_target_pairs={{0,16},{16,0},{1,17},{17,1},{2,18},{18,2},{3,19},{19,3},{4,20},{20... | collective-permute-start | bytes 1572872 | tf_op jit(solution)/shard_map/ppermute | solution.py:61
  91.9 10.9 %collective-permute-start.24 = (f32[32,16,128]{2,1,0:T(8,128)S(1)}, f32[32,16,128]{2,1,0:T(8,128)S(1)}, u32[]{:S(2)}, u32[]{:S(2)}) collective-permute-start(f32[32,16,128]{2,1,0:T(8,128)S(1)} %get-tuple-element.105.e_ref), channel_id=1, source_target_pairs={{8,1},{1,8},{9,2},{2,9},{10,3},{3,10},{11,4},{4,11},{12,5},{5,12},... | collective-permute-start | bytes 786440 | tf_op jit(solution)/shard_map/ppermute | solution.py:61
  92.6 13.2 %collective-permute-start.29 = (f32[32,16,128]{2,1,0:T(8,128)S(1)}, f32[32,16,128]{2,1,0:T(8,128)S(1)}, u32[]{:S(2)}, u32[]{:S(2)}) collective-permute-start(f32[32,16,128]{2,1,0:T(8,128)S(1)} %get-tuple-element.109.refs_2_), channel_id=1, source_target_pairs={{8,1},{1,8},{9,2},{2,9},{10,3},{3,10},{11,4},{4,11},{12,5},{5,12},... | collective-permute-start | bytes 786440 | tf_op jit(solution)/shard_map/ppermute | solution.py:61
  103.3 10.3 %collective-permute-start.31 = (f32[32,32,128]{2,1,0:T(8,128)S(1)}, f32[32,32,128]{2,1,0:T(8,128)S(1)}, u32[]{:S(2)}, u32[]{:S(2)}) collective-permute-start(f32[32,32,128]{2,1,0:T(8,128)S(1)} %conv_x.26.refs_6_.refs_0_), channel_id=1, source_target_pairs={{0,16},{16,0},{1,17},{17,1},{2,18},{18,2},{3,19},{19,3},{4,20},{20... | collective-permute-start | bytes 1572872 | tf_op jit(solution)/shard_map/ppermute | solution.py:61
  104.0 12.3 %collective-permute-start.33 = (f32[64,16,128]{2,1,0:T(8,128)S(1)}, f32[64,16,128]{2,1,0:T(8,128)S(1)}, u32[]{:S(2)}, u32[]{:S(2)}) collective-permute-start(f32[64,16,128]{2,1,0:T(8,128)S(1)} %conv_z.31.i_ref.refs_3_), channel_id=1, source_target_pairs={{0,8},{8,0},{1,9},{9,1},{2,10},{10,2},{3,11},{11,3},{4,12},{12,4},... | collective-permute-start | bytes 1572872 | tf_op jit(solution)/shard_map/ppermute | solution.py:61
  104.8 11.5 %collective-permute-start.32 = (f32[32,16,128]{2,1,0:T(8,128)S(1)}, f32[32,16,128]{2,1,0:T(8,128)S(1)}, u32[]{:S(2)}, u32[]{:S(2)}) collective-permute-start(f32[32,16,128]{2,1,0:T(8,128)S(1)} %get-tuple-element.115.e_ref), channel_id=1, source_target_pairs={{8,1},{1,8},{9,2},{2,9},{10,3},{3,10},{11,4},{4,11},{12,5},{5,12},... | collective-permute-start | bytes 786440 | tf_op jit(solution)/shard_map/ppermute | solution.py:61
  106.2 13.0 %collective-permute-start.34 = (f32[32,16,128]{2,1,0:T(8,128)S(1)}, f32[32,16,128]{2,1,0:T(8,128)S(1)}, u32[]{:S(2)}, u32[]{:S(2)}) collective-permute-start(f32[32,16,128]{2,1,0:T(8,128)S(1)} %get-tuple-element.116.refs_2_), channel_id=1, source_target_pairs={{8,1},{1,8},{9,2},{2,9},{10,3},{3,10},{11,4},{4,11},{12,5},{5,12},... | collective-permute-start | bytes 786440 | tf_op jit(solution)/shard_map/ppermute | solution.py:61
  (8 other events, 41.4 us)

commit v7 on v6

--- a/solution.py
+++ b/solution.py
@@ -265,7 +265,7 @@
     return ids_ref[0] != ids_ref[1]
 
 
-def first_y(ids, s, own, received, mat, block=16):
+def first_y(ids, s, own, received, mat, block=8):
     slab, width, size_y = own.shape
 
     def body(ids_ref, own_ref, got_ref, h_ref, l_ref, *refs):
@@ -288,7 +288,7 @@
     return out[:2], out[2:]
 
 
-def update_y(s, estimate, parts, adj, fwd, after=None, block=16):
+def update_y(s, estimate, parts, adj, fwd, after=None, block=8):
     slab, width, half = estimate[0].shape
 
     def body(*refs):
@@ -312,7 +312,7 @@
     return out[:2], out[2:]
 
 
-def last_give(ids, estimate, parts, adj, block=16):
+def last_give(ids, estimate, parts, adj, block=8):
     slab, width, half = estimate[0][0].shape
 
     def body(ids_ref, *refs):
@@ -335,7 +335,7 @@
     )(ids, *estimate[0], *estimate[1], *parts, *adj)
 
 
-def last_own(ids, estimate, parts, adj, block=16):
+def last_own(ids, estimate, parts, adj, block=8):
     slab, width, half = estimate[0][0].shape
     group = width // 2
 

time: 126 us -> 125 us (level)
  transfers between devices with their start and end apart: 36 -> 36, of which waited for: 17 -> 17; matrix products, arithmetic and copies ran while one was open for 0% -> 0% of each run, Pallas kernels for 22% -> 21%
where the time goes in v7:
time: 125 us
  waiting for transfers between devices  64.8 us (52%)
  Pallas kernels  31.5 us (25%)
  starting transfers between devices  26.5 us (21%)
  local copies, waits for them, and re-layouts  1.61 us (1%)
    ppermute x36, waiting for transfers between devices, send(): return lax.ppermute(v, AXES, pairs)  64.8 us
    ppermute x36, starting transfers between devices, send(): return lax.ppermute(v, AXES, pairs)  26.5 us
    pallas_call x16, Pallas kernels, conv_z(): pl.pallas_call(body, in_specs=[VMEM] * len(args), out_specs=[VMEM] * len(...  12.3 us
    pallas_call x18, Pallas kernels, call(): return pl.pallas_call(body, in_specs=in_specs, **options)(*args)  9.27 us
  transfers between devices with their start and end apart: 36, of which 17 were waited for; matrix products, arithmetic and copies ran while one was open for 0% of the time, Pallas kernels for 21%

profile of v7, /device:TPU:25, one launch (start us, length us, event | category | flops | bytes accessed | tf_op | source)
XLA Modules:
  0.0 125.0 jit_solution(11274291317162994297)
XLA Ops:
  0.1 1.6 %copy-done = f32[32,64,256]{2,1,0:T(8,128)S(1)} copy-done((f32[32,64,256]{2,1,0:T(8,128)S(1)}, f32[32,64,256]{2,1,0:T(8,128)}, u32[]{:S(2)}) %copy-start) | copy-done | bytes 2097176
  6.5 1.3 %collective-permute-start.5 = (f32[32,32,128]{2,1,0:T(8,128)S(1)}, f32[32,32,128]{2,1,0:T(8,128)S(1)}, u32[]{:S(2)}, u32[]{:S(2)}) collective-permute-start(f32[32,32,128]{2,1,0:T(8,128)S(1)} %get-tuple-element.73.refs_0_), channel_id=1, source_target_pairs={{0,16},{16,0},{1,17},{17,1},{2,18},{18,2},{3,19},{19,3},{4,20},{20... | collective-permute-start | bytes 1572872 | tf_op jit(solution)/shard_map/ppermute | solution.py:61
  7.8 1.7 %collective-permute-start.1 = (f32[32,16,128]{2,1,0:T(8,128)S(1)}, f32[32,16,128]{2,1,0:T(8,128)S(1)}, u32[]{:S(2)}, u32[]{:S(2)}) collective-permute-start(f32[32,16,128]{2,1,0:T(8,128)S(1)} %get-tuple-element.69.e_ref), channel_id=1, source_target_pairs={{8,1},{1,8},{9,2},{2,9},{10,3},{3,10},{11,4},{4,11},{12,5},{5,12},... | collective-permute-start | bytes 786440 | tf_op jit(solution)/shard_map/ppermute | solution.py:61
  10.5 1.1 first_y.3
  12.0 1.3 %collective-permute-start.4 = (f32[32,16,128]{2,1,0:T(8,128)S(1)}, f32[32,16,128]{2,1,0:T(8,128)S(1)}, u32[]{:S(2)}, u32[]{:S(2)}) collective-permute-start(f32[32,16,128]{2,1,0:T(8,128)S(1)} %get-tuple-element.72.refs_3_), channel_id=1, source_target_pairs={{0,8},{8,0},{1,9},{9,1},{2,10},{10,2},{3,11},{11,3},{4,12},{12,4},... | collective-permute-start | bytes 786440 | tf_op jit(solution)/shard_map/ppermute | solution.py:61
  13.3 6.2 %collective-permute-done.1.outer_ref = f32[32,16,128]{2,1,0:T(8,128)S(1)} collective-permute-done((f32[32,16,128]{2,1,0:T(8,128)S(1)}, f32[32,16,128]{2,1,0:T(8,128)S(1)}, u32[]{:S(2)}, u32[]{:S(2)}) %collective-permute-start.1) | collective-permute-done | bytes 262176 | tf_op jit(solution)/shard_map/ppermute | solution.py:61
  22.4 2.0 %collective-permute-start.11 = (f32[32,16,128]{2,1,0:T(8,128)S(1)}, f32[32,16,128]{2,1,0:T(8,128)S(1)}, u32[]{:S(2)}, u32[]{:S(2)}) collective-permute-start(f32[32,16,128]{2,1,0:T(8,128)S(1)} %get-tuple-element.82.e_ref), channel_id=1, source_target_pairs={{8,1},{1,8},{9,2},{2,9},{10,3},{3,10},{11,4},{4,11},{12,5},{5,12},... | collective-permute-start | bytes 786440 | tf_op jit(solution)/shard_map/ppermute | solution.py:61
  24.9 6.8 %collective-permute-done.6.refs_2_ = f32[32,32,128]{2,1,0:T(8,128)S(1)} collective-permute-done((f32[32,32,128]{2,1,0:T(8,128)S(1)}, f32[32,32,128]{2,1,0:T(8,128)S(1)}, u32[]{:S(2)}, u32[]{:S(2)}) %collective-permute-start.6) | collective-permute-done | bytes 524320 | tf_op jit(solution)/shard_map/ppermute | solution.py:61
  32.7 1.4 %collective-permute-done.11.outer_ref = f32[32,16,128]{2,1,0:T(8,128)S(1)} collective-permute-done((f32[32,16,128]{2,1,0:T(8,128)S(1)}, f32[32,16,128]{2,1,0:T(8,128)S(1)}, u32[]{:S(2)}, u32[]{:S(2)}) %collective-permute-start.11) | collective-permute-done | bytes 262176 | tf_op jit(solution)/shard_map/ppermute | solution.py:61
  34.5 1.3 %collective-permute-start.13 = (f32[32,32,128]{2,1,0:T(8,128)S(1)}, f32[32,32,128]{2,1,0:T(8,128)S(1)}, u32[]{:S(2)}, u32[]{:S(2)}) collective-permute-start(f32[32,32,128]{2,1,0:T(8,128)S(1)} %conv_x.19.refs_7_.refs_0_), channel_id=1, source_target_pairs={{0,16},{16,0},{1,17},{17,1},{2,18},{18,2},{3,19},{19,3},{4,20},{20... | collective-permute-start | bytes 1572872 | tf_op jit(solution)/shard_map/ppermute | solution.py:61
  37.8 1.4 %collective-permute-start.12 = (f32[32,16,128]{2,1,0:T(8,128)S(1)}, f32[32,16,128]{2,1,0:T(8,128)S(1)}, u32[]{:S(2)}, u32[]{:S(2)}) collective-permute-start(f32[32,16,128]{2,1,0:T(8,128)S(1)} %get-tuple-element.83.refs_2_), channel_id=1, source_target_pairs={{8,1},{1,8},{9,2},{2,9},{10,3},{3,10},{11,4},{4,11},{12,5},{5,12},... | collective-permute-start | bytes 786440 | tf_op jit(solution)/shard_map/ppermute | solution.py:61
  39.2 9.0 %collective-permute-done.7.outer_ref = f32[32,16,128]{2,1,0:T(8,128)S(1)} collective-permute-done((f32[32,16,128]{2,1,0:T(8,128)S(1)}, f32[32,16,128]{2,1,0:T(8,128)S(1)}, u32[]{:S(2)}, u32[]{:S(2)}) %collective-permute-start.7) | collective-permute-done | bytes 262176 | tf_op jit(solution)/shard_map/ppermute | solution.py:61
  51.4 1.3 %collective-permute-start.17 = (f32[32,16,128]{2,1,0:T(8,128)S(1)}, f32[32,16,128]{2,1,0:T(8,128)S(1)}, u32[]{:S(2)}, u32[]{:S(2)}) collective-permute-start(f32[32,16,128]{2,1,0:T(8,128)S(1)} %get-tuple-element.94.refs_2_), channel_id=1, source_target_pairs={{8,1},{1,8},{9,2},{2,9},{10,3},{3,10},{11,4},{4,11},{12,5},{5,12},... | collective-permute-start | bytes 786440 | tf_op jit(solution)/shard_map/ppermute | solution.py:61
  52.6 6.7 %collective-permute-done.14.refs_2_ = f32[32,32,128]{2,1,0:T(8,128)S(1)} collective-permute-done((f32[32,32,128]{2,1,0:T(8,128)S(1)}, f32[32,32,128]{2,1,0:T(8,128)S(1)}, u32[]{:S(2)}, u32[]{:S(2)}) %collective-permute-start.14) | collective-permute-done | bytes 524320 | tf_op jit(solution)/shard_map/ppermute | solution.py:61
  62.2 1.2 update_y.2
  63.5 1.3 %collective-permute-start.22 = (f32[32,32,128]{2,1,0:T(8,128)S(1)}, f32[32,32,128]{2,1,0:T(8,128)S(1)}, u32[]{:S(2)}, u32[]{:S(2)}) collective-permute-start(f32[32,32,128]{2,1,0:T(8,128)S(1)} %get-tuple-element.101.refs_0_), channel_id=1, source_target_pairs={{0,16},{16,0},{1,17},{17,1},{2,18},{18,2},{3,19},{19,3},{4,20},{20... | collective-permute-start | bytes 1572872 | tf_op jit(solution)/shard_map/ppermute | solution.py:61
  65.4 1.4 %update_y.3 = (f32[32,32,128]{2,1,0:T(8,128)S(1)}, f32[32,32,128]{2,1,0:T(8,128)S(1)}, f32[32,16,128]{2,1,0:T(8,128)S(1)}, f32[32,16,128]{2,1,0:T(8,128)S(1)}, f32[32,32,128]{2,1,0:T(8,128)S(1)}) custom-call(f32[32,32,128]{2,1,0:T(8,128)S(1)} %get-tuple-element.77.refs_4_.refs_0_, f32[32,32,128]{2,1,0:T(8,128)S(1)} %get-tuple-element.80.refs_5_.refs_1_, ...), custom_call_target="tpu_custom_call" | custom-call | tf_op jit(solution)/shard_map/update_y/pallas_call | solution.py:34
  66.9 1.5 %collective-permute-start.20 = (f32[32,16,128]{2,1,0:T(8,128)S(1)}, f32[32,16,128]{2,1,0:T(8,128)S(1)}, u32[]{:S(2)}, u32[]{:S(2)}) collective-permute-start(f32[32,16,128]{2,1,0:T(8,128)S(1)} %get-tuple-element.99.refs_2_), channel_id=1, source_target_pairs={{8,1},{1,8},{9,2},{2,9},{10,3},{3,10},{11,4},{4,11},{12,5},{5,12},... | collective-permute-start | bytes 786440 | tf_op jit(solution)/shard_map/ppermute | solution.py:61
  68.4 1.3 %collective-permute-start.21 = (f32[32,16,128]{2,1,0:T(8,128)S(1)}, f32[32,16,128]{2,1,0:T(8,128)S(1)}, u32[]{:S(2)}, u32[]{:S(2)}) collective-permute-start(f32[32,16,128]{2,1,0:T(8,128)S(1)} %get-tuple-element.100.refs_3_), channel_id=1, source_target_pairs={{0,8},{8,0},{1,9},{9,1},{2,10},{10,2},{3,11},{11,3},{4,12},{12,4},... | collective-permute-start | bytes 786440 | tf_op jit(solution)/shard_map/ppermute | solution.py:61
  69.7 4.3 %collective-permute-done.18.outer_ref = f32[32,16,128]{2,1,0:T(8,128)S(1)} collective-permute-done((f32[32,16,128]{2,1,0:T(8,128)S(1)}, f32[32,16,128]{2,1,0:T(8,128)S(1)}, u32[]{:S(2)}, u32[]{:S(2)}) %collective-permute-start.18) | collective-permute-done | bytes 262176 | tf_op jit(solution)/shard_map/ppermute | solution.py:61
  78.3 1.5 %collective-permute-start.26 = (f32[32,16,128]{2,1,0:T(8,128)S(1)}, f32[32,16,128]{2,1,0:T(8,128)S(1)}, u32[]{:S(2)}, u32[]{:S(2)}) collective-permute-start(f32[32,16,128]{2,1,0:T(8,128)S(1)} %get-tuple-element.106.refs_2_), channel_id=1, source_target_pairs={{8,1},{1,8},{9,2},{2,9},{10,3},{3,10},{11,4},{4,11},{12,5},{5,12},... | collective-permute-start | bytes 786440 | tf_op jit(solution)/shard_map/ppermute | solution.py:61
  79.7 6.0 %collective-permute-done.23.refs_2_ = f32[32,32,128]{2,1,0:T(8,128)S(1)} collective-permute-done((f32[32,32,128]{2,1,0:T(8,128)S(1)}, f32[32,32,128]{2,1,0:T(8,128)S(1)}, u32[]{:S(2)}, u32[]{:S(2)}) %collective-permute-start.23) | collective-permute-done | bytes 524320 | tf_op jit(solution)/shard_map/ppermute | solution.py:61
  86.8 1.8 %collective-permute-done.28.outer_ref = f32[32,16,128]{2,1,0:T(8,128)S(1)} collective-permute-done((f32[32,16,128]{2,1,0:T(8,128)S(1)}, f32[32,16,128]{2,1,0:T(8,128)S(1)}, u32[]{:S(2)}, u32[]{:S(2)}) %collective-permute-start.28) | collective-permute-done | bytes 262176 | tf_op jit(solution)/shard_map/ppermute | solution.py:61
  89.0 1.8 %collective-permute-start.30 = (f32[32,32,128]{2,1,0:T(8,128)S(1)}, f32[32,32,128]{2,1,0:T(8,128)S(1)}, u32[]{:S(2)}, u32[]{:S(2)}) collective-permute-start(f32[32,32,128]{2,1,0:T(8,128)S(1)} %conv_x.27.refs_7_.refs_0_), channel_id=1, source_target_pairs={{0,16},{16,0},{1,17},{17,1},{2,18},{18,2},{3,19},{19,3},{4,20},{20... | collective-permute-start | bytes 1572872 | tf_op jit(solution)/shard_map/ppermute | solution.py:61
  92.4 1.7 %collective-permute-start.29 = (f32[32,16,128]{2,1,0:T(8,128)S(1)}, f32[32,16,128]{2,1,0:T(8,128)S(1)}, u32[]{:S(2)}, u32[]{:S(2)}) collective-permute-start(f32[32,16,128]{2,1,0:T(8,128)S(1)} %get-tuple-element.109.refs_2_), channel_id=1, source_target_pairs={{8,1},{1,8},{9,2},{2,9},{10,3},{3,10},{11,4},{4,11},{12,5},{5,12},... | collective-permute-start | bytes 786440 | tf_op jit(solution)/shard_map/ppermute | solution.py:61
  94.1 8.6 %collective-permute-done.24.outer_ref = f32[32,16,128]{2,1,0:T(8,128)S(1)} collective-permute-done((f32[32,16,128]{2,1,0:T(8,128)S(1)}, f32[32,16,128]{2,1,0:T(8,128)S(1)}, u32[]{:S(2)}, u32[]{:S(2)}) %collective-permute-start.24) | collective-permute-done | bytes 262176 | tf_op jit(solution)/shard_map/ppermute | solution.py:61
  107.0 6.4 %collective-permute-done.31.refs_2_ = f32[32,32,128]{2,1,0:T(8,128)S(1)} collective-permute-done((f32[32,32,128]{2,1,0:T(8,128)S(1)}, f32[32,32,128]{2,1,0:T(8,128)S(1)}, u32[]{:S(2)}, u32[]{:S(2)}) %collective-permute-start.31) | collective-permute-done | bytes 524320 | tf_op jit(solution)/shard_map/ppermute | solution.py:61
  114.9 1.3 %collective-permute-done.32.outer_ref = f32[32,16,128]{2,1,0:T(8,128)S(1)} collective-permute-done((f32[32,16,128]{2,1,0:T(8,128)S(1)}, f32[32,16,128]{2,1,0:T(8,128)S(1)}, u32[]{:S(2)}, u32[]{:S(2)}) %collective-permute-start.32) | collective-permute-done | bytes 262176 | tf_op jit(solution)/shard_map/ppermute | solution.py:61
  116.6 2.4 %collective-permute-done.34.refs_1_ = f32[32,16,128]{2,1,0:T(8,128)S(1)} collective-permute-done((f32[32,16,128]{2,1,0:T(8,128)S(1)}, f32[32,16,128]{2,1,0:T(8,128)S(1)}, u32[]{:S(2)}, u32[]{:S(2)}) %collective-permute-start.34) | collective-permute-done | bytes 262176 | tf_op jit(solution)/shard_map/ppermute | solution.py:61
  119.4 1.2 last_give.1
  120.7 2.0 %last_own.1._ = f32[32,64,256]{2,1,0:T(8,128)} custom-call(s32[3]{0:T(128)S(1)} %pad_add_fusion.ids_ref, f32[32,32,128]{2,1,0:T(8,128)S(1)} %get-tuple-element.91.refs_9_.refs_0_, f32[32,32,128]{2,1,0:T(8,128)S(1)} %get-tuple-element.92.refs_1_, f32[32,32,128]{2,1,0:T(8,128)S(1)} %get-tuple-element.95.refs_2_, f32[32,32,128]{2,1,0:T(8,128)S(1)} %get-tuple-element.96.refs_3_, ...), custom_call_target="tpu_custom_call" | custom-call | tf_op jit(solution)/shard_map/last_own/pallas_call | solution.py:369
  123.3 1.5 %put_half.1 = f32[32,64,256]{2,1,0:T(8,128)} custom-call(s32[3]{0:T(128)S(1)} %pad_add_fusion.ids_ref, f32[32,32,256]{2,1,0:T(8,128)S(1)} %collective-permute-done.35.src_ref, f32[32,64,256]{2,1,0:T(8,128)} %last_own.1._), custom_call_target="tpu_custom_call", output_to_operand_aliasing={{}: (2, {})} | custom-call | tf_op jit(solution)/shard_map/put_half/pallas_call | solution.py:431
  (92 shorter events, 34.0 us)
Async XLA Ops:
  6.5 13.7 %collective-permute-start.5 = (f32[32,32,128]{2,1,0:T(8,128)S(1)}, f32[32,32,128]{2,1,0:T(8,128)S(1)}, u32[]{:S(2)}, u32[]{:S(2)}) collective-permute-start(f32[32,32,128]{2,1,0:T(8,128)S(1)} %get-tuple-element.73.refs_0_), channel_id=1, source_target_pairs={{0,16},{16,0},{1,17},{17,1},{2,18},{18,2},{3,19},{19,3},{4,20},{20... | collective-permute-start | bytes 1572872 | tf_op jit(solution)/shard_map/ppermute | solution.py:61
  7.8 11.7 %collective-permute-start.1 = (f32[32,16,128]{2,1,0:T(8,128)S(1)}, f32[32,16,128]{2,1,0:T(8,128)S(1)}, u32[]{:S(2)}, u32[]{:S(2)}) collective-permute-start(f32[32,16,128]{2,1,0:T(8,128)S(1)} %get-tuple-element.69.e_ref), channel_id=1, source_target_pairs={{8,1},{1,8},{9,2},{2,9},{10,3},{3,10},{11,4},{4,11},{12,5},{5,12},... | collective-permute-start | bytes 786440 | tf_op jit(solution)/shard_map/ppermute | solution.py:61
  9.6 10.0 %collective-permute-start.2 = (f32[32,16,128]{2,1,0:T(8,128)S(1)}, f32[32,16,128]{2,1,0:T(8,128)S(1)}, u32[]{:S(2)}, u32[]{:S(2)}) collective-permute-start(f32[32,16,128]{2,1,0:T(8,128)S(1)} %get-tuple-element.70.i_ref), channel_id=1, source_target_pairs={{0,8},{8,0},{1,9},{9,1},{2,10},{10,2},{3,11},{11,3},{4,12},{12,4},... | collective-permute-start | bytes 786440 | tf_op jit(solution)/shard_map/ppermute | solution.py:61
  11.7 12.7 %collective-permute-start.3 = (f32[32,16,128]{2,1,0:T(8,128)S(1)}, f32[32,16,128]{2,1,0:T(8,128)S(1)}, u32[]{:S(2)}, u32[]{:S(2)}) collective-permute-start(f32[32,16,128]{2,1,0:T(8,128)S(1)} %get-tuple-element.71.refs_2_), channel_id=1, source_target_pairs={{8,1},{1,8},{9,2},{2,9},{10,3},{3,10},{11,4},{4,11},{12,5},{5,12},... | collective-permute-start | bytes 786440 | tf_op jit(solution)/shard_map/ppermute | solution.py:61
  12.0 12.4 %collective-permute-start.4 = (f32[32,16,128]{2,1,0:T(8,128)S(1)}, f32[32,16,128]{2,1,0:T(8,128)S(1)}, u32[]{:S(2)}, u32[]{:S(2)}) collective-permute-start(f32[32,16,128]{2,1,0:T(8,128)S(1)} %get-tuple-element.72.refs_3_), channel_id=1, source_target_pairs={{0,8},{8,0},{1,9},{9,1},{2,10},{10,2},{3,11},{11,3},{4,12},{12,4},... | collective-permute-start | bytes 786440 | tf_op jit(solution)/shard_map/ppermute | solution.py:61
  19.9 11.7 %collective-permute-start.6 = (f32[32,32,128]{2,1,0:T(8,128)S(1)}, f32[32,32,128]{2,1,0:T(8,128)S(1)}, u32[]{:S(2)}, u32[]{:S(2)}) collective-permute-start(f32[32,32,128]{2,1,0:T(8,128)S(1)} %conv_x.16.refs_6_.refs_0_), channel_id=1, source_target_pairs={{0,16},{16,0},{1,17},{17,1},{2,18},{18,2},{3,19},{19,3},{4,20},{20... | collective-permute-start | bytes 1572872 | tf_op jit(solution)/shard_map/ppermute | solution.py:61
  20.9 13.2 %collective-permute-start.10 = (f32[64,16,128]{2,1,0:T(8,128)S(1)}, f32[64,16,128]{2,1,0:T(8,128)S(1)}, u32[]{:S(2)}, u32[]{:S(2)}) collective-permute-start(f32[64,16,128]{2,1,0:T(8,128)S(1)} %conv_z.19.i_ref.refs_3_), channel_id=1, source_target_pairs={{0,8},{8,0},{1,9},{9,1},{2,10},{10,2},{3,11},{11,3},{4,12},{12,4},... | collective-permute-start | bytes 1572872 | tf_op jit(solution)/shard_map/ppermute | solution.py:61
  22.4 11.7 %collective-permute-start.11 = (f32[32,16,128]{2,1,0:T(8,128)S(1)}, f32[32,16,128]{2,1,0:T(8,128)S(1)}, u32[]{:S(2)}, u32[]{:S(2)}) collective-permute-start(f32[32,16,128]{2,1,0:T(8,128)S(1)} %get-tuple-element.82.e_ref), channel_id=1, source_target_pairs={{8,1},{1,8},{9,2},{2,9},{10,3},{3,10},{11,4},{4,11},{12,5},{5,12},... | collective-permute-start | bytes 786440 | tf_op jit(solution)/shard_map/ppermute | solution.py:61
  24.8 12.5 %collective-permute-start.9 = (f32[32,16,128]{2,1,0:T(8,128)S(1)}, f32[32,16,128]{2,1,0:T(8,128)S(1)}, u32[]{:S(2)}, u32[]{:S(2)}) collective-permute-start(f32[32,16,128]{2,1,0:T(8,128)S(1)} %get-tuple-element.79.refs_2_), channel_id=1, source_target_pairs={{8,1},{1,8},{9,2},{2,9},{10,3},{3,10},{11,4},{4,11},{12,5},{5,12},... | collective-permute-start | bytes 786440 | tf_op jit(solution)/shard_map/ppermute | solution.py:61
  32.6 15.5 %collective-permute-start.8 = (f32[64,16,128]{2,1,0:T(8,128)S(1)}, f32[64,16,128]{2,1,0:T(8,128)S(1)}, u32[]{:S(2)}, u32[]{:S(2)}) collective-permute-start(f32[64,16,128]{2,1,0:T(8,128)S(1)} %conv_z.18.i_ref.refs_3_), channel_id=1, source_target_pairs={{0,8},{8,0},{1,9},{9,1},{2,10},{10,2},{3,11},{11,3},{4,12},{12,4},... | collective-permute-start | bytes 1572872 | tf_op jit(solution)/shard_map/ppermute | solution.py:61
  34.5 14.3 %collective-permute-start.13 = (f32[32,32,128]{2,1,0:T(8,128)S(1)}, f32[32,32,128]{2,1,0:T(8,128)S(1)}, u32[]{:S(2)}, u32[]{:S(2)}) collective-permute-start(f32[32,32,128]{2,1,0:T(8,128)S(1)} %conv_x.19.refs_7_.refs_0_), channel_id=1, source_target_pairs={{0,16},{16,0},{1,17},{17,1},{2,18},{18,2},{3,19},{19,3},{4,20},{20... | collective-permute-start | bytes 1572872 | tf_op jit(solution)/shard_map/ppermute | solution.py:61
  36.8 11.4 %collective-permute-start.7 = (f32[32,16,128]{2,1,0:T(8,128)S(1)}, f32[32,16,128]{2,1,0:T(8,128)S(1)}, u32[]{:S(2)}, u32[]{:S(2)}) collective-permute-start(f32[32,16,128]{2,1,0:T(8,128)S(1)} %get-tuple-element.78.e_ref), channel_id=1, source_target_pairs={{8,1},{1,8},{9,2},{2,9},{10,3},{3,10},{11,4},{4,11},{12,5},{5,12},... | collective-permute-start | bytes 786440 | tf_op jit(solution)/shard_map/ppermute | solution.py:61
  37.8 13.2 %collective-permute-start.12 = (f32[32,16,128]{2,1,0:T(8,128)S(1)}, f32[32,16,128]{2,1,0:T(8,128)S(1)}, u32[]{:S(2)}, u32[]{:S(2)}) collective-permute-start(f32[32,16,128]{2,1,0:T(8,128)S(1)} %get-tuple-element.83.refs_2_), channel_id=1, source_target_pairs={{8,1},{1,8},{9,2},{2,9},{10,3},{3,10},{11,4},{4,11},{12,5},{5,12},... | collective-permute-start | bytes 786440 | tf_op jit(solution)/shard_map/ppermute | solution.py:61
  48.5 10.8 %collective-permute-start.14 = (f32[32,32,128]{2,1,0:T(8,128)S(1)}, f32[32,32,128]{2,1,0:T(8,128)S(1)}, u32[]{:S(2)}, u32[]{:S(2)}) collective-permute-start(f32[32,32,128]{2,1,0:T(8,128)S(1)} %conv_x.18.refs_6_.refs_0_), channel_id=1, source_target_pairs={{0,16},{16,0},{1,17},{17,1},{2,18},{18,2},{3,19},{19,3},{4,20},{20... | collective-permute-start | bytes 1572872 | tf_op jit(solution)/shard_map/ppermute | solution.py:61
  49.5 12.3 %collective-permute-start.16 = (f32[64,16,128]{2,1,0:T(8,128)S(1)}, f32[64,16,128]{2,1,0:T(8,128)S(1)}, u32[]{:S(2)}, u32[]{:S(2)}) collective-permute-start(f32[64,16,128]{2,1,0:T(8,128)S(1)} %conv_z.23.i_ref.refs_3_), channel_id=1, source_target_pairs={{0,8},{8,0},{1,9},{9,1},{2,10},{10,2},{3,11},{11,3},{4,12},{12,4},... | collective-permute-start | bytes 1572872 | tf_op jit(solution)/shard_map/ppermute | solution.py:61
  50.3 11.5 %collective-permute-start.15 = (f32[32,16,128]{2,1,0:T(8,128)S(1)}, f32[32,16,128]{2,1,0:T(8,128)S(1)}, u32[]{:S(2)}, u32[]{:S(2)}) collective-permute-start(f32[32,16,128]{2,1,0:T(8,128)S(1)} %get-tuple-element.88.e_ref), channel_id=1, source_target_pairs={{8,1},{1,8},{9,2},{2,9},{10,3},{3,10},{11,4},{4,11},{12,5},{5,12},... | collective-permute-start | bytes 786440 | tf_op jit(solution)/shard_map/ppermute | solution.py:61
  51.4 13.7 %collective-permute-start.17 = (f32[32,16,128]{2,1,0:T(8,128)S(1)}, f32[32,16,128]{2,1,0:T(8,128)S(1)}, u32[]{:S(2)}, u32[]{:S(2)}) collective-permute-start(f32[32,16,128]{2,1,0:T(8,128)S(1)} %get-tuple-element.94.refs_2_), channel_id=1, source_target_pairs={{8,1},{1,8},{9,2},{2,9},{10,3},{3,10},{11,4},{4,11},{12,5},{5,12},... | collective-permute-start | bytes 786440 | tf_op jit(solution)/shard_map/ppermute | solution.py:61
  63.5 12.1 %collective-permute-start.22 = (f32[32,32,128]{2,1,0:T(8,128)S(1)}, f32[32,32,128]{2,1,0:T(8,128)S(1)}, u32[]{:S(2)}, u32[]{:S(2)}) collective-permute-start(f32[32,32,128]{2,1,0:T(8,128)S(1)} %get-tuple-element.101.refs_0_), channel_id=1, source_target_pairs={{0,16},{16,0},{1,17},{17,1},{2,18},{18,2},{3,19},{19,3},{4,20},{20... | collective-permute-start | bytes 1572872 | tf_op jit(solution)/shard_map/ppermute | solution.py:61
  66.9 11.0 %collective-permute-start.20 = (f32[32,16,128]{2,1,0:T(8,128)S(1)}, f32[32,16,128]{2,1,0:T(8,128)S(1)}, u32[]{:S(2)}, u32[]{:S(2)}) collective-permute-start(f32[32,16,128]{2,1,0:T(8,128)S(1)} %get-tuple-element.99.refs_2_), channel_id=1, source_target_pairs={{8,1},{1,8},{9,2},{2,9},{10,3},{3,10},{11,4},{4,11},{12,5},{5,12},... | collective-permute-start | bytes 786440 | tf_op jit(solution)/shard_map/ppermute | solution.py:61
  68.4 9.4 %collective-permute-start.21 = (f32[32,16,128]{2,1,0:T(8,128)S(1)}, f32[32,16,128]{2,1,0:T(8,128)S(1)}, u32[]{:S(2)}, u32[]{:S(2)}) collective-permute-start(f32[32,16,128]{2,1,0:T(8,128)S(1)} %get-tuple-element.100.refs_3_), channel_id=1, source_target_pairs={{0,8},{8,0},{1,9},{9,1},{2,10},{10,2},{3,11},{11,3},{4,12},{12,4},... | collective-permute-start | bytes 786440 | tf_op jit(solution)/shard_map/ppermute | solution.py:61
  74.5 11.3 %collective-permute-start.23 = (f32[32,32,128]{2,1,0:T(8,128)S(1)}, f32[32,32,128]{2,1,0:T(8,128)S(1)}, u32[]{:S(2)}, u32[]{:S(2)}) collective-permute-start(f32[32,32,128]{2,1,0:T(8,128)S(1)} %conv_x.24.refs_6_.refs_0_), channel_id=1, source_target_pairs={{0,16},{16,0},{1,17},{17,1},{2,18},{18,2},{3,19},{19,3},{4,20},{20... | collective-permute-start | bytes 1572872 | tf_op jit(solution)/shard_map/ppermute | solution.py:61
  76.3 12.3 %collective-permute-start.27 = (f32[64,16,128]{2,1,0:T(8,128)S(1)}, f32[64,16,128]{2,1,0:T(8,128)S(1)}, u32[]{:S(2)}, u32[]{:S(2)}) collective-permute-start(f32[64,16,128]{2,1,0:T(8,128)S(1)} %conv_z.27.i_ref.refs_3_), channel_id=1, source_target_pairs={{0,8},{8,0},{1,9},{9,1},{2,10},{10,2},{3,11},{11,3},{4,12},{12,4},... | collective-permute-start | bytes 1572872 | tf_op jit(solution)/shard_map/ppermute | solution.py:61
  77.1 11.5 %collective-permute-start.28 = (f32[32,16,128]{2,1,0:T(8,128)S(1)}, f32[32,16,128]{2,1,0:T(8,128)S(1)}, u32[]{:S(2)}, u32[]{:S(2)}) collective-permute-start(f32[32,16,128]{2,1,0:T(8,128)S(1)} %get-tuple-element.108.e_ref), channel_id=1, source_target_pairs={{8,1},{1,8},{9,2},{2,9},{10,3},{3,10},{11,4},{4,11},{12,5},{5,12},... | collective-permute-start | bytes 786440 | tf_op jit(solution)/shard_map/ppermute | solution.py:61
  78.3 13.7 %collective-permute-start.26 = (f32[32,16,128]{2,1,0:T(8,128)S(1)}, f32[32,16,128]{2,1,0:T(8,128)S(1)}, u32[]{:S(2)}, u32[]{:S(2)}) collective-permute-start(f32[32,16,128]{2,1,0:T(8,128)S(1)} %get-tuple-element.106.refs_2_), channel_id=1, source_target_pairs={{8,1},{1,8},{9,2},{2,9},{10,3},{3,10},{11,4},{4,11},{12,5},{5,12},... | collective-permute-start | bytes 786440 | tf_op jit(solution)/shard_map/ppermute | solution.py:61
  86.7 16.0 %collective-permute-start.25 = (f32[64,16,128]{2,1,0:T(8,128)S(1)}, f32[64,16,128]{2,1,0:T(8,128)S(1)}, u32[]{:S(2)}, u32[]{:S(2)}) collective-permute-start(f32[64,16,128]{2,1,0:T(8,128)S(1)} %conv_z.26.i_ref.refs_3_), channel_id=1, source_target_pairs={{0,8},{8,0},{1,9},{9,1},{2,10},{10,2},{3,11},{11,3},{4,12},{12,4},... | collective-permute-start | bytes 1572872 | tf_op jit(solution)/shard_map/ppermute | solution.py:61
  89.0 14.1 %collective-permute-start.30 = (f32[32,32,128]{2,1,0:T(8,128)S(1)}, f32[32,32,128]{2,1,0:T(8,128)S(1)}, u32[]{:S(2)}, u32[]{:S(2)}) collective-permute-start(f32[32,32,128]{2,1,0:T(8,128)S(1)} %conv_x.27.refs_7_.refs_0_), channel_id=1, source_target_pairs={{0,16},{16,0},{1,17},{17,1},{2,18},{18,2},{3,19},{19,3},{4,20},{20... | collective-permute-start | bytes 1572872 | tf_op jit(solution)/shard_map/ppermute | solution.py:61
  91.8 10.9 %collective-permute-start.24 = (f32[32,16,128]{2,1,0:T(8,128)S(1)}, f32[32,16,128]{2,1,0:T(8,128)S(1)}, u32[]{:S(2)}, u32[]{:S(2)}) collective-permute-start(f32[32,16,128]{2,1,0:T(8,128)S(1)} %get-tuple-element.105.e_ref), channel_id=1, source_target_pairs={{8,1},{1,8},{9,2},{2,9},{10,3},{3,10},{11,4},{4,11},{12,5},{5,12},... | collective-permute-start | bytes 786440 | tf_op jit(solution)/shard_map/ppermute | solution.py:61
  92.4 13.2 %collective-permute-start.29 = (f32[32,16,128]{2,1,0:T(8,128)S(1)}, f32[32,16,128]{2,1,0:T(8,128)S(1)}, u32[]{:S(2)}, u32[]{:S(2)}) collective-permute-start(f32[32,16,128]{2,1,0:T(8,128)S(1)} %get-tuple-element.109.refs_2_), channel_id=1, source_target_pairs={{8,1},{1,8},{9,2},{2,9},{10,3},{3,10},{11,4},{4,11},{12,5},{5,12},... | collective-permute-start | bytes 786440 | tf_op jit(solution)/shard_map/ppermute | solution.py:61
  103.1 10.3 %collective-permute-start.31 = (f32[32,32,128]{2,1,0:T(8,128)S(1)}, f32[32,32,128]{2,1,0:T(8,128)S(1)}, u32[]{:S(2)}, u32[]{:S(2)}) collective-permute-start(f32[32,32,128]{2,1,0:T(8,128)S(1)} %conv_x.26.refs_6_.refs_0_), channel_id=1, source_target_pairs={{0,16},{16,0},{1,17},{17,1},{2,18},{18,2},{3,19},{19,3},{4,20},{20... | collective-permute-start | bytes 1572872 | tf_op jit(solution)/shard_map/ppermute | solution.py:61
  103.9 12.3 %collective-permute-start.33 = (f32[64,16,128]{2,1,0:T(8,128)S(1)}, f32[64,16,128]{2,1,0:T(8,128)S(1)}, u32[]{:S(2)}, u32[]{:S(2)}) collective-permute-start(f32[64,16,128]{2,1,0:T(8,128)S(1)} %conv_z.31.i_ref.refs_3_), channel_id=1, source_target_pairs={{0,8},{8,0},{1,9},{9,1},{2,10},{10,2},{3,11},{11,3},{4,12},{12,4},... | collective-permute-start | bytes 1572872 | tf_op jit(solution)/shard_map/ppermute | solution.py:61
  104.7 11.5 %collective-permute-start.32 = (f32[32,16,128]{2,1,0:T(8,128)S(1)}, f32[32,16,128]{2,1,0:T(8,128)S(1)}, u32[]{:S(2)}, u32[]{:S(2)}) collective-permute-start(f32[32,16,128]{2,1,0:T(8,128)S(1)} %get-tuple-element.115.e_ref), channel_id=1, source_target_pairs={{8,1},{1,8},{9,2},{2,9},{10,3},{3,10},{11,4},{4,11},{12,5},{5,12},... | collective-permute-start | bytes 786440 | tf_op jit(solution)/shard_map/ppermute | solution.py:61
  106.1 12.9 %collective-permute-start.34 = (f32[32,16,128]{2,1,0:T(8,128)S(1)}, f32[32,16,128]{2,1,0:T(8,128)S(1)}, u32[]{:S(2)}, u32[]{:S(2)}) collective-permute-start(f32[32,16,128]{2,1,0:T(8,128)S(1)} %get-tuple-element.116.refs_2_), channel_id=1, source_target_pairs={{8,1},{1,8},{9,2},{2,9},{10,3},{3,10},{11,4},{4,11},{12,5},{5,12},... | collective-permute-start | bytes 786440 | tf_op jit(solution)/shard_map/ppermute | solution.py:61
  (8 other events, 41.4 us)
